TPU v7x, 32 devices: a whole 2x2x4 slice. The times are simulated.
32 devices in a mesh: fsdp: 2 (over core), ctx: 4 (over y, x), tp: 4 (over z).
Axes of the slice: x: 2, y: 2, z: 4, core: 2. Of those that a mesh axis runs over, the one named last changes fastest.
Arguments:
- tokens: bfloat16 [4, 1536, 2048], P(None, ('fsdp', 'ctx')), may hold values from -6 to 6
- cotangent: bfloat16 [4, 1536, 2048], P(None, ('fsdp', 'ctx')), may hold values from -6 to 6
- lengths: int32 [4, 2, 8], replicated, may hold values from 1 to 761, as said below
- order: int32 [4, 1536], replicated, may hold values from 0 to 1535, as said below
- gain_in: bfloat16 [2048], P(('fsdp', 'ctx')), may hold values from 0.5 to 1.5
- query_proj: bfloat16 [2048, 2048], P(('fsdp', 'ctx'), 'tp'), may hold values from -0.125 to 0.125
- key_proj: bfloat16 [2048, 2048], P(('fsdp', 'ctx'), 'tp'), may hold values from -0.125 to 0.125
- value_proj: bfloat16 [2048, 4096], P(('fsdp', 'ctx'), 'tp'), may hold values from -0.125 to 0.125
- gate_proj: bfloat16 [2048, 4096], P(('fsdp', 'ctx'), 'tp'), may hold values from -0.125 to 0.125
- alpha_proj: bfloat16 [2048, 16], P(('fsdp', 'ctx'), 'tp'), may hold values from -0.25 to 0.25
- beta_proj: bfloat16 [2048, 16], P(('fsdp', 'ctx'), 'tp'), may hold values from -0.125 to 0.125
- query_conv: bfloat16 [4, 16, 128], P(None, 'tp', ('fsdp', 'ctx')), may hold values from -3 to 3
- key_conv: bfloat16 [4, 16, 128], P(None, 'tp', ('fsdp', 'ctx')), may hold values from -3 to 3
- value_conv: bfloat16 [4, 16, 256], P(None, 'tp', ('fsdp', 'ctx')), may hold values from -3 to 3
- decay_log: float32 [16], P('tp'), may hold values from -0.9 to 2.5
- step_bias: float32 [16], P('tp'), may hold values from -7 to -5
- gain_head: bfloat16 [256], P(('fsdp', 'ctx')), may hold values from 0.5 to 1.5
- out_proj: bfloat16 [4096, 2048], P('tp', ('fsdp', 'ctx')), may hold values from -0.125 to 0.125
- gain_mid: bfloat16 [2048], P(('fsdp', 'ctx')), may hold values from 0.5 to 1.5
- ffn_gate: bfloat16 [2048, 5632], P(('fsdp', 'ctx'), 'tp'), may hold values from -0.125 to 0.125
- ffn_up: bfloat16 [2048, 5632], P(('fsdp', 'ctx'), 'tp'), may hold values from -0.125 to 0.125
- ffn_down: bfloat16 [5632, 2048], P('tp', ('fsdp', 'ctx')), may hold values from -0.078125 to 0.078125
Outputs:
- mixed: bfloat16 [4, 1536, 2048], P(None, ('fsdp', 'ctx'))
- grad_tokens: bfloat16 [4, 1536, 2048], P(None, ('fsdp', 'ctx'))
- grad_gain_in: float32 [2048], P(('fsdp', 'ctx'))
- grad_query_proj: float32 [2048, 2048], P(('fsdp', 'ctx'), 'tp')
- grad_key_proj: float32 [2048, 2048], P(('fsdp', 'ctx'), 'tp')
- grad_value_proj: float32 [2048, 4096], P(('fsdp', 'ctx'), 'tp')
- grad_gate_proj: float32 [2048, 4096], P(('fsdp', 'ctx'), 'tp')
- grad_alpha_proj: float32 [2048, 16], P(('fsdp', 'ctx'), 'tp')
- grad_beta_proj: float32 [2048, 16], P(('fsdp', 'ctx'), 'tp')
- grad_query_conv: float32 [4, 16, 128], P(None, 'tp', ('fsdp', 'ctx'))
- grad_key_conv: float32 [4, 16, 128], P(None, 'tp', ('fsdp', 'ctx'))
- value_convolved_gradient: float32 [4, 16, 256], P(None, 'tp', ('fsdp', 'ctx'))
- grad_decay_log: float32 [16], P('tp')
- grad_step_bias: float32 [16], P('tp')
- head_gain_gradient: float32 [256], P(('fsdp', 'ctx'))
- grad_out_proj: float32 [4096, 2048], P('tp', ('fsdp', 'ctx'))
- grad_gain_mid: float32 [2048], P(('fsdp', 'ctx'))
- grad_ffn_gate: float32 [2048, 5632], P(('fsdp', 'ctx'), 'tp')
- grad_ffn_up: float32 [2048, 5632], P(('fsdp', 'ctx'), 'tp')
- grad_ffn_down: float32 [5632, 2048], P('tp', ('fsdp', 'ctx'))
Inputs may be any that keep to these rules, and one draw needn't show every extreme that they name: Each pack's lengths sum to at most 768; every sequence has at least one place; every pack has exactly one sequence of 761 places, never its first. `order`: each micro-batch's row is a permutation; the tokens of given indices g * 192 to (g + 1) * 192 - 1 fill exactly 24 places in each range h * 192 to (h + 1) * 192 - 1 of packed places.
All inputs are finite; a program needn't handle non-finite values.
Results may differ from a plain program's by a relative error of at most 0.018.
Values may be sent and summed in bfloat16 or wider, within the bound.
No kernel may reach another device: no remote copies, remote signals or barrier semaphores. Data moves between devices by JAX's collectives and lax.ppermute only.
A program may use at most 448 MiB of HBM per device.

v0:
```python
import jax
import jax.numpy as jnp
from jax import lax
from jax.sharding import PartitionSpec as P

BLOCK = 64


square_eps = 1e-05
unit_eps = 1e-06


def from_behind(block, axis, distance):
    devices = range(lax.axis_size(axis))
    route = [(i - distance, i) for i in devices if i - distance in devices]
    return lax.ppermute(block, axis, route)


def prefix_2(part, axis, combine, identity):
    place = lax.axis_index(axis)
    gathered = jax.tree.map(lambda a: lax.all_gather(a, axis), part)
    state = jax.tree.map(lambda a, e: jnp.zeros_like(a) + jnp.asarray(e, a.dtype), part, identity)

    def prefix_one(turn, state):
        return combine(
            state, jax.tree.map(lambda a: lax.dynamic_index_in_dim(a, turn, 0, False), gathered)
        )

    return lax.fori_loop(0, place, prefix_one, state)


def entering(shard, axis, join, neutral):
    count = lax.axis_size(axis)
    place = lax.axis_index(axis)
    ahead = count - 1 - place
    gathered = jax.tree.map(
        lambda a, kind: lax.all_gather(a.astype(kind), axis),
        shard,
        jax.tree.map(lambda a: jnp.bfloat16 if a.dtype == jnp.float32 else a.dtype, shard),
    )
    state = jax.tree.map(lambda a, e: jnp.zeros_like(a) + jnp.asarray(e, a.dtype), shard, neutral)

    def entering_one(turn, state):
        source = count - 1 - turn
        return join(
            state,
            jax.tree.map(
                lambda a, own: lax.dynamic_index_in_dim(a, source, 0, False).astype(own.dtype),
                gathered,
                shard,
            ),
        )

    return lax.fori_loop(0, ahead, entering_one, state)


def exact_sum(spec, left, right):
    return jnp.einsum(spec, left, right, precision=lax.Precision.HIGHEST)


def matmul(left, right):
    return jnp.dot(left, right, preferred_element_type=jnp.float32)


def matmul_tn(left, right):
    return lax.dot_general(
        left, right, (((0,), (0,)), ((), ())), preferred_element_type=jnp.float32
    )


def matmul_nt(left, right):
    return lax.dot_general(
        left, right, (((1,), (1,)), ((), ())), preferred_element_type=jnp.float32
    )


def scale_rows(values, gain_vec):
    return (
        values
        * lax.rsqrt(jnp.mean(values * values, axis=-1, keepdims=True) + square_eps)
        * gain_vec
    )


def unit_rows(values):
    return values * lax.rsqrt(jnp.sum(values * values, axis=-1, keepdims=True) + unit_eps)


def place_info(length_row, places):
    end_places = jnp.cumsum(length_row)
    starts = end_places - length_row
    segment = jnp.sum((places[:, None] >= starts[None, :]).astype(jnp.int32), axis=1) - 1
    inside = jnp.logical_and(places >= 0, places < end_places[-1]).astype(jnp.float32)
    return (segment, inside)


def convolve(extended, segment_ext, weight):
    span_size = weight.shape[0]
    row_count = extended.shape[0] - span_size + 1
    segment = segment_ext[span_size - 1 :]
    running = jnp.zeros((row_count, extended.shape[1]), jnp.float32)
    for offset in range(span_size):
        same_seq = (segment_ext[offset : offset + row_count] == segment).astype(jnp.float32)
        running = (
            running
            + weight[offset][None, :] * extended[offset : offset + row_count] * same_seq[:, None]
        )
    return jax.nn.silu(running)


def solve_lower(matrix, target):
    return jax.scipy.linalg.solve_triangular(matrix, target, lower=True, unit_diagonal=True)


def compose(earlier, later):
    return (
        exact_sum("hij,hjk->hik", later[0], earlier[0]),
        exact_sum("hij,hjk->hik", later[0], earlier[1]) + later[1],
    )


def block_heads(
    memory_state, last_seg, queries, keys_unit, values, betas, log_decays, segment, with_output
):
    size_block = segment.shape[0]
    cumulative = jnp.cumsum(log_decays, axis=0)
    lower = jnp.tril(jnp.ones((size_block, size_block), jnp.bool_))
    strict = jnp.tril(jnp.ones((size_block, size_block), jnp.float32), -1)
    inner = jnp.logical_and(lower, segment[:, None] == segment[None, :]).astype(jnp.float32)
    spread = jnp.where(lower[:, :, None], cumulative[:, None, :] - cumulative[None, :, :], 0.0)
    decays = jnp.transpose(jnp.exp(spread) * inner[:, :, None], (2, 0, 1))
    carried = jnp.exp(cumulative) * (segment == last_seg).astype(jnp.float32)[:, None]
    tail = (
        jnp.exp(cumulative[-1][None, :] - cumulative)
        * (segment == segment[-1]).astype(jnp.float32)[:, None]
    )
    head_keep = jnp.exp(cumulative[-1]) * (segment[-1] == last_seg).astype(jnp.float32)
    key_gram = exact_sum("thk,shk->hts", keys_unit, keys_unit)
    lower_mat = decays * key_gram * jnp.transpose(betas)[:, None, :] * strict[None]
    known = exact_sum("thk,hkw->htw", keys_unit, memory_state) * jnp.transpose(carried)[:, :, None]
    targets = jnp.transpose(values, (1, 0, 2)) - known
    pseudo = jax.vmap(solve_lower)(lower_mat, targets)
    weighted = pseudo * jnp.transpose(betas)[:, :, None]
    new_state = memory_state * head_keep[:, None, None] + exact_sum(
        "shk,hsw->hkw", keys_unit, weighted * jnp.transpose(tail)[:, :, None]
    )
    if not with_output:
        return (new_state, None)
    query_key = exact_sum("thk,shk->hts", queries, keys_unit)
    outputs = exact_sum("thk,hkw->htw", queries, memory_state) * jnp.transpose(carried)[:, :, None]
    outputs = outputs + exact_sum("hts,hsw->htw", decays * query_key, weighted)
    return (new_state, jnp.transpose(outputs, (1, 0, 2)))


def run_device(
    memory_state, last_seg, queries, keys_unit, values, betas, log_decays, segment, with_output
):
    row_count = segment.shape[0]
    blocks = row_count // BLOCK

    def to_blocks(item):
        return item.reshape((blocks, BLOCK) + item.shape[1:])

    inputs = tuple(
        (to_blocks(item) for item in (queries, keys_unit, values, betas, log_decays, segment))
    )

    def one_block(carried_in, block_data):
        current, previous = carried_in
        query_part, key_part, value_part, beta_part, decay_part, segment_part = block_data
        new_state, outputs = block_heads(
            current,
            previous,
            query_part,
            key_part,
            value_part,
            beta_part,
            decay_part,
            segment_part,
            with_output,
        )
        return ((new_state, segment_part[-1]), outputs)

    (final_state, unused), outputs = lax.scan(one_block, (memory_state, last_seg), inputs)
    if with_output:
        outputs = outputs.reshape(row_count, values.shape[1], values.shape[2])
    return (final_state, outputs)


def per_device(
    tokens,
    cotangent,
    lengths,
    order,
    gain_in,
    query_proj,
    key_proj,
    value_proj,
    gate_proj,
    alpha_proj,
    beta_proj,
    query_conv,
    key_conv,
    value_conv,
    decay_log,
    step_bias,
    gain_head,
    out_proj,
    gain_mid,
    ffn_gate,
    ffn_up,
    ffn_down,
):
    group_count = lax.axis_size(("fsdp", "ctx"))
    ctx_count = lax.axis_size("ctx")
    ctx_place = lax.axis_index("ctx")
    fsdp_place = lax.axis_index("fsdp")
    device_place = fsdp_place * ctx_count + ctx_place
    micro_count = tokens.shape[0]
    row_count = tokens.shape[1]
    all_rows = order.shape[1]
    span_size = query_conv.shape[0]
    head_local = decay_log.shape[0]
    key_size = query_conv.shape[2] * group_count
    value_size = value_conv.shape[2] * group_count
    rim_rows = span_size - 1
    row_places = jnp.arange(row_count, dtype=jnp.int32)
    ext_places = (
        ctx_place * row_count - rim_rows + jnp.arange(row_count + rim_rows, dtype=jnp.int32)
    )
    identity = jnp.broadcast_to(
        jnp.eye(key_size, dtype=jnp.float32), (head_local, key_size, key_size)
    )
    empty_state = jnp.zeros((head_local, key_size, value_size), jnp.float32)
    running = None
    decay_total = jnp.zeros((head_local,), jnp.float32)
    bias_total = jnp.zeros((head_local,), jnp.float32)
    mixed_rows = []
    grad_rows = []
    for micro_step in range(micro_count):
        order_row = order[micro_step]
        given_place = (
            jnp.zeros_like(order_row).at[order_row].set(jnp.arange(all_rows, dtype=jnp.int32))
        )
        send_order = jnp.argsort(
            lax.dynamic_slice_in_dim(given_place, device_place * row_count, row_count)
        )
        slot_source = (
            lax.dynamic_slice_in_dim(order_row, device_place * row_count, row_count) // row_count
        )
        recv_order = jnp.argsort(slot_source * all_rows + device_place * row_count + row_places)
        arrived = (
            lax.all_to_all(
                tokens[micro_step][send_order],
                ("fsdp", "ctx"),
                split_axis=0,
                concat_axis=0,
                tiled=True,
            ),
            lax.all_to_all(
                cotangent[micro_step][send_order],
                ("fsdp", "ctx"),
                split_axis=0,
                concat_axis=0,
                tiled=True,
            ),
        )
        tokens_here = jnp.zeros_like(arrived[0]).at[recv_order].set(arrived[0])
        grads_here = jnp.zeros_like(arrived[1]).at[recv_order].set(arrived[1])
        (
            gain_full,
            query_full,
            key_full,
            value_full,
            gate_full,
            alpha_full,
            beta_full,
            qconv_full,
            kconv_full,
            vconv_full,
            head_gain_full,
            out_full,
        ) = (
            lax.all_gather(gain_in, ("fsdp", "ctx"), axis=0, tiled=True),
            lax.all_gather(query_proj, ("fsdp", "ctx"), axis=0, tiled=True),
            lax.all_gather(key_proj, ("fsdp", "ctx"), axis=0, tiled=True),
            lax.all_gather(value_proj, ("fsdp", "ctx"), axis=0, tiled=True),
            lax.all_gather(gate_proj, ("fsdp", "ctx"), axis=0, tiled=True),
            lax.all_gather(alpha_proj, ("fsdp", "ctx"), axis=0, tiled=True),
            lax.all_gather(beta_proj, ("fsdp", "ctx"), axis=0, tiled=True),
            lax.all_gather(query_conv, ("fsdp", "ctx"), axis=2, tiled=True),
            lax.all_gather(key_conv, ("fsdp", "ctx"), axis=2, tiled=True),
            lax.all_gather(value_conv, ("fsdp", "ctx"), axis=2, tiled=True),
            lax.all_gather(gain_head, ("fsdp", "ctx"), axis=0, tiled=True),
            lax.all_gather(out_proj, ("fsdp", "ctx"), axis=1, tiled=True),
        )
        mid_gain_full, ffn_gate_full, ffn_up_full, ffn_down_full = (
            lax.all_gather(gain_mid, ("fsdp", "ctx"), axis=0, tiled=True),
            lax.all_gather(ffn_gate, ("fsdp", "ctx"), axis=0, tiled=True),
            lax.all_gather(ffn_up, ("fsdp", "ctx"), axis=0, tiled=True),
            lax.all_gather(ffn_down, ("fsdp", "ctx"), axis=1, tiled=True),
        )
        segment_ext, inside_ext = place_info(lengths[micro_step, fsdp_place], ext_places)
        segment = segment_ext[rim_rows:]
        inside = inside_ext[rim_rows:]
        last_before = segment_ext[rim_rows - 1]
        x_float = tokens_here.astype(jnp.float32)
        first_value, first_pull = jax.vjp(scale_rows, x_float, gain_full.astype(jnp.float32))
        normed_in = first_value.astype(jnp.bfloat16)
        proj_query = matmul(normed_in, query_full)
        proj_key = matmul(normed_in, key_full)
        proj_value = matmul(normed_in, value_full)
        proj_gate = matmul(normed_in, gate_full)
        proj_alpha = matmul(normed_in, alpha_full)
        proj_beta = matmul(normed_in, beta_full)
        rims = from_behind(
            (proj_query[-rim_rows:], proj_key[-rim_rows:], proj_value[-rim_rows:]), "ctx", 1
        )
        ext_query = jnp.concatenate([rims[0], proj_query], axis=0)
        ext_key = jnp.concatenate([rims[1], proj_key], axis=0)
        ext_value = jnp.concatenate([rims[2], proj_value], axis=0)

        def prepare(
            query_ext,
            key_ext,
            value_ext,
            alpha_in,
            beta_in,
            conv_query,
            conv_key,
            conv_value,
            decay_in,
            bias_in,
        ):
            query_act = convolve(query_ext, segment_ext, conv_query.reshape(span_size, -1))
            key_act = convolve(key_ext, segment_ext, conv_key.reshape(span_size, -1))
            value_act = convolve(value_ext, segment_ext, conv_value.reshape(span_size, -1))
            queries = unit_rows(query_act.reshape(row_count, head_local, key_size)) * key_size ** (
                -0.5
            )
            keys_unit = unit_rows(key_act.reshape(row_count, head_local, key_size))
            values = value_act.reshape(row_count, head_local, value_size)
            betas = jax.nn.sigmoid(beta_in) * inside[:, None]
            log_decays = -jnp.exp(decay_in) * jax.nn.softplus(alpha_in + bias_in)
            return (queries, keys_unit, values, betas, log_decays)

        (queries, keys_unit, values, betas, log_decays), prepare_pull = jax.vjp(
            prepare,
            ext_query,
            ext_key,
            ext_value,
            proj_alpha,
            proj_beta,
            qconv_full.astype(jnp.float32),
            kconv_full.astype(jnp.float32),
            vconv_full.astype(jnp.float32),
            decay_log,
            step_bias,
        )
        aug_state = jnp.concatenate([empty_state, identity], axis=2)
        aug_values = jnp.concatenate(
            [values, jnp.zeros((row_count, head_local, key_size), jnp.float32)], axis=2
        )
        end_aug, unused = run_device(
            aug_state,
            last_before,
            queries,
            keys_unit,
            aug_values,
            betas,
            log_decays,
            segment,
            False,
        )
        transfer = end_aug[:, :, value_size:]
        offset_state = end_aug[:, :, :value_size]
        prefix = prefix_2((transfer, offset_state), "ctx", compose, (identity, empty_state))

        def deltas(query_in, key_in, value_in, beta_in, decay_in, state_start):
            return run_device(
                state_start,
                last_before,
                query_in,
                key_in,
                value_in,
                beta_in,
                decay_in,
                segment,
                True,
            )

        (end_state, outputs), delta_pull = jax.vjp(
            deltas, queries, keys_unit, values, betas, log_decays, prefix[1]
        )

        def finish(output_in, gate_in, gain_vec):
            gated = scale_rows(output_in, gain_vec) * jax.nn.silu(
                gate_in.reshape(row_count, head_local, value_size)
            )
            gated = gated * inside[:, None, None]
            return gated.reshape(row_count, head_local * value_size)

        normed_mix, finish_pull = jax.vjp(
            finish, outputs, proj_gate, head_gain_full.astype(jnp.float32)
        )
        normed_low = normed_mix.astype(jnp.bfloat16)
        mixer = lax.psum(matmul(normed_low, out_full), "tp")
        hidden_in = x_float + mixer
        mid_value, mid_pull = jax.vjp(scale_rows, hidden_in, mid_gain_full.astype(jnp.float32))
        mid_low = mid_value.astype(jnp.bfloat16)
        gate_value = matmul(mid_low, ffn_gate_full)
        up_value = matmul(mid_low, ffn_up_full)
        gate_sig = jax.nn.sigmoid(gate_value)
        gate_act = gate_value * gate_sig
        hidden_low = (gate_act * up_value).astype(jnp.bfloat16)
        ffn_out = lax.psum(matmul(hidden_low, ffn_down_full).astype(jnp.bfloat16), "tp").astype(
            jnp.float32
        )
        result = (hidden_in + ffn_out).astype(jnp.bfloat16)
        grad_down = matmul_tn(hidden_low, grads_here)
        grad_hidden = matmul_nt(grads_here, ffn_down_full)
        gate_grad = (
            grad_hidden * up_value * gate_sig * (1.0 + gate_value * (1.0 - gate_sig))
        ).astype(jnp.bfloat16)
        up_grad = (grad_hidden * gate_act).astype(jnp.bfloat16)
        grad_gate_ffn = matmul_tn(mid_low, gate_grad)
        grad_up_ffn = matmul_tn(mid_low, up_grad)
        mid_grad = lax.psum(
            matmul_nt(gate_grad, ffn_gate_full) + matmul_nt(up_grad, ffn_up_full), "tp"
        )
        hidden_back, grad_mid_gain = mid_pull(mid_grad)
        hidden_grad = grads_here.astype(jnp.float32) + hidden_back
        mix_low = hidden_grad.astype(jnp.bfloat16)
        grad_out = matmul_tn(normed_low, mix_low)
        out_back, gate_back, grad_head_gain = finish_pull(matmul_nt(mix_low, out_full))
        local_back = delta_pull((jnp.zeros_like(end_state), out_back))[5]
        back_prefix = entering(
            (jnp.swapaxes(transfer, 1, 2), local_back), "ctx", compose, (identity, empty_state)
        )
        query_back, key_back, value_back, beta_back, decay_back, unused_state = delta_pull(
            (back_prefix[1], out_back)
        )
        (
            ext_q_back,
            ext_k_back,
            ext_v_back,
            alpha_back,
            beta_in_back,
            qconv_grad,
            kconv_grad,
            vconv_grad,
            decay_grad,
            bias_grad,
        ) = prepare_pull((query_back, key_back, value_back, beta_back, decay_back))
        returned = from_behind(
            (ext_q_back[:rim_rows], ext_k_back[:rim_rows], ext_v_back[:rim_rows]), "ctx", -1
        )
        query_grad = (
            ext_q_back[rim_rows:].at[row_count - rim_rows :].add(returned[0]).astype(jnp.bfloat16)
        )
        key_grad = (
            ext_k_back[rim_rows:].at[row_count - rim_rows :].add(returned[1]).astype(jnp.bfloat16)
        )
        value_grad = (
            ext_v_back[rim_rows:].at[row_count - rim_rows :].add(returned[2]).astype(jnp.bfloat16)
        )
        gate_proj_grad = gate_back.astype(jnp.bfloat16)
        alpha_grad = alpha_back.astype(jnp.bfloat16)
        beta_grad = beta_in_back.astype(jnp.bfloat16)
        first_back = (
            matmul_nt(query_grad, query_full)
            + matmul_nt(key_grad, key_full)
            + matmul_nt(value_grad, value_full)
        )
        first_back = (
            first_back + matmul_nt(gate_proj_grad, gate_full) + matmul_nt(alpha_grad, alpha_full)
        )
        first_back = first_back + matmul_nt(beta_grad, beta_full)
        first_sum, head_gain_sum = (
            lax.psum(first_back.astype(jnp.bfloat16), "tp").astype(jnp.float32),
            lax.psum(grad_head_gain.astype(jnp.bfloat16), "tp").astype(jnp.float32),
        )
        token_back, grad_first_gain = first_pull(first_sum)
        token_grad = (hidden_grad + token_back).astype(jnp.bfloat16)
        back_given = (
            lax.all_to_all(
                result[recv_order], ("fsdp", "ctx"), split_axis=0, concat_axis=0, tiled=True
            ),
            lax.all_to_all(
                token_grad[recv_order], ("fsdp", "ctx"), split_axis=0, concat_axis=0, tiled=True
            ),
        )
        mixed_rows.append(jnp.zeros_like(back_given[0]).at[send_order].set(back_given[0]))
        grad_rows.append(jnp.zeros_like(back_given[1]).at[send_order].set(back_given[1]))
        grads_local = (
            grad_first_gain,
            matmul_tn(normed_in, query_grad),
            matmul_tn(normed_in, key_grad),
            matmul_tn(normed_in, value_grad),
            matmul_tn(normed_in, gate_proj_grad),
            matmul_tn(normed_in, alpha_grad),
            matmul_tn(normed_in, beta_grad),
            qconv_grad,
            kconv_grad,
            vconv_grad,
            head_gain_sum,
            grad_out,
            grad_mid_gain,
            grad_gate_ffn,
            grad_up_ffn,
            grad_down,
        )
        shares = (
            lax.psum_scatter(
                grads_local[0].astype(jnp.bfloat16),
                ("fsdp", "ctx"),
                scatter_dimension=0,
                tiled=True,
            ).astype(jnp.float32),
            lax.psum_scatter(
                grads_local[1].astype(jnp.bfloat16),
                ("fsdp", "ctx"),
                scatter_dimension=0,
                tiled=True,
            ).astype(jnp.float32),
            lax.psum_scatter(
                grads_local[2].astype(jnp.bfloat16),
                ("fsdp", "ctx"),
                scatter_dimension=0,
                tiled=True,
            ).astype(jnp.float32),
            lax.psum_scatter(
                grads_local[3].astype(jnp.bfloat16),
                ("fsdp", "ctx"),
                scatter_dimension=0,
                tiled=True,
            ).astype(jnp.float32),
            lax.psum_scatter(
                grads_local[4].astype(jnp.bfloat16),
                ("fsdp", "ctx"),
                scatter_dimension=0,
                tiled=True,
            ).astype(jnp.float32),
            lax.psum_scatter(
                grads_local[5].astype(jnp.bfloat16),
                ("fsdp", "ctx"),
                scatter_dimension=0,
                tiled=True,
            ).astype(jnp.float32),
            lax.psum_scatter(
                grads_local[6].astype(jnp.bfloat16),
                ("fsdp", "ctx"),
                scatter_dimension=0,
                tiled=True,
            ).astype(jnp.float32),
            lax.psum_scatter(
                grads_local[7].astype(jnp.bfloat16),
                ("fsdp", "ctx"),
                scatter_dimension=2,
                tiled=True,
            ).astype(jnp.float32),
            lax.psum_scatter(
                grads_local[8].astype(jnp.bfloat16),
                ("fsdp", "ctx"),
                scatter_dimension=2,
                tiled=True,
            ).astype(jnp.float32),
            lax.psum_scatter(
                grads_local[9].astype(jnp.bfloat16),
                ("fsdp", "ctx"),
                scatter_dimension=2,
                tiled=True,
            ).astype(jnp.float32),
            lax.psum_scatter(
                grads_local[10].astype(jnp.bfloat16),
                ("fsdp", "ctx"),
                scatter_dimension=0,
                tiled=True,
            ).astype(jnp.float32),
            lax.psum_scatter(
                grads_local[11].astype(jnp.bfloat16),
                ("fsdp", "ctx"),
                scatter_dimension=1,
                tiled=True,
            ).astype(jnp.float32),
            lax.psum_scatter(
                grads_local[12].astype(jnp.bfloat16),
                ("fsdp", "ctx"),
                scatter_dimension=0,
                tiled=True,
            ).astype(jnp.float32),
            lax.psum_scatter(
                grads_local[13].astype(jnp.bfloat16),
                ("fsdp", "ctx"),
                scatter_dimension=0,
                tiled=True,
            ).astype(jnp.float32),
            lax.psum_scatter(
                grads_local[14].astype(jnp.bfloat16),
                ("fsdp", "ctx"),
                scatter_dimension=0,
                tiled=True,
            ).astype(jnp.float32),
            lax.psum_scatter(
                grads_local[15].astype(jnp.bfloat16),
                ("fsdp", "ctx"),
                scatter_dimension=1,
                tiled=True,
            ).astype(jnp.float32),
        )
        if running is None:
            running = tuple(shares)
        else:
            running = tuple((left + right for left, right in zip(running, shares)))
        decay_total = decay_total + decay_grad
        bias_total = bias_total + bias_grad
    decay_sum, bias_sum = lax.psum((decay_total, bias_total), ("fsdp", "ctx"))
    return (
        jnp.stack(mixed_rows),
        jnp.stack(grad_rows),
        running[0],
        running[1],
        running[2],
        running[3],
        running[4],
        running[5],
        running[6],
        running[7],
        running[8],
        running[9],
        decay_sum,
        bias_sum,
        running[10],
        running[11],
        running[12],
        running[13],
        running[14],
        running[15],
    )


def solution(mesh):
    in_specs = (
        P(None, ("fsdp", "ctx"), None),
        P(None, ("fsdp", "ctx"), None),
        P(),
        P(),
        P(("fsdp", "ctx")),
        P(("fsdp", "ctx"), "tp"),
        P(("fsdp", "ctx"), "tp"),
        P(("fsdp", "ctx"), "tp"),
        P(("fsdp", "ctx"), "tp"),
        P(("fsdp", "ctx"), "tp"),
        P(("fsdp", "ctx"), "tp"),
        P(None, "tp", ("fsdp", "ctx")),
        P(None, "tp", ("fsdp", "ctx")),
        P(None, "tp", ("fsdp", "ctx")),
        P("tp"),
        P("tp"),
        P(("fsdp", "ctx")),
        P("tp", ("fsdp", "ctx")),
        P(("fsdp", "ctx")),
        P(("fsdp", "ctx"), "tp"),
        P(("fsdp", "ctx"), "tp"),
        P("tp", ("fsdp", "ctx")),
    )
    out_specs = (
        P(None, ("fsdp", "ctx"), None),
        P(None, ("fsdp", "ctx"), None),
        P(("fsdp", "ctx")),
        P(("fsdp", "ctx"), "tp"),
        P(("fsdp", "ctx"), "tp"),
        P(("fsdp", "ctx"), "tp"),
        P(("fsdp", "ctx"), "tp"),
        P(("fsdp", "ctx"), "tp"),
        P(("fsdp", "ctx"), "tp"),
        P(None, "tp", ("fsdp", "ctx")),
        P(None, "tp", ("fsdp", "ctx")),
        P(None, "tp", ("fsdp", "ctx")),
        P("tp"),
        P("tp"),
        P(("fsdp", "ctx")),
        P("tp", ("fsdp", "ctx")),
        P(("fsdp", "ctx")),
        P(("fsdp", "ctx"), "tp"),
        P(("fsdp", "ctx"), "tp"),
        P("tp", ("fsdp", "ctx")),
    )
    return jax.shard_map(
        per_device, mesh=mesh, in_specs=in_specs, out_specs=out_specs, check_vma=False
    )
```

profile of v0, /device:TPU:0, one launch (start us, length us, event | category | flops | bytes accessed | tf_op | source)
XLA Modules:
  0.0 6244.0 jit_solution(14830435733981158090)
XLA Ops:
  329.0 93.7 %while.608 = (s32[]{:T(128)}, f32[4,128,384]{2,1,0:T(8,128)S(1)}, s32[]{:T(128)}, f32[3,64,4]{2,1,0:T(8,128)}, s32[3,64]{1,0:T(4,128)}, /*index=5*/f32[3,64,4,12...) while((s32[]{:T(128)}, f32[4,128,384]{2,1,0:T(8,128)S(1)}, ...), condition=%wide.region_10.13_spmd, body=%wide.region_8.12_spmd.sunk | while | flops 403628864 | bytes 5056055 | solution.py:184
  449.1 103.9 %while.610 = (s32[]{:T(128)}, f32[4,128,384]{2,1,0:T(8,128)S(1)}, s32[]{:T(128)}, f32[3,64,4]{2,1,0:T(8,128)}, s32[3,64]{1,0:T(4,128)}, /*index=5*/f32[3,64,4,12...) while((s32[]{:T(128)}, f32[4,128,384]{2,1,0:T(8,128)S(1)}, ...), condition=%wide.region_32.36_spmd, body=%wide.region_30.35_spmd.sunk | while | flops 403628864 | bytes 5066407 | solution.py:184
  581.4 93.7 %while.612 = (s32[]{:T(128)}, f32[4,128,384]{2,1,0:T(8,128)S(1)}, s32[]{:T(128)}, f32[3,64,4]{2,1,0:T(8,128)}, s32[3,64]{1,0:T(4,128)}, /*index=5*/f32[3,64,4,12...) while((s32[]{:T(128)}, f32[4,128,384]{2,1,0:T(8,128)S(1)}, ...), condition=%wide.region_54.58_spmd, body=%wide.region_52.57_spmd.sunk | while | flops 403628864 | bytes 5056055 | solution.py:184
  698.1 83.1 %while.614 = (s32[]{:T(128)}, f32[4,128,384]{2,1,0:T(8,128)S(1)}, s32[]{:T(128)}, f32[3,64,4]{2,1,0:T(8,128)}, s32[3,64]{1,0:T(4,128)}, /*index=5*/f32[3,64,4,12...) while((s32[]{:T(128)}, f32[4,128,384]{2,1,0:T(8,128)S(1)}, ...), condition=%wide.region_76.80_spmd, body=%wide.region_74.79_spmd.sunk | while | flops 403628864 | bytes 5047807 | solution.py:184
  910.5 157.1 %while.624 = (s32[]{:T(128)}, f32[4,128,256]{2,1,0:T(8,128)S(1)}, s32[]{:T(128)}, f32[3,64,4,256]{3,1,2,0:T(8,128)}, f32[3,64,64,4]{2,1,3,0:T(8,128)}, /*index=5...) while((s32[]{:T(128)}, f32[4,128,256]{2,1,0:T(8,128)S(1)}, ...), condition=%wide.region_16.20_spmd.clone.clone, body=%wide.region_14.19_spmd.clone.clone.sunk | while | flops 454252096 | bytes 11294323 | solution.py:184
  1088.1 139.7 %while.625 = (s32[]{:T(128)}, f32[4,128,256]{2,1,0:T(8,128)S(1)}, s32[]{:T(128)}, f32[3,64,4,256]{3,1,2,0:T(8,128)}, f32[3,64,64,4]{2,1,3,0:T(8,128)}, /*index=5...) while((s32[]{:T(128)}, f32[4,128,256]{2,1,0:T(8,128)S(1)}, ...), condition=%wide.region_38.42_spmd.clone.clone, body=%wide.region_36.41_spmd.clone.clone.sunk | while | flops 454252096 | bytes 11238819 | solution.py:184
  1247.9 137.4 %while.626 = (s32[]{:T(128)}, f32[4,128,256]{2,1,0:T(8,128)S(1)}, s32[]{:T(128)}, f32[3,64,4,256]{3,1,2,0:T(8,128)}, f32[3,64,64,4]{2,1,3,0:T(8,128)}, /*index=5...) while((s32[]{:T(128)}, f32[4,128,256]{2,1,0:T(8,128)S(1)}, ...), condition=%wide.region_60.64_spmd.clone.clone, body=%wide.region_58.63_spmd.clone.clone.sunk | while | flops 454252096 | bytes 11294323 | solution.py:184
  1404.6 133.1 %while.627 = (s32[]{:T(128)}, f32[4,128,256]{2,1,0:T(8,128)S(1)}, s32[]{:T(128)}, f32[3,64,4,256]{3,1,2,0:T(8,128)}, f32[3,64,64,4]{2,1,3,0:T(8,128)}, /*index=5...) while((s32[]{:T(128)}, f32[4,128,256]{2,1,0:T(8,128)S(1)}, ...), condition=%wide.region_82.86_spmd.clone.clone, body=%wide.region_80.85_spmd.clone.clone.sunk | while | flops 454252096 | bytes 11304355 | solution.py:184
  1676.1 136.6 %all-reduce.134.cloned.1.call-done = (f32[192,2048]{1,0:T(8,128)}, f32[192,2048]{1,0:T(8,128)}, f32[192,2048]{1,0:T(8,128)}, f32[192,2048]{1,0:T(8,128)}) async-done(((f32[192,2048]{1,0:T(8,128)}, f32[192,2048]{1,0:T(8,128)}, f32[192,2048]{1,0:T(8,128)}, f32[192,2048]{1,0:T(8,128)}), (f32[192,2048]{1,0:T(8,128)}, f32[192,2048]{1,0:T(8,128)}, f32[192,2048]{1,0:T(8,128)}, ...) | async-done | bytes 6291472 | tf_op jit(solution)/shard_map/psum | solution.py:407
  2073.9 140.3 %all-reduce.132.cloned.1.call-done = (f32[192,2048]{1,0:T(8,128)}, f32[192,2048]{1,0:T(8,128)}, f32[192,2048]{1,0:T(8,128)}, f32[192,2048]{1,0:T(8,128)}) async-done(((f32[192,2048]{1,0:T(8,128)}, f32[192,2048]{1,0:T(8,128)}, f32[192,2048]{1,0:T(8,128)}, f32[192,2048]{1,0:T(8,128)}), (f32[192,2048]{1,0:T(8,128)}, f32[192,2048]{1,0:T(8,128)}, f32[192,2048]{1,0:T(8,128)}, ...) | async-done | bytes 6291472 | tf_op jit(solution)/shard_map/psum | solution.py:428
  2264.7 93.7 %while.631 = (s32[]{:T(128)}, f32[4,128,256]{2,1,0:T(8,128)}, f32[3,64,4,128]{3,1,2,0:T(8,128)}, f32[3,64,4,256]{3,1,2,0:T(8,128)S(1)}, f32[3,4,64,1]{2,1,3,0:T(...) while((s32[]{:T(128)}, f32[4,128,256]{2,1,0:T(8,128)}, ...), condition=%wide.region_168.174_spmd.clone, body=%wide.region_167.173_spmd.clone.sunk | while | flops 403746880 | bytes 7594743 | solution.py:184
  2360.7 90.3 %while.628 = (s32[]{:T(128)}, f32[4,128,256]{2,1,0:T(8,128)}, f32[3,64,4,128]{3,1,2,0:T(8,128)}, f32[3,64,4,256]{3,1,2,0:T(8,128)}, f32[3,4,64,1]{2,1,3,0:T(4,12...) while((s32[]{:T(128)}, f32[4,128,256]{2,1,0:T(8,128)}, ...), condition=%wide.region_93.98_spmd.clone, body=%wide.region_92.97_spmd.clone.sunk | while | flops 403746880 | bytes 7592199 | solution.py:184
  2452.9 93.8 %while.629 = (s32[]{:T(128)}, f32[4,128,256]{2,1,0:T(8,128)}, f32[3,64,4,128]{3,1,2,0:T(8,128)}, f32[3,64,4,256]{3,1,2,0:T(8,128)S(1)}, f32[3,4,64,1]{2,1,3,0:T(...) while((s32[]{:T(128)}, f32[4,128,256]{2,1,0:T(8,128)}, ...), condition=%wide.region_118.124_spmd.clone, body=%wide.region_117.123_spmd.clone.sunk | while | flops 403746880 | bytes 7594743 | solution.py:184
  2548.9 86.4 %while.630 = (s32[]{:T(128)}, f32[4,128,256]{2,1,0:T(8,128)}, f32[3,64,4,128]{3,1,2,0:T(8,128)}, f32[3,64,4,256]{3,1,2,0:T(8,128)S(1)}, f32[3,4,64,1]{2,1,3,0:T(...) while((s32[]{:T(128)}, f32[4,128,256]{2,1,0:T(8,128)}, ...), condition=%wide.region_143.149_spmd.clone, body=%wide.region_142.148_spmd.clone.sunk | while | flops 403746880 | bytes 9691923 | solution.py:184
  2661.9 163.5 %while.623 = (s32[]{:T(128)}, f32[4,128,256]{2,1,0:T(8,128)}, f32[3,64,4,128]{3,1,2,0:T(8,128)}, f32[3,64,4,128]{3,1,2,0:T(8,128)}, f32[3,64,4,256]{3,2,1,0:T(4,...) while((s32[]{:T(128)}, f32[4,128,256]{2,1,0:T(8,128)}, ...), condition=%wide.region_182.188_spmd.clone, body=%wide.region_171.187_spmd.clone.sunk | while | flops 921016384 | bytes 27362264 | solution.py:184
  2843.3 179.9 %while.620 = (s32[]{:T(128)}, f32[4,128,256]{2,1,0:T(8,128)}, f32[3,64,4,128]{3,1,2,0:T(8,128)}, f32[3,64,4,128]{3,1,2,0:T(8,128)}, f32[3,64,4,256]{3,2,1,0:T(4,...) while((s32[]{:T(128)}, f32[4,128,256]{2,1,0:T(8,128)}, ...), condition=%wide.region_107.113_spmd.clone, body=%wide.region_96.112_spmd.clone.sunk | while | flops 921016384 | bytes 24475304 | solution.py:184
  3040.1 162.7 %while.621 = (s32[]{:T(128)}, f32[4,128,256]{2,1,0:T(8,128)}, f32[3,64,4,128]{3,1,2,0:T(8,128)}, f32[3,64,4,128]{3,1,2,0:T(8,128)}, f32[3,64,4,256]{3,2,1,0:T(4,...) while((s32[]{:T(128)}, f32[4,128,256]{2,1,0:T(8,128)}, ...), condition=%wide.region_132.138_spmd.clone, body=%wide.region_121.137_spmd.clone.sunk | while | flops 921016384 | bytes 24219052 | solution.py:184
  3262.0 147.7 %while.622 = (s32[]{:T(128)}, f32[4,128,256]{2,1,0:T(8,128)S(1)}, f32[3,64,4,128]{3,1,2,0:T(8,128)}, f32[3,64,4,128]{3,1,2,0:T(8,128)}, f32[3,64,4,256]{3,2,1,0:...) while((s32[]{:T(128)}, f32[4,128,256]{2,1,0:T(8,128)S(1)}, ...), condition=%wide.region_157.163_spmd.clone, body=%wide.region_146.162_spmd.clone.sunk | while | flops 921016384 | bytes 24206660 | solution.py:184
  4190.3 227.2 %all-reduce.136.cloned.1.call-done = (bf16[192,2048]{1,0:T(8,128)(2,1)}, bf16[192,2048]{1,0:T(8,128)(2,1)}, bf16[192,2048]{1,0:T(8,128)(2,1)}, bf16[192,2048]{1,...) async-done(((bf16[192,2048]{1,0:T(8,128)(2,1)}, bf16[192,2048]{1,0:T(8,128)(2,1)}, ...) | async-done | bytes 6291472 | tf_op jit(solution)/shard_map/psum | solution.py:416
  4624.5 62.8 %reduce-scatter.133.cloned.1.call-done = bf16[256,1408]{1,0:T(8,128)(2,1)} async-done(((bf16[2048,1408]{1,0:T(8,128)(2,1)}), bf16[256,1408]{1,0:T(8,128)(2,1)}) %reduce-scatter.133.cloned.1.call-update) | async-done | bytes 720912 | tf_op jit(solution)/shard_map/reduce_scatter | solution.py:592
  4749.6 62.8 %reduce-scatter.145.cloned.1.call-done = bf16[256,1408]{1,0:T(8,128)(2,1)} async-done(((bf16[2048,1408]{1,0:T(8,128)(2,1)}), bf16[256,1408]{1,0:T(8,128)(2,1)}) %reduce-scatter.145.cloned.1.call-update) | async-done | bytes 720912 | tf_op jit(solution)/shard_map/reduce_scatter | solution.py:598
  4874.9 62.8 %reduce-scatter.141.cloned.1.call-done = bf16[256,1408]{1,0:T(8,128)(2,1)} async-done(((bf16[2048,1408]{1,0:T(8,128)(2,1)}), bf16[256,1408]{1,0:T(8,128)(2,1)}) %reduce-scatter.141.cloned.1.call-update) | async-done | bytes 720912 | tf_op jit(solution)/shard_map/reduce_scatter | solution.py:598
  5000.2 62.8 %reduce-scatter.153.cloned.1.call-done = bf16[1408,256]{1,0:T(8,128)(2,1)} async-done(((bf16[1408,2048]{1,0:T(8,128)(2,1)}), bf16[1408,256]{1,0:T(8,128)(2,1)}) %reduce-scatter.153.cloned.1.call-update) | async-done | bytes 720912 | tf_op jit(solution)/shard_map/reduce_scatter | solution.py:604
  5125.5 62.9 %reduce-scatter.149.cloned.1.call-done = bf16[1408,256]{1,0:T(8,128)(2,1)} async-done(((bf16[1408,2048]{1,0:T(8,128)(2,1)}), bf16[1408,256]{1,0:T(8,128)(2,1)}) %reduce-scatter.149.cloned.1.call-update) | async-done | bytes 720912 | tf_op jit(solution)/shard_map/reduce_scatter | solution.py:604
  (4349 shorter events, 5388.8 us)
Async XLA Ops:
  3711.8 1288.5 %reduce-scatter.155.cloned.1.call-start = ((), (), s32[]{:S(2)}) async-start(), calls=%async_computation.107 | async-start | bytes 6488064 | tf_op jit(solution)/shard_map/reduce_scatter | solution.py:604
  3717.2 1345.7 %reduce-scatter.153.cloned.1.call-start = ((), (), s32[]{:S(2)}) async-start(), calls=%async_computation.106 | async-start | bytes 6488064 | tf_op jit(solution)/shard_map/reduce_scatter | solution.py:604
  3722.9 1402.6 %reduce-scatter.151.cloned.1.call-start = ((), (), s32[]{:S(2)}) async-start(), calls=%async_computation.105 | async-start | bytes 6488064 | tf_op jit(solution)/shard_map/reduce_scatter | solution.py:604
  3728.4 1460.0 %reduce-scatter.149.cloned.1.call-start = ((), (), s32[]{:S(2)}) async-start(), calls=%async_computation.104 | async-start | bytes 6488064 | tf_op jit(solution)/shard_map/reduce_scatter | solution.py:604
  3734.0 1499.5 %reduce-scatter.99.cloned.1.call-start = ((), (), s32[]{:S(2)}) async-start(), calls=%async_computation.79 | async-start | bytes 2359296 | tf_op jit(solution)/shard_map/reduce_scatter | solution.py:520
  3737.2 1541.8 %reduce-scatter.97.cloned.1.call-start = ((), (), s32[]{:S(2)}) async-start(), calls=%async_computation.78 | async-start | bytes 2359296 | tf_op jit(solution)/shard_map/reduce_scatter | solution.py:520
  3740.4 1583.0 %reduce-scatter.95.cloned.1.call-start = ((), (), s32[]{:S(2)}) async-start(), calls=%async_computation.77 | async-start | bytes 2359296 | tf_op jit(solution)/shard_map/reduce_scatter | solution.py:520
  3743.6 1624.5 %reduce-scatter.93.cloned.1.call-start = ((), (), s32[]{:S(2)}) async-start(), calls=%async_computation.76 | async-start | bytes 2359296 | tf_op jit(solution)/shard_map/reduce_scatter | solution.py:520
  3746.8 1666.0 %reduce-scatter.107.cloned.1.call-start = ((), (), s32[]{:S(2)}) async-start(), calls=%async_computation.83 | async-start | bytes 2359296 | tf_op jit(solution)/shard_map/reduce_scatter | solution.py:526
  3750.4 1707.3 %reduce-scatter.105.cloned.1.call-start = ((), (), s32[]{:S(2)}) async-start(), calls=%async_computation.82 | async-start | bytes 2359296 | tf_op jit(solution)/shard_map/reduce_scatter | solution.py:526
  3753.6 1748.6 %reduce-scatter.103.cloned.1.call-start = ((), (), s32[]{:S(2)}) async-start(), calls=%async_computation.81 | async-start | bytes 2359296 | tf_op jit(solution)/shard_map/reduce_scatter | solution.py:526
  3756.8 1790.2 %reduce-scatter.101.cloned.1.call-start = ((), (), s32[]{:S(2)}) async-start(), calls=%async_computation.80 | async-start | bytes 2359296 | tf_op jit(solution)/shard_map/reduce_scatter | solution.py:526
  3760.0 1841.5 %reduce-scatter.123.cloned.1.call-start = ((), (), s32[]{:S(2)}) async-start(), calls=%async_computation.91 | async-start | bytes 4718592 | tf_op jit(solution)/shard_map/reduce_scatter | solution.py:538
  3764.4 1892.1 %reduce-scatter.121.cloned.1.call-start = ((), (), s32[]{:S(2)}) async-start(), calls=%async_computation.90 | async-start | bytes 4718592 | tf_op jit(solution)/shard_map/reduce_scatter | solution.py:538
  3769.0 1942.1 %reduce-scatter.119.cloned.1.call-start = ((), (), s32[]{:S(2)}) async-start(), calls=%async_computation.89 | async-start | bytes 4718592 | tf_op jit(solution)/shard_map/reduce_scatter | solution.py:538
  3773.4 1992.6 %reduce-scatter.117.cloned.1.call-start = ((), (), s32[]{:S(2)}) async-start(), calls=%async_computation.88 | async-start | bytes 4718592 | tf_op jit(solution)/shard_map/reduce_scatter | solution.py:538
  3777.9 2042.9 %reduce-scatter.131.cloned.1.call-start = ((), (), s32[]{:S(2)}) async-start(), calls=%async_computation.95 | async-start | bytes 4718592 | tf_op jit(solution)/shard_map/reduce_scatter | solution.py:580
  3782.8 2093.0 %reduce-scatter.129.cloned.1.call-start = ((), (), s32[]{:S(2)}) async-start(), calls=%async_computation.94 | async-start | bytes 4718592 | tf_op jit(solution)/shard_map/reduce_scatter | solution.py:580
  3787.7 2142.7 %reduce-scatter.127.cloned.1.call-start = ((), (), s32[]{:S(2)}) async-start(), calls=%async_computation.93 | async-start | bytes 4718592 | tf_op jit(solution)/shard_map/reduce_scatter | solution.py:580
  3792.8 2192.7 %reduce-scatter.125.cloned.1.call-start = ((), (), s32[]{:S(2)}) async-start(), calls=%async_computation.92 | async-start | bytes 4718592 | tf_op jit(solution)/shard_map/reduce_scatter | solution.py:580
  3797.7 2245.0 %reduce-scatter.115.cloned.1.call-start = ((), (), s32[]{:S(2)}) async-start(), calls=%async_computation.87 | async-start | bytes 4718592 | tf_op jit(solution)/shard_map/reduce_scatter | solution.py:532
  3801.3 2295.4 %reduce-scatter.113.cloned.1.call-start = ((), (), s32[]{:S(2)}) async-start(), calls=%async_computation.86 | async-start | bytes 4718592 | tf_op jit(solution)/shard_map/reduce_scatter | solution.py:532
  3806.3 2345.0 %reduce-scatter.111.cloned.1.call-start = ((), (), s32[]{:S(2)}) async-start(), calls=%async_computation.85 | async-start | bytes 4718592 | tf_op jit(solution)/shard_map/reduce_scatter | solution.py:532
  3810.8 2395.6 %reduce-scatter.109.cloned.1.call-start = ((), (), s32[]{:S(2)}) async-start(), calls=%async_computation.84 | async-start | bytes 4718592 | tf_op jit(solution)/shard_map/reduce_scatter | solution.py:532
  (941 other events, 43580.1 us)
Sparse Core Ops, SparseCore 0:
  1572.8 239.8 all-reduce.133
  1990.3 223.8 all-reduce.131
  4192.1 225.2 all-reduce.135
  4420.9 73.0 reduce-scatter.138
  4497.7 64.3 reduce-scatter.136
  4565.4 59.0 reduce-scatter.134
  4628.2 59.0 reduce-scatter.132
  4690.5 59.0 reduce-scatter.146
  4753.3 59.0 reduce-scatter.144
  4815.8 59.0 reduce-scatter.142
  4878.6 59.0 reduce-scatter.140
  4941.1 59.0 reduce-scatter.154
  5003.9 59.0 reduce-scatter.152
  5066.4 59.0 reduce-scatter.150
  5129.3 59.0 reduce-scatter.148
  5550.1 51.3 reduce-scatter.122
  5605.2 51.3 reduce-scatter.120
  5659.8 51.3 reduce-scatter.118
  5714.7 51.3 reduce-scatter.116
  5824.5 51.3 reduce-scatter.128
  5934.2 51.3 reduce-scatter.124
  5988.7 53.8 reduce-scatter.114
  6099.9 51.3 reduce-scatter.110
  6155.0 51.3 reduce-scatter.108
  (51 shorter events, 1809.7 us)
where the time goes:
time: 6280 us; the launch traced here: 6240 us
  waiting for transfers between devices  2670 us (43%)
  other arithmetic  1440 us (23%)
  matrix products  880 us (14%)
  local copies, waits for them, and re-layouts  796 us (13%)
  blocking collectives  261 us (4%)
  starting transfers between devices  140 us (2%)
    another operation x192, other arithmetic, solve_lower(): jax.scipy.linalg.solve_triangular(matrix, target, lower=True, unit_diagon...  997 us
    dot_general x312, matrix products, exact_sum(): return jnp.einsum(spec, left, right, precision=lax.Precision.HIGHEST)  424 us
    unnamed x95, waiting for transfers between devices  343 us
    reduce_scatter x4, waiting for transfers between devices, per_device(): lax.psum_scatter(grads_local[14].astype(jnp.bfloat16), ('fsdp', 'ctx'), s...  247 us
    reduce_scatter x4, waiting for transfers between devices, per_device(): lax.psum_scatter(grads_local[15].astype(jnp.bfloat16), ('fsdp', 'ctx'), s...  242 us
    psum x1, waiting for transfers between devices, per_device(): lax.psum(matmul(hidden_low, ffn_down_full).astype(jnp.bfloat16), 'tp')  227 us
    reduce_scatter x4, waiting for transfers between devices, per_device(): lax.psum_scatter(grads_local[4].astype(jnp.bfloat16), ('fsdp', 'ctx'), sc...  217 us
    reduce_scatter x4, waiting for transfers between devices, per_device(): lax.psum_scatter(grads_local[11].astype(jnp.bfloat16), ('fsdp', 'ctx'), s...  217 us

commit v1 on v0

v1 whole, which is shorter than its diff:
```python
import functools
import jax
import jax.numpy as jnp
from jax import lax
from jax.sharding import PartitionSpec as P
from jax.experimental import pallas as pl
from jax.experimental.pallas import tpu as pltpu

CHUNK = 128
LANES = 128
PAD = 8
square_eps = 1e-05
unit_eps = 1e-06
F32 = jnp.float32
BF16 = jnp.bfloat16


def dot_nn(left, right):
    return lax.dot_general(left, right, (((1,), (0,)), ((), ())), preferred_element_type=F32)


def dot_nt(left, right):
    return lax.dot_general(left, right, (((1,), (1,)), ((), ())), preferred_element_type=F32)


def dot_tn(left, right):
    return lax.dot_general(left, right, (((0,), (0,)), ((), ())), preferred_element_type=F32)


def halves(value):
    high = value.astype(BF16)
    return high, (value - high.astype(F32)).astype(BF16)


def dot_fine(left, right):
    left_high, left_low = halves(left)
    right_high, right_low = halves(right)
    return (
        dot_nn(left_high, right_high)
        + dot_nn(left_high, right_low)
        + dot_nn(left_low, right_high)
    )


def sum_by(mask, value):
    high, rest = halves(value)
    middle, low = halves(value - high.astype(F32))
    return dot_nn(mask, high) + dot_nn(mask, middle) + dot_nn(mask, low)


def sigmoid(value):
    return 1.0 / (1.0 + jnp.exp(-value))


def softplus(value):
    return jnp.maximum(value, 0.0) + jnp.log1p(jnp.exp(-jnp.abs(value)))


def inverse_lower(lower_mat, row_id, col_id):
    size = lower_mat.shape[0]

    def level(width):
        same = row_id // (2 * width) == col_id // (2 * width)
        return same & ((row_id // width) % 2 == 1) & ((col_id // width) % 2 == 0)

    unit = jnp.where(row_id == col_id, 1.0, 0.0)
    result = unit - jnp.where(level(1), lower_mat, 0.0)
    width = 2
    while width < size:
        part = jnp.where(level(width), lower_mat, 0.0)
        result = result - dot_fine(dot_fine(result, part), result)
        width *= 2
    return result


def chunk_basics(gates, par, info, seg_row, row_id, col_id, lane_id, head_count):
    step = gates + par[1:2, :]
    log_decay = jnp.where(lane_id < head_count, par[0:1, :] * softplus(step), 0.0)
    beta_raw = sigmoid(gates)
    valid = info[:, 1:2]
    lower = row_id >= col_id
    cumulative = sum_by(jnp.where(lower, 1.0, 0.0).astype(BF16), log_decay)
    both = jnp.where(lane_id < head_count, cumulative, beta_raw * valid)
    turned = jnp.transpose(both)
    inner = lower & (info[:, 0:1] == seg_row)
    return step, log_decay, beta_raw, both, turned, inner


def activations(ext, taps, masks, start, stop, rows):
    value = taps[3:4, start:stop] * ext[PAD : PAD + rows, start:stop]
    for distance in (1, 2, 3):
        shifted = ext[PAD - distance : PAD - distance + rows, start:stop]
        value = value + masks[distance - 1] * (taps[3 - distance : 4 - distance, start:stop] * shifted)
    return value


def forward_kernel(
    head_count, key_size, value_size,
    proj, info_ref, segr, par_ref, taps, gain_ref,
    normed_out, state_out, inverse_out, pseudo_out, output_out,
    state, ext,
):
    rows = proj.shape[0]
    width = head_count * (2 * key_size + value_size)
    gate_at = width
    tail_at = width + head_count * value_size

    @pl.when(pl.program_id(0) == 0)
    def start():
        state[...] = jnp.zeros_like(state)
        ext[0:PAD, :] = jnp.zeros((PAD, width), F32)

    ext[PAD : PAD + rows, :] = proj[:, 0:width]
    info = info_ref[...]
    row_id = lax.broadcasted_iota(jnp.int32, (rows, rows), 0)
    col_id = lax.broadcasted_iota(jnp.int32, (rows, rows), 1)
    lane_id = lax.broadcasted_iota(jnp.int32, (rows, LANES), 1)
    masks = tuple(info[:, 1 + d : 2 + d] for d in (1, 2, 3))
    valid = info[:, 1:2]
    unused, log_decay, beta_raw, both, turned, inner = chunk_basics(
        proj[:, tail_at : tail_at + LANES], par_ref[...], info, segr[0:1, :],
        row_id, col_id, lane_id, head_count,
    )
    carried_mask = info[:, 8:9]
    tail_mask = info[:, 9:10]
    strict = row_id > col_id
    key_at = head_count * key_size
    value_at = 2 * key_at
    for head in range(head_count):
        ks = key_size
        vs = value_size
        act_q = activations(ext, taps, masks, head * ks, (head + 1) * ks, rows)
        act_k = activations(ext, taps, masks, key_at + head * ks, key_at + (head + 1) * ks, rows)
        act_v = activations(ext, taps, masks, value_at + head * vs, value_at + (head + 1) * vs, rows)
        cq = act_q * sigmoid(act_q)
        ck = act_k * sigmoid(act_k)
        values = act_v * sigmoid(act_v)
        query = cq * (lax.rsqrt(jnp.sum(cq * cq, axis=1, keepdims=True) + unit_eps) * ks ** -0.5)
        key = ck * lax.rsqrt(jnp.sum(ck * ck, axis=1, keepdims=True) + unit_eps)
        qb = query.astype(BF16)
        kb = key.astype(BF16)
        cum = both[:, head : head + 1]
        beta = both[:, head_count + head : head_count + head + 1]
        cum_row = turned[head : head + 1, :]
        beta_row = turned[head_count + head : head_count + head + 1, :]
        decays = jnp.where(inner, jnp.exp(jnp.minimum(cum - cum_row, 0.0)), 0.0)
        lower_mat = jnp.where(strict, decays * dot_nt(kb, kb) * beta_row, 0.0)
        inverse = inverse_lower(lower_mat, row_id, col_id)
        carried = jnp.exp(cum) * carried_mask
        last = cum[rows - 1 : rows, :]
        tail = jnp.exp(last - cum) * tail_mask
        keep = carried[rows - 1 : rows, :]
        before = state[head]
        state_out[0, head] = before
        sb = before.astype(BF16)
        target = values - carried * dot_nn(kb, sb)
        ib = inverse.astype(BF16)
        pseudo = dot_nn(ib, target.astype(BF16))
        inverse_out[0, head] = ib
        pseudo_out[:, head * vs : (head + 1) * vs] = pseudo
        weighted = beta * pseudo
        mix = decays * dot_nt(qb, kb)
        output = carried * dot_nn(qb, sb) + dot_nn(mix.astype(BF16), weighted.astype(BF16))
        output_out[:, head * vs : (head + 1) * vs] = output
        state[head] = keep * before + dot_tn(kb, (tail * weighted).astype(BF16))
        gate = proj[:, gate_at + head * vs : gate_at + (head + 1) * vs]
        scale = lax.rsqrt(jnp.mean(output * output, axis=1, keepdims=True) + square_eps)
        normed = output * scale * gain_ref[0:1, :] * (gate * sigmoid(gate)) * valid
        normed_out[:, head * vs : (head + 1) * vs] = normed.astype(BF16)
    ext[0:PAD, :] = ext[rows : rows + PAD, :]


def backward_kernel(
    head_count, key_size, value_size,
    proj, prior, info_ref, segr, par_ref, taps, gain_ref,
    state_in, inverse_in, pseudo_in, output_in, dnormed,
    grad_out, conv_out, gain_out, small_out,
    dstate, ext, dext,
):
    rows = proj.shape[0]
    width = head_count * (2 * key_size + value_size)
    gate_at = width
    tail_at = width + head_count * value_size
    place = pl.program_id(0)
    count = pl.num_programs(0)

    @pl.when(place == 0)
    def start():
        dstate[...] = jnp.zeros_like(dstate)
        dext[rows : rows + PAD, :] = jnp.zeros((PAD, width), F32)
        conv_out[...] = jnp.zeros_like(conv_out)
        gain_out[...] = jnp.zeros_like(gain_out)
        small_out[...] = jnp.zeros_like(small_out)

    first = place == count - 1
    ext[0:PAD, :] = jnp.where(first, 0.0, prior[:, 0:width])
    ext[PAD : PAD + rows, :] = proj[:, 0:width]
    info = info_ref[...]
    row_id = lax.broadcasted_iota(jnp.int32, (rows, rows), 0)
    col_id = lax.broadcasted_iota(jnp.int32, (rows, rows), 1)
    lane_id = lax.broadcasted_iota(jnp.int32, (rows, LANES), 1)
    masks = tuple(info[:, 1 + d : 2 + d] for d in (1, 2, 3))
    later = tuple(info[:, 4 + d : 5 + d] for d in (1, 2, 3))
    valid = info[:, 1:2]
    step, log_decay, beta_raw, both, turned, inner = chunk_basics(
        proj[:, tail_at : tail_at + LANES], par_ref[...], info, segr[0:1, :],
        row_id, col_id, lane_id, head_count,
    )
    carried_mask = info[:, 8:9]
    tail_mask = info[:, 9:10]
    strict = row_id > col_id
    last_row = lax.broadcasted_iota(jnp.int32, (rows, 1), 0) == rows - 1
    row_of = lax.broadcasted_iota(jnp.int32, (LANES, rows), 0)
    ks = key_size
    vs = value_size
    key_at = head_count * ks
    value_at = 2 * key_at
    dcum = jnp.zeros((rows, LANES), F32)
    dturned = jnp.zeros((LANES, rows), F32)

    def fold(value):
        return jnp.sum(value.reshape(rows // PAD, PAD, value.shape[1]), axis=0)

    def conv_back(da, start, stop):
        dext[0:rows, start:stop] = da
        back = taps[3:4, start:stop] * da
        conv_out[3 * PAD : 4 * PAD, start:stop] += fold(da * ext[PAD : PAD + rows, start:stop])
        for d in (1, 2, 3):
            back = back + later[d - 1] * (taps[3 - d : 4 - d, start:stop] * dext[d : d + rows, start:stop])
            shifted = ext[PAD - d : PAD - d + rows, start:stop]
            conv_out[(3 - d) * PAD : (4 - d) * PAD, start:stop] += fold(masks[d - 1] * da * shifted)
        grad_out[:, start:stop] = back.astype(BF16)

    for head in range(head_count):
        act_q = activations(ext, taps, masks, head * ks, (head + 1) * ks, rows)
        act_k = activations(ext, taps, masks, key_at + head * ks, key_at + (head + 1) * ks, rows)
        act_v = activations(ext, taps, masks, value_at + head * vs, value_at + (head + 1) * vs, rows)
        sig_q, sig_k, sig_v = sigmoid(act_q), sigmoid(act_k), sigmoid(act_v)
        cq, ck, values = act_q * sig_q, act_k * sig_k, act_v * sig_v
        rate_q = lax.rsqrt(jnp.sum(cq * cq, axis=1, keepdims=True) + unit_eps)
        rate_k = lax.rsqrt(jnp.sum(ck * ck, axis=1, keepdims=True) + unit_eps)
        unit_q = cq * rate_q
        query = unit_q * ks ** -0.5
        key = ck * rate_k
        qb = query.astype(BF16)
        kb = key.astype(BF16)
        cum = both[:, head : head + 1]
        beta = both[:, head_count + head : head_count + head + 1]
        cum_row = turned[head : head + 1, :]
        beta_row = turned[head_count + head : head_count + head + 1, :]
        decays = jnp.where(inner, jnp.exp(jnp.minimum(cum - cum_row, 0.0)), 0.0)
        carried = jnp.exp(cum) * carried_mask
        tail = jnp.exp(cum[rows - 1 : rows, :] - cum) * tail_mask
        keep = carried[rows - 1 : rows, :]
        before = state_in[0, head]
        sb = before.astype(BF16)
        ib = inverse_in[0, head]
        pseudo = pseudo_in[:, head * vs : (head + 1) * vs]
        output = output_in[:, head * vs : (head + 1) * vs]
        gate = proj[:, gate_at + head * vs : gate_at + (head + 1) * vs]
        given = dnormed[:, head * vs : (head + 1) * vs] * valid
        gain = gain_ref[0:1, :]
        scale = lax.rsqrt(jnp.mean(output * output, axis=1, keepdims=True) + square_eps)
        unit_o = output * scale
        sig_g = sigmoid(gate)
        silu_g = gate * sig_g
        dunit = given * gain * silu_g
        doutput = scale * (dunit - unit_o * jnp.mean(unit_o * dunit, axis=1, keepdims=True))
        dgate = given * unit_o * gain * (sig_g * (1.0 + gate * (1.0 - sig_g)))
        gain_out[:, head * vs : (head + 1) * vs] += fold(given * unit_o * silu_g)
        grad_out[:, gate_at + head * vs : gate_at + (head + 1) * vs] = dgate.astype(BF16)
        dob = doutput.astype(BF16)
        weighted = beta * pseudo
        wb = weighted.astype(BF16)
        gram = dot_nt(kb, kb)
        cross = dot_nt(qb, kb)
        mix = decays * cross
        after = dstate[head]
        ab = after.astype(BF16)
        from_state = dot_nn(kb, ab)
        dweighted = dot_tn(mix.astype(BF16), dob) + tail * from_state
        dbeta = jnp.sum(dweighted * pseudo, axis=1, keepdims=True)
        dtarget = dot_tn(ib, (beta * dweighted).astype(BF16))
        dtb = dtarget.astype(BF16)
        read = dot_nn(kb, sb)
        dcarried = jnp.sum(doutput * dot_nn(qb, sb), axis=1, keepdims=True) - jnp.sum(
            dtarget * read, axis=1, keepdims=True
        )
        dtail = jnp.sum(weighted * from_state, axis=1, keepdims=True)
        dkeep = jnp.sum(jnp.sum(after * before, axis=1, keepdims=True), axis=0, keepdims=True)
        cdo = (carried * doutput).astype(BF16)
        cdt = (carried * dtarget).astype(BF16)
        dstate[head] = keep * after + dot_tn(qb, cdo) - dot_tn(kb, cdt)
        dmix = dot_nt(dob, wb)
        dcross = (dmix * decays).astype(BF16)
        dlower = jnp.where(strict, -dot_nt(dtb, pseudo.astype(BF16)), 0.0) * decays
        dgram = (dlower * beta_row).astype(BF16)
        plain = dlower * gram
        inner_grad = dmix * mix + plain * beta_row
        dquery = dot_nt(cdo, sb) + dot_nn(dcross, kb)
        dkey = (
            dot_tn(dcross, qb)
            + dot_nn(dgram, kb)
            + dot_tn(dgram, kb)
            + dot_nt((tail * weighted).astype(BF16), ab)
            - dot_nt(cdt, sb)
        )
        dlast = jnp.sum(dtail * tail, axis=0, keepdims=True) + dkeep * keep
        dcum_col = (
            jnp.sum(inner_grad, axis=1, keepdims=True)
            + dcarried * carried
            - dtail * tail
            + jnp.where(last_row, dlast, 0.0)
        )
        dcum = jnp.where(lane_id == head, dcum_col, dcum)
        dcum = jnp.where(lane_id == head_count + head, dbeta, dcum)
        dturned = jnp.where(row_of == head, -jnp.sum(inner_grad, axis=0, keepdims=True), dturned)
        dturned = jnp.where(
            row_of == head_count + head, jnp.sum(plain, axis=0, keepdims=True), dturned
        )
        dq_scaled = dquery * ks ** -0.5
        dcq = (dq_scaled - unit_q * jnp.sum(unit_q * dq_scaled, axis=1, keepdims=True)) * rate_q
        dck = (dkey - key * jnp.sum(key * dkey, axis=1, keepdims=True)) * rate_k
        conv_back(dcq * (sig_q * (1.0 + act_q * (1.0 - sig_q))), head * ks, (head + 1) * ks)
        conv_back(
            dck * (sig_k * (1.0 + act_k * (1.0 - sig_k))), key_at + head * ks, key_at + (head + 1) * ks
        )
        conv_back(
            dtarget * (sig_v * (1.0 + act_v * (1.0 - sig_v))),
            value_at + head * vs,
            value_at + (head + 1) * vs,
        )
    dboth = dcum + jnp.transpose(dturned)
    upper = jnp.where(row_id <= col_id, 1.0, 0.0).astype(BF16)
    dlog = sum_by(upper, jnp.where(lane_id < head_count, dboth, 0.0))
    dalpha = dlog * par_ref[0:1, :] * sigmoid(step)
    dbeta_raw = dboth * valid * beta_raw * (1.0 - beta_raw)
    tail_grad = jnp.where(
        lane_id < head_count, dalpha, jnp.where(lane_id < 2 * head_count, dbeta_raw, 0.0)
    )
    grad_out[:, tail_at : tail_at + LANES] = tail_grad.astype(BF16)
    small_out[0:PAD, :] += fold(dlog * log_decay)
    small_out[PAD : 2 * PAD, :] += fold(jnp.where(lane_id < head_count, dalpha, 0.0))
    dext[rows : rows + PAD, :] = dext[0:PAD, :]


def delta_forward(proj, info, seg_rows, par, taps, gain, sizes):
    head_count, key_size, value_size = sizes
    total, columns = proj.shape
    steps = total // CHUNK
    width = head_count * (2 * key_size + value_size)
    span = head_count * value_size
    whole = lambda a: pl.BlockSpec(a.shape, lambda i: (0, 0))
    by_rows = lambda n: pl.BlockSpec((CHUNK, n), lambda i: (i, 0))
    return pl.pallas_call(
        functools.partial(forward_kernel, head_count, key_size, value_size),
        grid=(steps,),
        in_specs=[
            by_rows(columns),
            by_rows(LANES),
            pl.BlockSpec((PAD, CHUNK), lambda i: (0, i)),
            whole(par),
            whole(taps),
            whole(gain),
        ],
        out_specs=[
            by_rows(span),
            pl.BlockSpec((1, head_count, key_size, value_size), lambda i: (i, 0, 0, 0)),
            pl.BlockSpec((1, head_count, CHUNK, CHUNK), lambda i: (i, 0, 0, 0)),
            by_rows(span),
            by_rows(span),
        ],
        out_shape=[
            jax.ShapeDtypeStruct((total, span), BF16),
            jax.ShapeDtypeStruct((steps, head_count, key_size, value_size), F32),
            jax.ShapeDtypeStruct((steps, head_count, CHUNK, CHUNK), BF16),
            jax.ShapeDtypeStruct((total, span), F32),
            jax.ShapeDtypeStruct((total, span), F32),
        ],
        scratch_shapes=[
            pltpu.VMEM((head_count, key_size, value_size), F32),
            pltpu.VMEM((CHUNK + PAD, width), F32),
        ],
        compiler_params=pltpu.CompilerParams(vmem_limit_bytes=48 * 1024 * 1024),
        name="delta_forward",
    )(proj, info, seg_rows, par, taps, gain)


def delta_backward(proj, info, seg_rows, par, taps, gain, saved, dnormed, sizes):
    head_count, key_size, value_size = sizes
    total, columns = proj.shape
    steps = total // CHUNK
    width = head_count * (2 * key_size + value_size)
    span = head_count * value_size
    states, inverses, pseudos, outputs = saved
    blocks = CHUNK // PAD
    turn = lambda i: steps - 1 - i
    whole = lambda a: pl.BlockSpec(a.shape, lambda i: (0, 0))
    by_rows = lambda n: pl.BlockSpec((CHUNK, n), lambda i: (turn(i), 0))
    return pl.pallas_call(
        functools.partial(backward_kernel, head_count, key_size, value_size),
        grid=(steps,),
        in_specs=[
            by_rows(columns),
            pl.BlockSpec((PAD, columns), lambda i: (jnp.maximum(turn(i) * blocks - 1, 0), 0)),
            by_rows(LANES),
            pl.BlockSpec((PAD, CHUNK), lambda i: (0, turn(i))),
            whole(par),
            whole(taps),
            whole(gain),
            pl.BlockSpec((1, head_count, key_size, value_size), lambda i: (turn(i), 0, 0, 0)),
            pl.BlockSpec((1, head_count, CHUNK, CHUNK), lambda i: (turn(i), 0, 0, 0)),
            by_rows(span),
            by_rows(span),
            by_rows(span),
        ],
        out_specs=[
            by_rows(columns),
            pl.BlockSpec((4 * PAD, width), lambda i: (0, 0)),
            pl.BlockSpec((PAD, span), lambda i: (0, 0)),
            pl.BlockSpec((2 * PAD, LANES), lambda i: (0, 0)),
        ],
        out_shape=[
            jax.ShapeDtypeStruct((total, columns), BF16),
            jax.ShapeDtypeStruct((4 * PAD, width), F32),
            jax.ShapeDtypeStruct((PAD, span), F32),
            jax.ShapeDtypeStruct((2 * PAD, LANES), F32),
        ],
        scratch_shapes=[
            pltpu.VMEM((head_count, key_size, value_size), F32),
            pltpu.VMEM((CHUNK + PAD, width), F32),
            pltpu.VMEM((CHUNK + PAD, width), F32),
        ],
        compiler_params=pltpu.CompilerParams(vmem_limit_bytes=48 * 1024 * 1024),
        name="delta_backward",
    )(proj, proj, info, seg_rows, par, taps, gain, states, inverses, pseudos, outputs, dnormed)


def place_arrays(length_row, total):
    places = jnp.arange(total, dtype=jnp.int32)
    ids = jnp.arange(length_row.shape[0])
    ends = jnp.sum(jnp.where(ids[None, :] <= ids[:, None], length_row[None, :], 0), axis=1)
    starts = ends - length_row

    def seg_at(at):
        return jnp.sum((at[:, None] >= starts[None, :]).astype(jnp.int32), axis=1) - 1

    segment = seg_at(places)
    valid = (places < ends[-1]).astype(F32)
    lanes = [segment.astype(F32), valid]
    for d in (1, 2, 3):
        lanes.append((seg_at(places - d) == segment).astype(F32))
    for d in (1, 2, 3):
        lanes.append(((seg_at(places + d) == segment) & (places + d < total)).astype(F32))
    head_place = places - places % CHUNK
    lanes.append(((seg_at(head_place - 1) == segment) & (head_place > 0)).astype(F32))
    lanes.append((seg_at(head_place + CHUNK - 1) == segment).astype(F32))
    info = jnp.stack(lanes, axis=1)
    info = jnp.pad(info, ((0, 0), (0, LANES - len(lanes))))
    rows = jnp.broadcast_to(segment.astype(F32)[None, :], (PAD, total))
    return info, rows


GROUP = ("fsdp", "ctx")


def pair_rows(values):
    high, low = halves(values)
    return jnp.stack([high, low], axis=-2)


def share_sum(part):
    count = lax.axis_size("tp")
    moved = lax.all_to_all(part, "tp", split_axis=0, concat_axis=0, tiled=True)
    return jnp.sum(moved.reshape(count, -1, part.shape[1]).astype(F32), axis=0)


def per_device(
    tokens, cotangent, lengths, order, gain_in, query_proj, key_proj, value_proj, gate_proj,
    alpha_proj, beta_proj, query_conv, key_conv, value_conv, decay_log, step_bias, gain_head,
    out_proj, gain_mid, ffn_gate, ffn_up, ffn_down,
):
    groups = lax.axis_size(GROUP)
    tp_count = lax.axis_size("tp")
    tp_place = lax.axis_index("tp")
    group = lax.axis_index(GROUP)
    micros, rows, width = tokens.shape
    packs = lengths.shape[1]
    all_rows = order.shape[1]
    pack_rows = all_rows // packs
    assert micros * packs == groups and pack_rows == tp_count * rows
    share = rows // groups
    heads = decay_log.shape[0]
    spans = query_conv.shape[0]
    key_size = query_conv.shape[2] * groups
    value_size = value_conv.shape[2] * groups
    sizes = (heads, key_size, value_size)
    key_cols = heads * key_size
    value_cols = heads * value_size
    own = width // groups
    my_micro = group // packs
    my_pack = group % packs

    strict_up = jnp.triu(jnp.ones((rows, rows), BF16), 1)
    mine = (order // rows == group).reshape(micros * packs * tp_count, rows)
    rank = jnp.dot(mine.astype(BF16), strict_up, preferred_element_type=F32).astype(jnp.int32)
    rank = rank.reshape(micros, packs, tp_count, rows)
    ids = jnp.arange(packs * tp_count, dtype=jnp.int32).reshape(packs, tp_count, 1)
    send_slot = (ids * share + rank).reshape(micros, 1, all_rows)
    held = rows + PAD
    pack_id = jnp.arange(groups, dtype=jnp.int32).reshape(micros, packs, 1, 1)
    tp_id = jnp.arange(tp_count, dtype=jnp.int32).reshape(tp_count, 1)
    back_slot = (tp_id * held + pack_id * share + rank).reshape(micros, 1, all_rows)
    local = group * rows + jnp.arange(rows, dtype=jnp.int32)
    hit = order[:, None, :] == local[None, :, None]
    send_at = jnp.sum(jnp.where(hit, send_slot, 0), axis=2)
    back_at = jnp.sum(jnp.where(hit, back_slot, 0), axis=2).reshape(micros * rows)
    row_ids = jnp.arange(rows, dtype=jnp.int32)
    send_pick = (row_ids[None, :, None] == send_at[:, None, :]).astype(BF16)
    back_ids = jnp.arange(tp_count * held, dtype=jnp.int32)
    back_pick = (back_at[:, None] == back_ids[None, :]).astype(BF16)

    pack_order = lax.dynamic_slice(order, (my_micro, my_pack * pack_rows), (1, pack_rows))
    source = (pack_order // rows).reshape(tp_count, rows)
    from_each = (source[:, :, None] == jnp.arange(groups, dtype=jnp.int32)).astype(BF16)
    before = jnp.einsum(
        "qp,tqg->tpg", strict_up, from_each, preferred_element_type=F32
    )
    source_rank = jnp.sum(before * from_each.astype(F32), axis=2).astype(jnp.int32)
    arrive_at = source * (tp_count * share) + tp_id * share + source_rank
    pack_ids = jnp.arange(pack_rows, dtype=jnp.int32)
    arrive_pick = (arrive_at.reshape(pack_rows, 1) == pack_ids[None, :]).astype(BF16)
    return_at = lax.dynamic_slice(source * share + source_rank, (tp_place, 0), (1, rows))
    return_pick = (row_ids[:, None] == return_at).astype(BF16)

    def to_pack(values):
        sent = jnp.einsum("msi,mid->msd", send_pick, values, preferred_element_type=F32)
        sent = sent.astype(BF16).reshape(micros * rows, width)
        moved = lax.all_to_all(sent, GROUP, split_axis=0, concat_axis=0, tiled=True)
        return jnp.dot(arrive_pick, moved, preferred_element_type=F32).astype(BF16)

    def to_given(values, extra):
        sent = jnp.dot(return_pick, values.astype(BF16), preferred_element_type=F32).astype(BF16)
        sent = sent.reshape(groups, share, width)
        if extra is not None:
            sent = jnp.concatenate([sent, extra], axis=1)
        return lax.all_to_all(sent, GROUP, split_axis=0, concat_axis=0, tiled=True)

    def spread(values):
        full = lax.all_gather(values, "tp", axis=0, tiled=True)
        picked = jnp.dot(back_pick, full, preferred_element_type=F32).astype(BF16)
        return picked.reshape(micros, rows, width), full

    small = jnp.concatenate(
        [
            gain_in[None],
            gain_mid[None],
            query_conv.reshape(-1, own),
            key_conv.reshape(-1, own),
            value_conv.reshape(-1, own),
            jnp.pad(gain_head, (0, own - gain_head.shape[0]))[None],
        ],
        axis=0,
    )
    small = jnp.pad(small, ((0, LANES - 2 * heads - small.shape[0]), (0, 0)))
    mixer_weight = lax.all_gather(
        jnp.concatenate(
            [query_proj, key_proj, value_proj, gate_proj, alpha_proj, beta_proj, small.T], axis=1
        ),
        GROUP, axis=0, tiled=True,
    )
    x_low = to_pack(tokens)
    out_weight = lax.all_gather(out_proj.T, GROUP, axis=0, tiled=True)
    pair_weight = lax.all_gather(
        jnp.concatenate([ffn_gate, ffn_up], axis=1), GROUP, axis=0, tiled=True
    )
    down_weight = lax.all_gather(ffn_down.T, GROUP, axis=0, tiled=True)
    dy_low = to_pack(cotangent)

    tail_at = 2 * key_cols + 2 * value_cols
    extras = mixer_weight[:, tail_at:].T[2 * heads :].astype(F32)
    gain_in_full = extras[0:1]
    gain_mid_full = extras[1:2]

    def taps_of(start, weight):
        count = weight.size // own
        flat = extras[start : start + count].reshape(count, groups, own)
        flat = jnp.transpose(flat, (1, 0, 2)).reshape(groups, spans, heads, weight.shape[2])
        return jnp.transpose(flat, (1, 2, 0, 3)).reshape(spans, -1), start + count

    query_taps, at = taps_of(2, query_conv)
    key_taps, at = taps_of(at, key_conv)
    value_taps, at = taps_of(at, value_conv)
    taps = jnp.pad(
        jnp.concatenate([query_taps, key_taps, value_taps], axis=1), ((0, PAD - spans), (0, 0))
    )
    head_gain = extras[at].reshape(groups, own)[:, : gain_head.shape[0]].reshape(1, value_size)
    head_gain = jnp.broadcast_to(head_gain, (PAD, value_size))
    par = jnp.zeros((PAD, LANES), F32)
    par = par.at[0, :heads].set(-jnp.exp(decay_log)).at[1, :heads].set(step_bias)
    length_row = lax.dynamic_slice(
        lengths, (my_micro, my_pack, 0), (1, 1, lengths.shape[2])
    ).reshape(-1)
    info, seg_rows = place_arrays(length_row, pack_rows)

    x_float = x_low.astype(F32)
    rate_in = lax.rsqrt(jnp.mean(x_float * x_float, axis=1, keepdims=True) + square_eps)
    normed_in = (x_float * rate_in * gain_in_full).astype(BF16)
    proj = dot_nn(normed_in, mixer_weight)
    normed_low, *saved = delta_forward(proj, info, seg_rows, par, taps, head_gain, sizes)

    def my_rows(values):
        return lax.dynamic_slice(values, (tp_place * rows, 0), (rows, values.shape[1])).astype(F32)

    hidden_in = my_rows(x_low) + share_sum(dot_nt(normed_low, out_weight).astype(BF16))
    rate_mid = lax.rsqrt(jnp.mean(hidden_in * hidden_in, axis=1, keepdims=True) + square_eps)
    mid_low = lax.all_gather(
        (hidden_in * rate_mid * gain_mid_full).astype(BF16), "tp", axis=0, tiled=True
    )
    units = ffn_gate.shape[1]
    both = dot_nn(mid_low, pair_weight)
    gate_value, up_value = both[:, :units], both[:, units:]
    gate_sig = sigmoid(gate_value)
    gate_act = gate_value * gate_sig
    hidden_low = (gate_act * up_value).astype(BF16)
    grad_hidden = dot_nn(dy_low, down_weight)
    pair_grad = jnp.concatenate(
        [
            (grad_hidden * up_value * (gate_sig * (1.0 + gate_value * (1.0 - gate_sig)))).astype(BF16),
            (grad_hidden * gate_act).astype(BF16),
        ],
        axis=1,
    )
    mid_grad = share_sum(dot_nt(pair_grad, pair_weight).astype(BF16))
    ffn_part = dot_nt(hidden_low, down_weight).astype(BF16)

    scaled = mid_grad * gain_mid_full
    hidden_grad = (
        my_rows(dy_low)
        + rate_mid * scaled
        - rate_mid**3 * hidden_in * jnp.mean(hidden_in * scaled, axis=1, keepdims=True)
    )
    grad_mid_gain = jnp.sum(mid_grad * hidden_in * rate_mid, axis=0)
    mix_low = lax.all_gather(hidden_grad.astype(BF16), "tp", axis=0, tiled=True)
    mix_low, ffn_part = lax.optimization_barrier((mix_low, ffn_part))
    dnormed = dot_nn(mix_low, out_weight)
    grad_proj, conv_grad, head_gain_grad, decay_grads = delta_backward(
        proj, info, seg_rows, par, taps, head_gain, saved, dnormed, sizes
    )
    first_grad = share_sum(dot_nt(grad_proj, mixer_weight).astype(BF16))

    result = hidden_in + share_sum(ffn_part)
    result_back = to_given(result, None).reshape(rows, width)
    mixed, unused = spread(jnp.pad(result_back, ((0, PAD), (0, 0))))

    def owners(value, axis):
        return lax.psum_scatter(
            value.astype(BF16), GROUP, scatter_dimension=axis, tiled=True
        ).astype(F32)

    grad_pair = owners(dot_tn(mid_low, pair_grad), 0)
    grad_down = owners(dot_tn(dy_low, hidden_low), 0).T
    grad_out = owners(dot_tn(mix_low, normed_low), 0).T
    grad_mixer = owners(dot_tn(normed_in, grad_proj), 0)

    x_own = my_rows(x_low)
    rate_own = lax.rsqrt(jnp.mean(x_own * x_own, axis=1, keepdims=True) + square_eps)
    scaled_in = first_grad * gain_in_full
    token_grad = (
        hidden_grad
        + rate_own * scaled_in
        - rate_own**3 * x_own * jnp.mean(x_own * scaled_in, axis=1, keepdims=True)
    )
    grad_in_gain = jnp.sum(first_grad * x_own * rate_own, axis=0)

    conv_sum = jnp.sum(conv_grad.reshape(spans, PAD, -1), axis=1)

    def taps_to(value, size):
        parted = value.reshape(spans, heads, groups, size // groups)
        return jnp.transpose(parted, (2, 0, 1, 3)).reshape(groups, -1)

    gain_sum = jnp.sum(head_gain_grad.reshape(PAD * heads, value_size), axis=0)
    decay_sums = jnp.sum(decay_grads.reshape(2, PAD, LANES), axis=1)[:, :heads].reshape(1, -1)
    parts = [
        grad_in_gain.reshape(groups, own),
        grad_mid_gain.reshape(groups, own),
        gain_sum.reshape(groups, -1),
        taps_to(conv_sum[:, :key_cols], key_size),
        taps_to(conv_sum[:, key_cols : 2 * key_cols], key_size),
        taps_to(conv_sum[:, 2 * key_cols :], value_size),
        jnp.broadcast_to(decay_sums, (groups, decay_sums.shape[1])),
    ]
    lens = [part.shape[1] for part in parts]
    packed = jnp.concatenate(parts, axis=1)
    packed = jnp.pad(packed, ((0, 0), (0, width - packed.shape[1])))
    extra = jnp.pad(pair_rows(packed), ((0, 0), (0, PAD - 2), (0, 0)))
    came = to_given(token_grad, extra)
    summed = jnp.sum(came[:, share : share + 2].astype(F32), axis=(0, 1))
    block = jnp.concatenate(
        [
            came[:, :share].reshape(rows, width),
            jnp.pad(pair_rows(summed), ((0, PAD - 2), (0, 0))),
        ],
        axis=0,
    )
    grad_tokens, full = spread(block)
    tp_summed = jnp.sum(
        full.reshape(tp_count, held, width)[:, rows : rows + 2].astype(F32), axis=(0, 1)
    )
    pieces = []
    offset = 0
    for index, length in enumerate(lens):
        origin = tp_summed if index < 3 else summed
        pieces.append(origin[offset : offset + length])
        offset += length
    decay_pair = pieces[6].reshape(2, heads)
    edges = [0, key_cols, 2 * key_cols, 2 * key_cols + value_cols, tail_at]
    return (
        mixed,
        grad_tokens,
        pieces[0],
        grad_mixer[:, edges[0] : edges[1]],
        grad_mixer[:, edges[1] : edges[2]],
        grad_mixer[:, edges[2] : edges[3]],
        grad_mixer[:, edges[3] : edges[4]],
        grad_mixer[:, tail_at : tail_at + heads],
        grad_mixer[:, tail_at + heads : tail_at + 2 * heads],
        pieces[3].reshape(query_conv.shape),
        pieces[4].reshape(key_conv.shape),
        pieces[5].reshape(value_conv.shape),
        decay_pair[0],
        decay_pair[1],
        pieces[2],
        grad_out,
        pieces[1],
        grad_pair[:, :units],
        grad_pair[:, units:],
        grad_down,
    )


def solution(mesh):
    in_specs = (
        P(None, ("fsdp", "ctx"), None),
        P(None, ("fsdp", "ctx"), None),
        P(),
        P(),
        P(("fsdp", "ctx")),
        P(("fsdp", "ctx"), "tp"),
        P(("fsdp", "ctx"), "tp"),
        P(("fsdp", "ctx"), "tp"),
        P(("fsdp", "ctx"), "tp"),
        P(("fsdp", "ctx"), "tp"),
        P(("fsdp", "ctx"), "tp"),
        P(None, "tp", ("fsdp", "ctx")),
        P(None, "tp", ("fsdp", "ctx")),
        P(None, "tp", ("fsdp", "ctx")),
        P("tp"),
        P("tp"),
        P(("fsdp", "ctx")),
        P("tp", ("fsdp", "ctx")),
        P(("fsdp", "ctx")),
        P(("fsdp", "ctx"), "tp"),
        P(("fsdp", "ctx"), "tp"),
        P("tp", ("fsdp", "ctx")),
    )
    out_specs = (
        P(None, ("fsdp", "ctx"), None),
        P(None, ("fsdp", "ctx"), None),
        P(("fsdp", "ctx")),
        P(("fsdp", "ctx"), "tp"),
        P(("fsdp", "ctx"), "tp"),
        P(("fsdp", "ctx"), "tp"),
        P(("fsdp", "ctx"), "tp"),
        P(("fsdp", "ctx"), "tp"),
        P(("fsdp", "ctx"), "tp"),
        P(None, "tp", ("fsdp", "ctx")),
        P(None, "tp", ("fsdp", "ctx")),
        P(None, "tp", ("fsdp", "ctx")),
        P("tp"),
        P("tp"),
        P(("fsdp", "ctx")),
        P("tp", ("fsdp", "ctx")),
        P(("fsdp", "ctx")),
        P(("fsdp", "ctx"), "tp"),
        P(("fsdp", "ctx"), "tp"),
        P("tp", ("fsdp", "ctx")),
    )
    return jax.shard_map(
        per_device, mesh=mesh, in_specs=in_specs, out_specs=out_specs, check_vma=False
    )
```

time: 6280 us -> 1040 us (0.17)
  waiting for transfers between devices: 2670 us -> 512 us
  other arithmetic: 1440 us -> 32.4 us
  local copies, waits for them, and re-layouts: 796 us -> 46.2 us
  matrix products: 880 us -> 182 us
  blocking collectives: 261 us -> 135 us
  starting transfers between devices: 140 us -> 24.4 us
  Pallas kernels: 0 us -> 93.5 us
    reduce_scatter x32 -> x4, waiting for transfers between devices: 1620 us -> 88.4 us  [owners(): lax.psum_scatter(value.astype(BF16), GROUP, scatter_dimension=axis, tiled...]
    another operation x246 -> x4, other arithmetic: 1020 us -> 0.05 us  [the longest x3 0.05 us: pair_rows(): return jnp.stack([high, low], axis=-2)]
    dot_general x444 -> x22, matrix products: 804 us -> 182 us  [the longest x4 54.6 us: dot_nn(): lax.dot_general(left, right, (((1,), (0,)), ((), ())), preferred_element_...]
    psum x3 -> x0, waiting for transfers between devices: 504 us -> none  [the longest x1 227 us: per_device(): lax.psum(matmul(hidden_low, ffn_down_full).astype(jnp.bfloat16), 'tp')]
    unnamed x95 -> x12, waiting for transfers between devices: 343 us -> 1.39 us
    all_gather x11 -> x0, blocking collectives: 188 us -> none  [the longest x4 42.3 us: entering(): lax.all_gather(a.astype(kind), axis)]
    all_to_all x0 -> x3, blocking collectives: none -> 135 us  [the longest x1 75.5 us: share_sum(): moved = lax.all_to_all(part, 'tp', split_axis=0, concat_axis=0, tiled=True)]
    all_to_all x16 -> x5, waiting for transfers between devices: 77.4 us -> 208 us  [the longest x3 166 us: share_sum(): moved = lax.all_to_all(part, 'tp', split_axis=0, concat_axis=0, tiled=True)]
where the time goes in v1:
time: 1040 us
  waiting for transfers between devices  512 us (49%)
  matrix products  182 us (18%)
  blocking collectives  135 us (13%)
  Pallas kernels  93.5 us (9%)
  local copies, waits for them, and re-layouts  46.2 us (4%)
  other arithmetic  32.4 us (3%)
  starting transfers between devices  24.4 us (2%)
  between operations  15.2 us (1%)
    all_to_all x3, waiting for transfers between devices, share_sum(): moved = lax.all_to_all(part, 'tp', split_axis=0, concat_axis=0, tiled=True)  166 us
    all_gather x2, waiting for transfers between devices, spread(): full = lax.all_gather(values, 'tp', axis=0, tiled=True)  89.2 us
    reduce_scatter x4, waiting for transfers between devices, owners(): lax.psum_scatter(value.astype(BF16), GROUP, scatter_dimension=axis, tiled...  88.4 us
    all_to_all x1, blocking collectives, share_sum(): moved = lax.all_to_all(part, 'tp', split_axis=0, concat_axis=0, tiled=True)  75.5 us
    pallas_call x1, Pallas kernels, delta_forward(): pl.pallas_call(functools.partial(forward_kernel, head_count, key_size, va...  59.3 us
    dot_general x4, matrix products, dot_nn(): lax.dot_general(left, right, (((1,), (0,)), ((), ())), preferred_element_...  54.6 us
    dot_general x4, matrix products, dot_tn(): lax.dot_general(left, right, (((0,), (0,)), ((), ())), preferred_element_...  49.2 us
    dot_general x4, matrix products, dot_nt(): lax.dot_general(left, right, (((1,), (1,)), ((), ())), preferred_element_...  46.6 us
  transfers between devices with their start and end apart: 17, of which 12 were waited for; matrix products, arithmetic and copies ran while one was open for 20% of the time, Pallas kernels for 9%

profile of v1, /device:TPU:0, one launch (start us, length us, event | category | flops | bytes accessed | tf_op | source)
XLA Modules:
  0.0 1039.8 jit_solution(9641286655238886532)
XLA Ops:
  41.8 41.6 %all-to-all-done = bf16[8,96,2048]{2,1,0:T(8,128)(2,1)S(1)} async-done(((bf16[8,96,2048]{2,1,0:T(8,128)(2,1)}), bf16[8,96,2048]{2,1,0:T(8,128)(2,1)S(1)}, u32[]{:S(2)}, u32[]{:S(2)}) %all-to-all-start) | async-done | bytes 3145760 | tf_op jit(solution)/shard_map/all_to_all | solution.py:539
  88.3 38.1 %all-gather.9.cloned.1.call-done = bf16[2048,3200]{1,0:T(8,128)(2,1)} async-done(((bf16[256,3200]{1,0:T(8,128)(2,1)}), bf16[2048,3200]{1,0:T(8,128)(2,1)}) %all-gather.9.cloned.1.call-update) | async-done | bytes 13107216 | tf_op jit(solution)/shard_map/all_gather | solution.py:566
  131.7 18.0 %fusion.22.proj.prior = f32[768,3200]{1,0:T(8,128)} fusion(bf16[2048,3200]{1,0:T(8,128)(2,1)} %all-gather.9.cloned.1.call-done, bf16[768,2048]{1,0:T(8,128)(2,1)} %get-tuple-element.227, f32[2048]{0:T(1024)S(1)} %get-tuple-element.174, f32[768]{0:T(1024)S(1)} %add_rsqrt_fusion), kind=kOutput, calls=%fused_computation.74 | convolution fusion | flops 10072621056 | bytes 26094592 | tf_op jit(solution)/shard_map/dot_general | solution.py:19
  149.7 59.3 %delta_forward.1 = (bf16[768,1024]{1,0:T(8,128)(2,1)S(1)}, f32[6,4,128,256]{3,2,1,0:T(8,128)S(1)}, bf16[6,4,128,128]{3,2,1,0:T(8,128)(2,1)S(1)}, f32[768,1024]{1,0:T(8,128)}, f32[768,1024]{1,0:T(8,128)}) custom-call(f32[768,3200]{1,0:T(8,128)} %fusion.22.proj.prior, f32[768,128]{1,0:T(8,128)S(1)} %pad.42.info_ref, f32[8,768]{1,0:T(8,128)S(1)} %broadcast_in_dim.65.segr, ...), custom_call_target="tpu_custom_call" | custom-call | tf_op jit(solution)/shard_map/delta_forward/pallas_call | solution.py:355
  224.0 71.3 %all-to-all-done.1 = bf16[4,192,2048]{2,1,0:T(8,128)(2,1)} async-done(((bf16[4,192,2048]{2,1,0:T(8,128)(2,1)}), bf16[4,192,2048]{2,1,0:T(8,128)(2,1)}, u32[]{:S(2)}, u32[]{:S(2)}) %all-to-all-start.1) | async-done | bytes 3145760 | tf_op jit(solution)/shard_map/all_to_all | solution.py:474
  306.0 40.5 %all_to_all.70 = bf16[8,96,2048]{2,1,0:T(8,128)(2,1)S(1)} all-to-all(bf16[8,96,2048]{2,1,0:T(8,128)(2,1)S(1)} %bitcast.95), channel_id=1, replica_groups=mesh['fsdp'=2,'ctx'=4,'tp'=4] {'fsdp','ctx'}, dimensions={0} | all-to-all | bytes 6291456 | tf_op jit(solution)/shard_map/all_to_all | solution.py:539
  350.6 13.6 %all-gather.15.cloned.1.call-done = bf16[768,2048]{1,0:T(8,128)(2,1)} async-done(((bf16[192,2048]{1,0:T(8,128)(2,1)}), bf16[768,2048]{1,0:T(8,128)(2,1)}) %all-gather.15.cloned.1.call-update) | async-done | bytes 3145744 | tf_op jit(solution)/shard_map/all_gather | solution.py:617
  364.2 15.8 %fusion.80 = f32[768,2816]{1,0:T(8,128)} fusion(bf16[768,2048]{1,0:T(8,128)(2,1)} %all-gather.15.cloned.1.call-done, bf16[2048,2816]{1,0:T(8,128)(2,1)} %all-gather.17.cloned.1.call-done), kind=kOutput, calls=%fused_computation.210 | convolution fusion | flops 8858370048 | bytes 23330816 | tf_op jit(solution)/shard_map/dot_general | solution.py:19
  380.0 29.0 %all-gather.13.cloned.1.call-done = bf16[2048,1408]{0,1:T(8,128)(2,1)} async-done(((bf16[256,1408]{0,1:T(8,128)(2,1)}), bf16[2048,1408]{0,1:T(8,128)(2,1)}) %all-gather.13.cloned.1.call-update) | async-done | bytes 5767184 | tf_op jit(solution)/shard_map/all_gather | solution.py:577
  409.0 12.5 %multiply_convert_fusion.2 = (bf16[768,1408]{1,0:T(8,128)(2,1)S(1)}, bf16[768,1408]{1,0:T(8,128)(2,1)S(1)}, bf16[768,1408]{1,0:T(8,128)(2,1)}) fusion(f32[768,2816]{1,0:T(8,128)} %fusion.80, bf16[768,2048]{1,0:T(8,128)(2,1)} %convolution_convert_fusion.6, bf16[2048,1408]{0,1:T(8,128)(2,1)} %all-gather.13.cloned.1.call-done), kind=kOutput, calls=%fused_computation.19 | convolution fusion | flops 4445405184 | bytes 24051712 | tf_op jit(solution)/shard_map/dot_general | solution.py:19
  421.5 13.6 %convolution_convert_fusion.13 = bf16[768,2048]{1,0:T(8,128)(2,1)S(1)} fusion(bf16[2048,2816]{1,0:T(8,128)(2,1)} %all-gather.17.cloned.1.call-done, bf16[768,1408]{1,0:T(8,128)(2,1)S(1)} %get-tuple-element.193, bf16[768,1408]{1,0:T(8,128)(2,1)S(1)} %get-tuple-element.192), kind=kOutput, calls=%fused_computation.32 | convolution fusion | flops 8868593664 | bytes 19005440 | tf_op jit(solution)/shard_map/dot_general | solution.py:23
  435.1 75.5 %all_to_all.71 = bf16[4,192,2048]{2,1,0:T(8,128)(2,1)S(1)} all-to-all(bf16[4,192,2048]{2,1,0:T(8,128)(2,1)S(1)} %bitcast.101), channel_id=1, replica_groups=mesh['fsdp'=2,'ctx'=4,'tp'=4] {'tp'}, dimensions={0} | all-to-all | bytes 6291456 | tf_op jit(solution)/shard_map/all_to_all | solution.py:474
  516.2 9.2 convolution_convert_fusion.2
  534.4 43.5 %all-gather.19.cloned.1.call-done = bf16[768,2048]{1,0:T(8,128)(2,1)} async-done(((bf16[192,2048]{1,0:T(8,128)(2,1)}), bf16[768,2048]{1,0:T(8,128)(2,1)}) %all-gather.19.cloned.1.call-update) | async-done | bytes 3145744 | tf_op jit(solution)/shard_map/all_gather | solution.py:644
  585.8 15.4 %convolution_convert_fusion.1 = bf16[2048,2816]{1,0:T(8,128)(2,1)} fusion(bf16[768,2048]{1,0:T(8,128)(2,1)} %all-gather.15.cloned.1.call-done, bf16[768,1408]{1,0:T(8,128)(2,1)} %copy-done.39, bf16[768,1408]{1,0:T(8,128)(2,1)} %copy-done.38), kind=kOutput, calls=%fused_computation.1 | convolution fusion | flops 8872787968 | bytes 19005440 | tf_op jit(solution)/shard_map/dot_general | solution.py:27
  615.5 34.2 %delta_backward.1 = (bf16[768,3200]{1,0:T(8,128)(2,1)}, f32[32,2048]{1,0:T(8,128)S(1)}, f32[8,1024]{1,0:T(8,128)S(1)}, f32[16,128]{1,0:T(8,128)S(1)}) custom-call(f32[768,3200]{1,0:T(8,128)} %fusion.22.proj.prior, f32[768,3200]{1,0:T(8,128)} %fusion.22.proj.prior, f32[768,128]{1,0:T(8,128)S(1)} %pad.42.info_ref, f32[8,768]{1,0:T(8,128)S(1)} %copy-done.9, ...), custom_call_target="tpu_custom_call" | custom-call | tf_op jit(solution)/shard_map/delta_backward/pallas_call | solution.py:400
  651.6 25.5 %all-to-all-done.4 = bf16[4,192,2048]{2,1,0:T(8,128)(2,1)} async-done(((bf16[4,192,2048]{2,1,0:T(8,128)(2,1)}), bf16[4,192,2048]{2,1,0:T(8,128)(2,1)}, u32[]{:S(2)}, u32[]{:S(2)}) %all-to-all-start.4) | async-done | bytes 3145760 | tf_op jit(solution)/shard_map/all_to_all | solution.py:474
  684.9 16.4 %convolution_convert_fusion.11 = bf16[768,2048]{1,0:T(8,128)(2,1)} fusion(bf16[768,3200]{1,0:T(8,128)(2,1)} %get-tuple-element.62, bf16[2048,3200]{1,0:T(8,128)(2,1)} %all-gather.9.cloned.1.call-done), kind=kOutput, calls=%fused_computation.30 | convolution fusion | flops 10067902464 | bytes 21168128 | tf_op jit(solution)/shard_map/dot_general | solution.py:23
  709.1 69.1 %all-to-all-done.6 = bf16[4,192,2048]{2,1,0:T(8,128)(2,1)} async-done(((bf16[4,192,2048]{2,1,0:T(8,128)(2,1)}), bf16[4,192,2048]{2,1,0:T(8,128)(2,1)}, u32[]{:S(2)}, u32[]{:S(2)}) %all-to-all-start.6) | async-done | bytes 3145760 | tf_op jit(solution)/shard_map/all_to_all | solution.py:474
  784.7 18.6 %all_to_all.72 = bf16[8,32,2048]{2,1,0:T(8,128)(2,1)S(1)} all-to-all(bf16[8,32,2048]{2,1,0:T(8,128)(2,1)S(1)} %fusion.20), channel_id=1, replica_groups=mesh['fsdp'=2,'ctx'=4,'tp'=4] {'fsdp','ctx'}, dimensions={0} | all-to-all | bytes 2097152 | tf_op jit(solution)/shard_map/all_to_all | solution.py:547
  804.6 16.8 %convolution_convert_fusion = bf16[2048,3200]{1,0:T(8,128)(2,1)} fusion(bf16[768,3200]{1,0:T(8,128)(2,1)} %get-tuple-element.62, bf16[768,2048]{1,0:T(8,128)(2,1)S(1)} %copy-done.20, f32[2048]{0:T(1024)S(1)} %copy-done.25, f32[768]{0:T(1024)S(1)} %copy-done.34), kind=kOutput, calls=%fused_computation | convolution fusion | flops 10079174656 | bytes 21179392 | tf_op jit(solution)/shard_map/dot_general | solution.py:27
  833.2 29.5 %all-gather.21.cloned.1.call-done = bf16[800,2048]{1,0:T(8,128)(2,1)} async-done(((bf16[200,2048]{1,0:T(8,128)(2,1)}), bf16[800,2048]{1,0:T(8,128)(2,1)}) %all-gather.21.cloned.1.call-update) | async-done | bytes 3276816 | tf_op jit(solution)/shard_map/all_gather | solution.py:550
  869.6 59.7 %all-gather.23.cloned.1.call-done = bf16[800,2048]{1,0:T(8,128)(2,1)} async-done(((bf16[200,2048]{1,0:T(8,128)(2,1)}), bf16[800,2048]{1,0:T(8,128)(2,1)}) %all-gather.23.cloned.1.call-update) | async-done | bytes 3276816 | tf_op jit(solution)/shard_map/all_gather | solution.py:550
  938.1 88.4 %reduce-scatter.5.cloned.1.call-done = bf16[256,3200]{1,0:T(8,128)(2,1)} async-done(((bf16[2048,3200]{1,0:T(8,128)(2,1)}), bf16[256,3200]{1,0:T(8,128)(2,1)}) %reduce-scatter.5.cloned.1.call-update) | async-done | bytes 1638416 | tf_op jit(solution)/shard_map/reduce_scatter | solution.py:657
  (280 shorter events, 169.5 us)
Async XLA Ops:
  7.2 119.1 %all-gather.9.cloned.1.call-start = ((), (), s32[]{:S(2)}) async-start(), calls=%async_computation.12 | async-start | bytes 14745600 | tf_op jit(solution)/shard_map/all_gather | solution.py:566
  17.4 194.2 %all-gather.11.cloned.1.call-start = ((), (), s32[]{:S(2)}) async-start(), calls=%async_computation.13 | async-start | bytes 4718592 | tf_op jit(solution)/shard_map/all_gather | solution.py:573
  18.2 332.5 %all-gather.17.cloned.1.call-start = ((), (), s32[]{:S(2)}) async-start(), calls=%async_computation.16 | async-start | bytes 12976128 | tf_op jit(solution)/shard_map/all_gather | solution.py:574
  25.8 57.6 %all-to-all-start = ((bf16[8,96,2048]{2,1,0:T(8,128)(2,1)}), bf16[8,96,2048]{2,1,0:T(8,128)(2,1)S(1)}, u32[]{:S(2)}, u32[]{:S(2)}) async-start(bf16[8,96,2048]{2,1,0:T(8,128)(2,1)} %bitcast.94), calls=%async_computation | async-start | bytes 6291456 | tf_op jit(solution)/shard_map/all_to_all | solution.py:539
  88.3 43.4 %copy-start.33 = (f32[768]{0:T(1024)}, f32[768]{0:T(1024)S(1)}, u32[]{:S(2)}) copy-start(f32[768]{0:T(1024)S(1)} %add_rsqrt_fusion) | copy-start | bytes 9220
  219.3 76.0 %all-to-all-start.1 = ((bf16[4,192,2048]{2,1,0:T(8,128)(2,1)}), bf16[4,192,2048]{2,1,0:T(8,128)(2,1)}, u32[]{:S(2)}, u32[]{:S(2)}) async-start(bf16[4,192,2048]{2,1,0:T(8,128)(2,1)} %bitcast.99), calls=%async_computation.1 | async-start | bytes 6291456 | tf_op jit(solution)/shard_map/all_to_all | solution.py:474
  224.0 140.3 %all-gather.15.cloned.1.call-start = ((), (), s32[]{:S(2)}) async-start(), calls=%async_computation.15 | async-start | bytes 3932160 | tf_op jit(solution)/shard_map/all_gather | solution.py:617
  302.5 106.5 %all-gather.13.cloned.1.call-start = ((), (), s32[]{:S(2)}) async-start(), calls=%async_computation.14 | async-start | bytes 6488064 | tf_op jit(solution)/shard_map/all_gather | solution.py:577
  303.1 274.9 %all-gather.19.cloned.1.call-start = ((), (), s32[]{:S(2)}) async-start(), calls=%async_computation.17 | async-start | bytes 3932160 | tf_op jit(solution)/shard_map/all_gather | solution.py:644
  306.0 40.5 %copy-start.35 = (s32[768]{0:T(1024)S(1)}, s32[768]{0:T(1024)}, u32[]{:S(2)}) copy-start(s32[768]{0:T(1024)} %add_add_fusion) | copy-start | bytes 9220
  516.2 306.0 %reduce-scatter.11.cloned.1.call-start = ((), (), s32[]{:S(2)}) async-start(), calls=%async_computation.23 | async-start | bytes 6488064 | tf_op jit(solution)/shard_map/reduce_scatter | solution.py:657
  525.5 302.2 %reduce-scatter.7.cloned.1.call-start = ((), (), s32[]{:S(2)}) async-start(), calls=%async_computation.21 | async-start | bytes 4718592 | tf_op jit(solution)/shard_map/reduce_scatter | solution.py:657
  585.8 244.3 %reduce-scatter.9.cloned.1.call-start = ((), (), s32[]{:S(2)}) async-start(), calls=%async_computation.22 | async-start | bytes 12976128 | tf_op jit(solution)/shard_map/reduce_scatter | solution.py:657
  601.2 75.8 %all-to-all-start.4 = ((bf16[4,192,2048]{2,1,0:T(8,128)(2,1)}), bf16[4,192,2048]{2,1,0:T(8,128)(2,1)}, u32[]{:S(2)}, u32[]{:S(2)}) async-start(bf16[4,192,2048]{2,1,0:T(8,128)(2,1)} %bitcast.98), calls=%async_computation.4 | async-start | bytes 6291456 | tf_op jit(solution)/shard_map/all_to_all | solution.py:474
  651.6 28.2 %copy-start.17 = (f32[192,2048]{1,0:T(8,128)S(1)}, f32[192,2048]{1,0:T(8,128)}, u32[]{:S(2)}) copy-start(f32[192,2048]{1,0:T(8,128)} %copy-done.15) | copy-start | bytes 4718596
  681.1 21.0 %all-to-all-start.5 = ((bf16[8,24,2048]{2,1,0:T(8,128)(2,1)}), bf16[8,24,2048]{2,1,0:T(8,128)(2,1)S(1)}, u32[]{:S(2)}, u32[]{:S(2)}) async-start(bf16[8,24,2048]{2,1,0:T(8,128)(2,1)} %bitcast.23), calls=%async_computation.5 | async-start | bytes 1572864 | tf_op jit(solution)/shard_map/all_to_all | solution.py:547
  702.2 76.1 %all-to-all-start.6 = ((bf16[4,192,2048]{2,1,0:T(8,128)(2,1)}), bf16[4,192,2048]{2,1,0:T(8,128)(2,1)}, u32[]{:S(2)}, u32[]{:S(2)}) async-start(bf16[4,192,2048]{2,1,0:T(8,128)(2,1)} %bitcast.26), calls=%async_computation.6 | async-start | bytes 6291456 | tf_op jit(solution)/shard_map/all_to_all | solution.py:474
  706.9 155.8 %all-gather.21.cloned.1.call-start = ((), (), s32[]{:S(2)}) async-start(), calls=%async_computation.18 | async-start | bytes 4096000 | tf_op jit(solution)/shard_map/all_gather | solution.py:550
  708.0 72.9 %copy-start.25 = (f32[2048]{0:T(1024)S(1)}, f32[2048]{0:T(1024)}, u32[]{:S(2)}) copy-start(f32[2048]{0:T(1024)} %copy-done.24) | copy-start | bytes 24580
  708.0 221.2 %all-gather.23.cloned.1.call-start = ((), (), s32[]{:S(2)}) async-start(), calls=%async_computation.19 | async-start | bytes 4096000 | tf_op jit(solution)/shard_map/all_gather | solution.py:550
  709.1 73.6 %copy-start.19 = (f32[192,2048]{1,0:T(8,128)S(1)}, f32[192,2048]{1,0:T(8,128)}, u32[]{:S(2)}) copy-start(f32[192,2048]{1,0:T(8,128)} %get-tuple-element.189) | copy-start | bytes 4718596
  784.7 19.9 %copy-start.20 = (bf16[768,2048]{1,0:T(8,128)(2,1)S(1)}, bf16[768,2048]{1,0:T(8,128)(2,1)}, u32[]{:S(2)}) copy-start(bf16[768,2048]{1,0:T(8,128)(2,1)} %get-tuple-element.227) | copy-start | bytes 9437188
  784.7 19.9 %copy-start.34 = (f32[768]{0:T(1024)S(1)}, f32[768]{0:T(1024)}, u32[]{:S(2)}) copy-start(f32[768]{0:T(1024)} %copy-done.33) | copy-start | bytes 9220
  804.5 222.0 %reduce-scatter.5.cloned.1.call-start = ((), (), s32[]{:S(2)}) async-start(), calls=%async_computation.20 | async-start | bytes 14745600 | tf_op jit(solution)/shard_map/reduce_scatter | solution.py:657
  (33 other events, 178.4 us)
Sparse Core Ops, SparseCore 0:
  17.5 108.7 all-gather.8
  128.2 37.5 all-gather.10
  168.3 67.8 all-gather.16
  302.6 61.5 all-gather.14
  365.9 42.9 all-gather.12
  516.3 61.6 all-gather.18
  581.4 57.6 reduce-scatter.10
  642.9 56.6 reduce-scatter.6
  703.1 88.5 reduce-scatter.8
  793.7 69.0 all-gather.20
  864.9 64.2 all-gather.22
  932.7 93.7 reduce-scatter.4

commit v2 on v1

--- a/solution.py
+++ b/solution.py
@@ -56,21 +56,41 @@
     return jnp.maximum(value, 0.0) + jnp.log1p(jnp.exp(-jnp.abs(value)))
 
 
-def inverse_lower(lower_mat, row_id, col_id):
-    size = lower_mat.shape[0]
+def low_dot(left, right):
+    return dot_nn(left.astype(BF16), right.astype(BF16))
+
+
+def inverses_lower(lower_mats, row_id, col_id):
+    size = row_id.shape[0]
 
     def level(width):
         same = row_id // (2 * width) == col_id // (2 * width)
         return same & ((row_id // width) % 2 == 1) & ((col_id // width) % 2 == 0)
 
     unit = jnp.where(row_id == col_id, 1.0, 0.0)
-    result = unit - jnp.where(level(1), lower_mat, 0.0)
+    mask = level(1)
+    results = [unit - jnp.where(mask, mat, 0.0) for mat in lower_mats]
     width = 2
     while width < size:
-        part = jnp.where(level(width), lower_mat, 0.0)
-        result = result - dot_fine(dot_fine(result, part), result)
+        mask = level(width)
+        parts = [low_dot(r, jnp.where(mask, mat, 0.0)) for r, mat in zip(results, lower_mats)]
+        results = [r - low_dot(p, r) for p, r in zip(parts, results)]
         width *= 2
-    return result
+    rests = [unit - r - dot_fine(mat, r) for r, mat in zip(results, lower_mats)]
+    return [r + low_dot(r, rest) for r, rest in zip(results, rests)]
+
+
+def in_turn(bodies):
+    asked = [next(body) for body in bodies]
+    while asked:
+        made = asked[0][0]([item[1] for item in asked]) if asked[0] else [None] * len(asked)
+        following = []
+        for body, value in zip(bodies, made):
+            try:
+                following.append(body.send(value))
+            except StopIteration:
+                pass
+        asked = following
 
 
 def chunk_basics(gates, par, info, seg_row, row_id, col_id, lane_id, head_count):
@@ -126,7 +146,7 @@
     strict = row_id > col_id
     key_at = head_count * key_size
     value_at = 2 * key_at
-    for head in range(head_count):
+    def one_head(head):
         ks = key_size
         vs = value_size
         act_q = activations(ext, taps, masks, head * ks, (head + 1) * ks, rows)
@@ -137,6 +157,7 @@
         values = act_v * sigmoid(act_v)
         query = cq * (lax.rsqrt(jnp.sum(cq * cq, axis=1, keepdims=True) + unit_eps) * ks ** -0.5)
         key = ck * lax.rsqrt(jnp.sum(ck * ck, axis=1, keepdims=True) + unit_eps)
+        yield
         qb = query.astype(BF16)
         kb = key.astype(BF16)
         cum = both[:, head : head + 1]
@@ -145,7 +166,8 @@
         beta_row = turned[head_count + head : head_count + head + 1, :]
         decays = jnp.where(inner, jnp.exp(jnp.minimum(cum - cum_row, 0.0)), 0.0)
         lower_mat = jnp.where(strict, decays * dot_nt(kb, kb) * beta_row, 0.0)
-        inverse = inverse_lower(lower_mat, row_id, col_id)
+        inverse = yield (lambda mats: inverses_lower(mats, row_id, col_id)), lower_mat
+        yield
         carried = jnp.exp(cum) * carried_mask
         last = cum[rows - 1 : rows, :]
         tail = jnp.exp(last - cum) * tail_mask
@@ -158,15 +180,19 @@
         pseudo = dot_nn(ib, target.astype(BF16))
         inverse_out[0, head] = ib
         pseudo_out[:, head * vs : (head + 1) * vs] = pseudo
+        yield
         weighted = beta * pseudo
         mix = decays * dot_nt(qb, kb)
         output = carried * dot_nn(qb, sb) + dot_nn(mix.astype(BF16), weighted.astype(BF16))
         output_out[:, head * vs : (head + 1) * vs] = output
         state[head] = keep * before + dot_tn(kb, (tail * weighted).astype(BF16))
+        yield
         gate = proj[:, gate_at + head * vs : gate_at + (head + 1) * vs]
         scale = lax.rsqrt(jnp.mean(output * output, axis=1, keepdims=True) + square_eps)
         normed = output * scale * gain_ref[0:1, :] * (gate * sigmoid(gate)) * valid
         normed_out[:, head * vs : (head + 1) * vs] = normed.astype(BF16)
+
+    in_turn([one_head(head) for head in range(head_count)])
     ext[0:PAD, :] = ext[rows : rows + PAD, :]
 
 
@@ -215,8 +241,7 @@
     vs = value_size
     key_at = head_count * ks
     value_at = 2 * key_at
-    dcum = jnp.zeros((rows, LANES), F32)
-    dturned = jnp.zeros((LANES, rows), F32)
+    sums = {}
 
     def fold(value):
         return jnp.sum(value.reshape(rows // PAD, PAD, value.shape[1]), axis=0)
@@ -231,7 +256,7 @@
             conv_out[(3 - d) * PAD : (4 - d) * PAD, start:stop] += fold(masks[d - 1] * da * shifted)
         grad_out[:, start:stop] = back.astype(BF16)
 
-    for head in range(head_count):
+    def one_head(head):
         act_q = activations(ext, taps, masks, head * ks, (head + 1) * ks, rows)
         act_k = activations(ext, taps, masks, key_at + head * ks, key_at + (head + 1) * ks, rows)
         act_v = activations(ext, taps, masks, value_at + head * vs, value_at + (head + 1) * vs, rows)
@@ -242,6 +267,7 @@
         unit_q = cq * rate_q
         query = unit_q * ks ** -0.5
         key = ck * rate_k
+        yield
         qb = query.astype(BF16)
         kb = key.astype(BF16)
         cum = both[:, head : head + 1]
@@ -252,6 +278,7 @@
         carried = jnp.exp(cum) * carried_mask
         tail = jnp.exp(cum[rows - 1 : rows, :] - cum) * tail_mask
         keep = carried[rows - 1 : rows, :]
+        yield
         before = state_in[0, head]
         sb = before.astype(BF16)
         ib = inverse_in[0, head]
@@ -269,20 +296,24 @@
         dgate = given * unit_o * gain * (sig_g * (1.0 + gate * (1.0 - sig_g)))
         gain_out[:, head * vs : (head + 1) * vs] += fold(given * unit_o * silu_g)
         grad_out[:, gate_at + head * vs : gate_at + (head + 1) * vs] = dgate.astype(BF16)
+        yield
         dob = doutput.astype(BF16)
         weighted = beta * pseudo
         wb = weighted.astype(BF16)
         gram = dot_nt(kb, kb)
         cross = dot_nt(qb, kb)
         mix = decays * cross
+        yield
         after = dstate[head]
         ab = after.astype(BF16)
         from_state = dot_nn(kb, ab)
         dweighted = dot_tn(mix.astype(BF16), dob) + tail * from_state
         dbeta = jnp.sum(dweighted * pseudo, axis=1, keepdims=True)
+        yield
         dtarget = dot_tn(ib, (beta * dweighted).astype(BF16))
         dtb = dtarget.astype(BF16)
         read = dot_nn(kb, sb)
+        yield
         dcarried = jnp.sum(doutput * dot_nn(qb, sb), axis=1, keepdims=True) - jnp.sum(
             dtarget * read, axis=1, keepdims=True
         )
@@ -291,12 +322,14 @@
         cdo = (carried * doutput).astype(BF16)
         cdt = (carried * dtarget).astype(BF16)
         dstate[head] = keep * after + dot_tn(qb, cdo) - dot_tn(kb, cdt)
+        yield
         dmix = dot_nt(dob, wb)
         dcross = (dmix * decays).astype(BF16)
         dlower = jnp.where(strict, -dot_nt(dtb, pseudo.astype(BF16)), 0.0) * decays
         dgram = (dlower * beta_row).astype(BF16)
         plain = dlower * gram
         inner_grad = dmix * mix + plain * beta_row
+        yield
         dquery = dot_nt(cdo, sb) + dot_nn(dcross, kb)
         dkey = (
             dot_tn(dcross, qb)
@@ -305,6 +338,7 @@
             + dot_nt((tail * weighted).astype(BF16), ab)
             - dot_nt(cdt, sb)
         )
+        yield
         dlast = jnp.sum(dtail * tail, axis=0, keepdims=True) + dkeep * keep
         dcum_col = (
             jnp.sum(inner_grad, axis=1, keepdims=True)
@@ -312,16 +346,18 @@
             - dtail * tail
             + jnp.where(last_row, dlast, 0.0)
         )
-        dcum = jnp.where(lane_id == head, dcum_col, dcum)
-        dcum = jnp.where(lane_id == head_count + head, dbeta, dcum)
-        dturned = jnp.where(row_of == head, -jnp.sum(inner_grad, axis=0, keepdims=True), dturned)
-        dturned = jnp.where(
-            row_of == head_count + head, jnp.sum(plain, axis=0, keepdims=True), dturned
+        sums[head] = (
+            dcum_col,
+            dbeta,
+            -jnp.sum(inner_grad, axis=0, keepdims=True),
+            jnp.sum(plain, axis=0, keepdims=True),
         )
+        yield
         dq_scaled = dquery * ks ** -0.5
         dcq = (dq_scaled - unit_q * jnp.sum(unit_q * dq_scaled, axis=1, keepdims=True)) * rate_q
         dck = (dkey - key * jnp.sum(key * dkey, axis=1, keepdims=True)) * rate_k
         conv_back(dcq * (sig_q * (1.0 + act_q * (1.0 - sig_q))), head * ks, (head + 1) * ks)
+        yield
         conv_back(
             dck * (sig_k * (1.0 + act_k * (1.0 - sig_k))), key_at + head * ks, key_at + (head + 1) * ks
         )
@@ -330,6 +366,16 @@
             value_at + head * vs,
             value_at + (head + 1) * vs,
         )
+
+    for head in range(head_count):
+        in_turn([one_head(head)])
+    dcum = jnp.zeros((rows, LANES), F32)
+    dturned = jnp.zeros((LANES, rows), F32)
+    for head, (dcum_col, dbeta, dcum_row, dbeta_row) in sums.items():
+        dcum = jnp.where(lane_id == head, dcum_col, dcum)
+        dcum = jnp.where(lane_id == head_count + head, dbeta, dcum)
+        dturned = jnp.where(row_of == head, dcum_row, dturned)
+        dturned = jnp.where(row_of == head_count + head, dbeta_row, dturned)
     dboth = dcum + jnp.transpose(dturned)
     upper = jnp.where(row_id <= col_id, 1.0, 0.0).astype(BF16)
     dlog = sum_by(upper, jnp.where(lane_id < head_count, dboth, 0.0))
@@ -436,6 +482,72 @@
     )(proj, proj, info, seg_rows, par, taps, gain, states, inverses, pseudos, outputs, dnormed)
 
 
+def middle_kernel(place, own, after, before, x_ref, gain, hidden_out, normed_out):
+    mixer = own[...].astype(F32) + after[...].astype(F32) + before[...].astype(F32)
+    hidden = mixer + x_ref[...].astype(F32)
+    rate = lax.rsqrt(jnp.mean(hidden * hidden, axis=1, keepdims=True) + square_eps)
+    hidden_out[...] = hidden
+    normed_out[...] = (hidden * rate * gain[0:1, :]).astype(BF16)
+
+
+def norm_back(grad, value, gain):
+    rate = lax.rsqrt(jnp.mean(value * value, axis=1, keepdims=True) + square_eps)
+    scaled = grad * gain
+    inner = jnp.mean(value * scaled, axis=1, keepdims=True)
+    return rate * scaled - rate * rate * rate * value * inner, grad * value * rate
+
+
+def rows_summed(value):
+    return jnp.sum(value.reshape(value.shape[0] // PAD, PAD, value.shape[1]), axis=0)
+
+
+def middle_back_kernel(place, moved, hidden, dy_ref, gain, grad_out, low_out, gain_out):
+    @pl.when(pl.program_id(0) == 0)
+    def start():
+        gain_out[...] = jnp.zeros_like(gain_out)
+
+    back, part = norm_back(moved[...].astype(F32), hidden[...], gain[0:1, :])
+    grad = dy_ref[...].astype(F32) + back
+    grad_out[...] = grad
+    low_out[...] = grad.astype(BF16)
+    gain_out[...] += rows_summed(part)
+
+
+def first_back_kernel(place, moved, after, x_ref, gain, grad_out, gain_out):
+    @pl.when(pl.program_id(0) == 0)
+    def start():
+        gain_out[...] = jnp.zeros_like(gain_out)
+
+    back, part = norm_back(moved[...].astype(F32), x_ref[...].astype(F32), gain[0:1, :])
+    grad_out[...] = (after[...] + back).astype(BF16)
+    gain_out[...] += rows_summed(part)
+
+
+def row_parts(kernel, place, arrays, outs, rows):
+    part = 48 if rows % 48 == 0 else rows
+    steps = rows // part
+
+    def spec(kind, shape):
+        if kind == "own":
+            return pl.BlockSpec((part, shape[1]), lambda i, p: (i, 0))
+        if kind == "all":
+            return pl.BlockSpec((part, shape[1]), lambda i, p: (p[0] * steps + i, 0))
+        return pl.BlockSpec(shape, lambda i, p: (0, 0))
+
+    return pl.pallas_call(
+        kernel,
+        grid_spec=pltpu.PrefetchScalarGridSpec(
+            num_scalar_prefetch=1,
+            grid=(steps,),
+            in_specs=[spec(kind, value.shape) for kind, value in arrays],
+            out_specs=[spec(kind, value.shape) for kind, value in outs],
+        ),
+        out_shape=[value for kind, value in outs],
+        compiler_params=pltpu.CompilerParams(vmem_limit_bytes=40 * 1024 * 1024),
+        name=kernel.__name__,
+    )(place, *[value for kind, value in arrays])
+
+
 def place_arrays(length_row, total):
     places = jnp.arange(total, dtype=jnp.int32)
     ids = jnp.arange(length_row.shape[0])
@@ -469,10 +581,107 @@
     return jnp.stack([high, low], axis=-2)
 
 
-def share_sum(part):
+SC_SUM = "bn"
+SC_COPY = ""
+
+
+def deal(part, name=""):
+    if name and name in SC_SUM:
+        return lax.psum_scatter(part, "tp", scatter_dimension=0, tiled=True)
+    return lax.all_to_all(part, "tp", split_axis=0, concat_axis=0, tiled=True)
+
+
+def add_dealt(moved, name=""):
+    if name and name in SC_SUM:
+        return moved.astype(F32)
     count = lax.axis_size("tp")
-    moved = lax.all_to_all(part, "tp", split_axis=0, concat_axis=0, tiled=True)
-    return jnp.sum(moved.reshape(count, -1, part.shape[1]).astype(F32), axis=0)
+    return jnp.sum(moved.reshape(count, -1, moved.shape[1]).astype(F32), axis=0)
+
+
+def copy_rows(own, name=""):
+    if name and name in SC_COPY:
+        return lax.all_gather(own, "tp", axis=0, tiled=True)
+    return deal(jnp.concatenate([own] * lax.axis_size("tp"), axis=0))
+
+
+def relay_send(value, route):
+    return lax.ppermute(value, "tp", route)
+
+
+def relay_first(own):
+    return relay_send(own, [(0, 1), (1, 2), (2, 3)]), relay_send(own, [(1, 0), (2, 1), (3, 2)])
+
+
+def relay_second(before, after):
+    place = lax.axis_index("tp")
+    before_2 = relay_send(before, [(1, 2), (2, 3)])
+    after_2 = relay_send(after, [(2, 1), (1, 0)])
+    far = relay_send(jnp.where(place == 1, before, after), [(1, 3), (2, 0)])
+    return before_2, after_2, far
+
+
+def relayed_blocks(own):
+    before, after = relay_first(own)
+    return (own, before, after, *relay_second(before, after))
+
+
+def sum_rows_relayed(part, rows, along):
+    place = lax.axis_index("tp")
+
+    def block(index):
+        return lax.dynamic_slice(part, (jnp.clip(index, 0, 3) * rows, 0), (rows, part.shape[1]))
+
+    from_after = relay_send(block(place - 2), [(2, 1), (3, 2)])
+    from_before = relay_send(block(place + 2), [(1, 2), (0, 1)])
+    far = relay_send(block(jnp.where(place == 3, 0, 3)), [(3, 1), (0, 2)])
+    from_after, from_before, far, along = together((from_after, from_before, far, along))
+    far = far.astype(F32)
+    to_before = (
+        block(place - 1).astype(F32) + from_after.astype(F32) + jnp.where(place == 1, far, 0.0)
+    )
+    to_after = (
+        block(place + 1).astype(F32) + from_before.astype(F32) + jnp.where(place == 2, far, 0.0)
+    )
+    return (
+        relay_send(to_before.astype(BF16), [(1, 0), (2, 1), (3, 2)]),
+        relay_send(to_after.astype(BF16), [(0, 1), (1, 2), (2, 3)]),
+        along,
+    )
+
+
+def copy_rows_ordered(own):
+    place = lax.axis_index("tp")
+    own, before, after, before_2, after_2, far = relayed_blocks(own)
+    parts = []
+    for source in range(4):
+        part = own
+        for apart, block in ((-1, before), (1, after), (-2, before_2), (2, after_2)):
+            if 0 <= source - apart < 4:
+                part = jnp.where(source - place == apart, block, part)
+        if source in (0, 3):
+            part = jnp.where(jnp.abs(source - place) == 3, far, part)
+        parts.append(part)
+    return jnp.concatenate(parts, axis=0)
+
+
+def relayed_block(place, source):
+    apart = source - place
+    near = jnp.where(apart == 0, 0, jnp.where(apart == -1, 1, 2))
+    return jnp.where(jnp.abs(apart) == 3, 5, jnp.where(apart == -2, 3, jnp.where(apart == 2, 4, near)))
+
+
+RELAYED = 6
+
+
+def copy_rows_turned(own):
+    count = lax.axis_size("tp")
+    blocks = [own]
+    for turn in range(1, count):
+        blocks.append(lax.ppermute(own, "tp", [(i, (i + turn) % count) for i in range(count)]))
+    return jnp.concatenate(blocks, axis=0)
+
+
+together = lax.optimization_barrier
 
 
 def per_device(
@@ -488,7 +697,7 @@
     packs = lengths.shape[1]
     all_rows = order.shape[1]
     pack_rows = all_rows // packs
-    assert micros * packs == groups and pack_rows == tp_count * rows
+    assert micros * packs == groups and pack_rows == tp_count * rows and tp_count == 4
     share = rows // groups
     heads = decay_log.shape[0]
     spans = query_conv.shape[0]
@@ -510,14 +719,18 @@
     held = rows + PAD
     pack_id = jnp.arange(groups, dtype=jnp.int32).reshape(micros, packs, 1, 1)
     tp_id = jnp.arange(tp_count, dtype=jnp.int32).reshape(tp_count, 1)
-    back_slot = (tp_id * held + pack_id * share + rank).reshape(micros, 1, all_rows)
+    back_slot = (relayed_block(tp_place, tp_id) * held + pack_id * share + rank).reshape(micros, 1, all_rows)
     local = group * rows + jnp.arange(rows, dtype=jnp.int32)
     hit = order[:, None, :] == local[None, :, None]
     send_at = jnp.sum(jnp.where(hit, send_slot, 0), axis=2)
     back_at = jnp.sum(jnp.where(hit, back_slot, 0), axis=2).reshape(micros * rows)
     row_ids = jnp.arange(rows, dtype=jnp.int32)
+    send_row = send_at // (share * tp_count) * share + send_at % share
+    send_ids = jnp.arange(packs * share, dtype=jnp.int32)[None, :, None]
+    sent_here = send_at // share % tp_count == tp_place
+    part_pick = ((send_ids == send_row[:, None, :]) & sent_here[:, None, :]).astype(BF16)
     send_pick = (row_ids[None, :, None] == send_at[:, None, :]).astype(BF16)
-    back_ids = jnp.arange(tp_count * held, dtype=jnp.int32)
+    back_ids = jnp.arange(RELAYED * held, dtype=jnp.int32)
     back_pick = (back_at[:, None] == back_ids[None, :]).astype(BF16)
 
     pack_order = lax.dynamic_slice(order, (my_micro, my_pack * pack_rows), (1, pack_rows))
@@ -530,72 +743,79 @@
     arrive_at = source * (tp_count * share) + tp_id * share + source_rank
     pack_ids = jnp.arange(pack_rows, dtype=jnp.int32)
     arrive_pick = (arrive_at.reshape(pack_rows, 1) == pack_ids[None, :]).astype(BF16)
+    part_at = (tp_place - tp_id) % tp_count * rows + source * share + source_rank
+    place_pick = (part_at.reshape(pack_rows, 1) == pack_ids[None, :]).astype(BF16)
     return_at = lax.dynamic_slice(source * share + source_rank, (tp_place, 0), (1, rows))
     return_pick = (row_ids[:, None] == return_at).astype(BF16)
 
-    def to_pack(values):
-        sent = jnp.einsum("msi,mid->msd", send_pick, values, preferred_element_type=F32)
-        sent = sent.astype(BF16).reshape(micros * rows, width)
-        moved = lax.all_to_all(sent, GROUP, split_axis=0, concat_axis=0, tiled=True)
-        return jnp.dot(arrive_pick, moved, preferred_element_type=F32).astype(BF16)
-
-    def to_given(values, extra):
-        sent = jnp.dot(return_pick, values.astype(BF16), preferred_element_type=F32).astype(BF16)
-        sent = sent.reshape(groups, share, width)
-        if extra is not None:
-            sent = jnp.concatenate([sent, extra], axis=1)
+    def picked(pick, values):
+        return jnp.einsum("msi,mid->msd", pick, values, preferred_element_type=F32).astype(BF16)
+
+    def exchange(sent):
         return lax.all_to_all(sent, GROUP, split_axis=0, concat_axis=0, tiled=True)
 
-    def spread(values):
-        full = lax.all_gather(values, "tp", axis=0, tiled=True)
-        picked = jnp.dot(back_pick, full, preferred_element_type=F32).astype(BF16)
-        return picked.reshape(micros, rows, width), full
+    def to_sources(values):
+        sent = jnp.dot(return_pick, values, preferred_element_type=F32).astype(BF16)
+        return sent.reshape(groups, share, width)
+
+    def to_given(blocks):
+        full = jnp.concatenate(blocks, axis=0)
+        values = jnp.dot(back_pick, full, preferred_element_type=F32).astype(BF16)
+        return values.reshape(micros, rows, width), full
 
     small = jnp.concatenate(
         [
-            gain_in[None],
-            gain_mid[None],
-            query_conv.reshape(-1, own),
-            key_conv.reshape(-1, own),
-            value_conv.reshape(-1, own),
-            jnp.pad(gain_head, (0, own - gain_head.shape[0]))[None],
+            gain_in,
+            gain_mid,
+            query_conv.reshape(-1),
+            key_conv.reshape(-1),
+            value_conv.reshape(-1),
+            gain_head,
         ],
         axis=0,
     )
-    small = jnp.pad(small, ((0, LANES - 2 * heads - small.shape[0]), (0, 0)))
+    small_size = small.shape[0]
+    small = jnp.pad(small, (0, width - small_size))
+    gates_pad = jnp.zeros((own, LANES - 2 * heads), BF16)
     mixer_weight = lax.all_gather(
         jnp.concatenate(
-            [query_proj, key_proj, value_proj, gate_proj, alpha_proj, beta_proj, small.T], axis=1
+            [query_proj, key_proj, value_proj, gate_proj, alpha_proj, beta_proj, gates_pad], axis=1
         ),
         GROUP, axis=0, tiled=True,
     )
-    x_low = to_pack(tokens)
+    dy_sent = jnp.concatenate(
+        [
+            picked(part_pick, cotangent).reshape(groups, share, width),
+            jnp.broadcast_to(small[None, None, :], (groups, PAD, width)),
+        ],
+        axis=1,
+    )
+    x_sent = picked(send_pick, tokens).reshape(pack_rows, width)
+    x_moved, dy_sent = together((exchange(x_sent), dy_sent))
+    x_low = jnp.dot(arrive_pick, x_moved, preferred_element_type=F32).astype(BF16)
+    dy_moved = exchange(dy_sent)
+    extras = dy_moved[:, share, :small_size].astype(F32)
+    dy_own = dy_moved[:, :share].reshape(rows, width)
     out_weight = lax.all_gather(out_proj.T, GROUP, axis=0, tiled=True)
-    pair_weight = lax.all_gather(
-        jnp.concatenate([ffn_gate, ffn_up], axis=1), GROUP, axis=0, tiled=True
-    )
     down_weight = lax.all_gather(ffn_down.T, GROUP, axis=0, tiled=True)
-    dy_low = to_pack(cotangent)
+    pair_shard = jnp.concatenate([ffn_gate, ffn_up], axis=1)
 
     tail_at = 2 * key_cols + 2 * value_cols
-    extras = mixer_weight[:, tail_at:].T[2 * heads :].astype(F32)
-    gain_in_full = extras[0:1]
-    gain_mid_full = extras[1:2]
+    gain_in_full = extras[:, :own].reshape(1, width)
+    gain_mid_full = extras[:, own : 2 * own].reshape(1, width)
 
     def taps_of(start, weight):
-        count = weight.size // own
-        flat = extras[start : start + count].reshape(count, groups, own)
-        flat = jnp.transpose(flat, (1, 0, 2)).reshape(groups, spans, heads, weight.shape[2])
-        return jnp.transpose(flat, (1, 2, 0, 3)).reshape(spans, -1), start + count
-
-    query_taps, at = taps_of(2, query_conv)
+        flat = extras[:, start : start + weight.size]
+        flat = flat.reshape(groups, spans, heads, weight.shape[2])
+        return jnp.transpose(flat, (1, 2, 0, 3)).reshape(spans, -1), start + weight.size
+
+    query_taps, at = taps_of(2 * own, query_conv)
     key_taps, at = taps_of(at, key_conv)
     value_taps, at = taps_of(at, value_conv)
     taps = jnp.pad(
         jnp.concatenate([query_taps, key_taps, value_taps], axis=1), ((0, PAD - spans), (0, 0))
     )
-    head_gain = extras[at].reshape(groups, own)[:, : gain_head.shape[0]].reshape(1, value_size)
-    head_gain = jnp.broadcast_to(head_gain, (PAD, value_size))
+    head_gain = jnp.broadcast_to(extras[:, at:].reshape(1, value_size), (PAD, value_size))
     par = jnp.zeros((PAD, LANES), F32)
     par = par.at[0, :heads].set(-jnp.exp(decay_log)).at[1, :heads].set(step_bias)
     length_row = lax.dynamic_slice(
@@ -607,23 +827,41 @@
     rate_in = lax.rsqrt(jnp.mean(x_float * x_float, axis=1, keepdims=True) + square_eps)
     normed_in = (x_float * rate_in * gain_in_full).astype(BF16)
     proj = dot_nn(normed_in, mixer_weight)
+    dy_all = copy_rows_turned(together((dy_own, mixer_weight))[0])
     normed_low, *saved = delta_forward(proj, info, seg_rows, par, taps, head_gain, sizes)
 
-    def my_rows(values):
-        return lax.dynamic_slice(values, (tp_place * rows, 0), (rows, values.shape[1])).astype(F32)
-
-    hidden_in = my_rows(x_low) + share_sum(dot_nt(normed_low, out_weight).astype(BF16))
-    rate_mid = lax.rsqrt(jnp.mean(hidden_in * hidden_in, axis=1, keepdims=True) + square_eps)
-    mid_low = lax.all_gather(
-        (hidden_in * rate_mid * gain_mid_full).astype(BF16), "tp", axis=0, tiled=True
-    )
+    mixed_part = dot_nt(normed_low, out_weight).astype(BF16)
+    from_after, from_before, dy_all = sum_rows_relayed(mixed_part, rows, dy_all)
+    pair_weight = lax.all_gather(pair_shard, GROUP, axis=0, tiled=True)
+    dy_low = jnp.dot(place_pick, dy_all, preferred_element_type=F32).astype(BF16)
+    own_f32 = jax.ShapeDtypeStruct((rows, width), F32)
+    own_low = jax.ShapeDtypeStruct((rows, width), BF16)
+    gain_part = jax.ShapeDtypeStruct((PAD, width), F32)
+    place = tp_place.reshape(1)
+    gain_in_8 = jnp.broadcast_to(gain_in_full, (PAD, width))
+    gain_mid_8 = jnp.broadcast_to(gain_mid_full, (PAD, width))
+    hidden_in, mid_own = row_parts(
+        middle_kernel,
+        place,
+        [
+            ("all", mixed_part),
+            ("own", from_after),
+            ("own", from_before),
+            ("all", x_low),
+            ("one", gain_mid_8),
+        ],
+        [("own", own_f32), ("own", own_low)],
+        rows,
+    )
+    mid_low = copy_rows_ordered(mid_own)
+    grad_hidden = dot_nn(dy_low, down_weight)
+    mid_low, grad_hidden = together((mid_low, grad_hidden))
     units = ffn_gate.shape[1]
     both = dot_nn(mid_low, pair_weight)
     gate_value, up_value = both[:, :units], both[:, units:]
     gate_sig = sigmoid(gate_value)
     gate_act = gate_value * gate_sig
     hidden_low = (gate_act * up_value).astype(BF16)
-    grad_hidden = dot_nn(dy_low, down_weight)
     pair_grad = jnp.concatenate(
         [
             (grad_hidden * up_value * (gate_sig * (1.0 + gate_value * (1.0 - gate_sig)))).astype(BF16),
@@ -631,47 +869,74 @@
         ],
         axis=1,
     )
-    mid_grad = share_sum(dot_nt(pair_grad, pair_weight).astype(BF16))
-    ffn_part = dot_nt(hidden_low, down_weight).astype(BF16)
-
-    scaled = mid_grad * gain_mid_full
-    hidden_grad = (
-        my_rows(dy_low)
-        + rate_mid * scaled
-        - rate_mid**3 * hidden_in * jnp.mean(hidden_in * scaled, axis=1, keepdims=True)
-    )
-    grad_mid_gain = jnp.sum(mid_grad * hidden_in * rate_mid, axis=0)
-    mix_low = lax.all_gather(hidden_grad.astype(BF16), "tp", axis=0, tiled=True)
-    mix_low, ffn_part = lax.optimization_barrier((mix_low, ffn_part))
+    back_part = dot_nt(pair_grad, pair_weight).astype(BF16)
+    back_part, pair_late, hidden_late, mid_late = together(
+        (back_part, pair_grad, hidden_low, mid_low)
+    )
+    back_moved = deal(back_part, "b")
+    ffn_part = dot_nt(hidden_late, down_weight).astype(BF16)
+    grad_ffn_part = jnp.concatenate(
+        [
+            dot_tn(mid_late, pair_late).astype(BF16),
+            dot_tn(dy_low, hidden_late).astype(BF16),
+        ],
+        axis=1,
+    )
+    back_moved, ffn_part, grad_ffn_part = together((back_moved, ffn_part, grad_ffn_part))
+
+    def owners(value):
+        return lax.psum_scatter(value, GROUP, scatter_dimension=0, tiled=True)
+
+    hidden_grad, mix_own, grad_mid_gain = row_parts(
+        middle_back_kernel,
+        place,
+        [("own", back_moved), ("own", hidden_in), ("all", dy_low), ("one", gain_mid_8)],
+        [("own", own_f32), ("own", own_low), ("one", gain_part)],
+        rows,
+    )
+    grad_mid_gain = jnp.sum(grad_mid_gain, axis=0)
+    mix_low = copy_rows_ordered(mix_own)
+    mix_low, ffn_part = together((mix_low, ffn_part))
+    grad_ffn = owners(grad_ffn_part)
     dnormed = dot_nn(mix_low, out_weight)
     grad_proj, conv_grad, head_gain_grad, decay_grads = delta_backward(
         proj, info, seg_rows, par, taps, head_gain, saved, dnormed, sizes
     )
-    first_grad = share_sum(dot_nt(grad_proj, mixer_weight).astype(BF16))
-
-    result = hidden_in + share_sum(ffn_part)
-    result_back = to_given(result, None).reshape(rows, width)
-    mixed, unused = spread(jnp.pad(result_back, ((0, PAD), (0, 0))))
-
-    def owners(value, axis):
-        return lax.psum_scatter(
-            value.astype(BF16), GROUP, scatter_dimension=axis, tiled=True
-        ).astype(F32)
-
-    grad_pair = owners(dot_tn(mid_low, pair_grad), 0)
-    grad_down = owners(dot_tn(dy_low, hidden_low), 0).T
-    grad_out = owners(dot_tn(mix_low, normed_low), 0).T
-    grad_mixer = owners(dot_tn(normed_in, grad_proj), 0)
-
-    x_own = my_rows(x_low)
-    rate_own = lax.rsqrt(jnp.mean(x_own * x_own, axis=1, keepdims=True) + square_eps)
-    scaled_in = first_grad * gain_in_full
-    token_grad = (
-        hidden_grad
-        + rate_own * scaled_in
-        - rate_own**3 * x_own * jnp.mean(x_own * scaled_in, axis=1, keepdims=True)
-    )
-    grad_in_gain = jnp.sum(first_grad * x_own * rate_own, axis=0)
+    first_part = dot_nt(grad_proj, mixer_weight).astype(BF16)
+    result_moved = deal(ffn_part, "y")
+    first_part, proj_late, mix_late, normed_late, grad_ffn, result_moved = together(
+        (first_part, grad_proj, mix_low, normed_low, grad_ffn, result_moved)
+    )
+    first_moved = deal(first_part, "n")
+    grad_mixer_part = jnp.concatenate(
+        [
+            dot_tn(normed_in, proj_late).astype(BF16),
+            dot_tn(mix_late, normed_late).astype(BF16),
+        ],
+        axis=1,
+    )
+    result = (hidden_in + add_dealt(result_moved, "y")).astype(BF16)
+    result_back = exchange(to_sources(result)).reshape(rows, width)
+    result_back = jnp.pad(result_back, ((0, PAD), (0, 0)))
+    result_near = relay_first(result_back)
+    first_moved, grad_mixer_part, *result_near = together(
+        (first_moved, grad_mixer_part, *result_near)
+    )
+
+    grad_mixer_all = owners(grad_mixer_part)
+    grad_mixer = grad_mixer_all[:, : mixer_weight.shape[1]].astype(F32)
+    grad_out = grad_mixer_all[:, mixer_weight.shape[1] :].astype(F32).T
+    grad_pair = grad_ffn[:, : 2 * units].astype(F32)
+    grad_down = grad_ffn[:, 2 * units :].astype(F32).T
+
+    token_grad, grad_in_gain = row_parts(
+        first_back_kernel,
+        place,
+        [("own", first_moved), ("own", hidden_grad), ("all", x_low), ("one", gain_in_8)],
+        [("own", own_low), ("one", gain_part)],
+        rows,
+    )
+    grad_in_gain = jnp.sum(grad_in_gain, axis=0)
 
     conv_sum = jnp.sum(conv_grad.reshape(spans, PAD, -1), axis=1)
 
@@ -694,7 +959,11 @@
     packed = jnp.concatenate(parts, axis=1)
     packed = jnp.pad(packed, ((0, 0), (0, width - packed.shape[1])))
     extra = jnp.pad(pair_rows(packed), ((0, 0), (0, PAD - 2), (0, 0)))
-    came = to_given(token_grad, extra)
+    grad_sent = to_sources(token_grad)
+    came = exchange(jnp.concatenate([grad_sent, extra], axis=1))
+    before, after = result_near
+    result_far = relay_second(before, after)
+    mixed, unused = to_given((result_back, before, after, *result_far))
     summed = jnp.sum(came[:, share : share + 2].astype(F32), axis=(0, 1))
     block = jnp.concatenate(
         [
@@ -703,9 +972,9 @@
         ],
         axis=0,
     )
-    grad_tokens, full = spread(block)
+    grad_tokens, full = to_given(relayed_blocks(block))
     tp_summed = jnp.sum(
-        full.reshape(tp_count, held, width)[:, rows : rows + 2].astype(F32), axis=(0, 1)
+        full.reshape(RELAYED, held, width)[:, rows : rows + 2].astype(F32), axis=(0, 1)
     )
     pieces = []
     offset = 0

time: 1040 us -> 799 us (0.77)
  waiting for transfers between devices: 512 us -> 311 us
  blocking collectives: 135 us -> 0 us
  starting transfers between devices: 24.4 us -> 84 us
  other arithmetic: 32.4 us -> 71.1 us
  local copies, waits for them, and re-layouts: 46.2 us -> 79 us
  Pallas kernels: 93.5 us -> 61.5 us
  matrix products: 182 us -> 166 us
    ppermute x0 -> x28, waiting for transfers between devices: none -> 216 us  [the longest x25 211 us: relay_send(): return lax.ppermute(value, 'tp', route)]
    all_gather x5 -> x1, waiting for transfers between devices: 146 us -> 0.01 us  [per_device(): pair_weight = lax.all_gather(pair_shard, GROUP, axis=0, tiled=True)]
    all_to_all x5, waiting for transfers between devices: 208 us -> 69 us  [the longest x4 58.8 us: exchange(): return lax.all_to_all(sent, GROUP, split_axis=0, concat_axis=0, tiled=True)]
    all_to_all x3 -> x0, blocking collectives: 135 us -> none  [the longest x1 75.5 us: share_sum(): moved = lax.all_to_all(part, 'tp', split_axis=0, concat_axis=0, tiled=True)]
    reduce_scatter x4, waiting for transfers between devices: 88.4 us -> 22.8 us  [the longest x2 22.8 us: deal(): return lax.psum_scatter(part, 'tp', scatter_dimension=0, tiled=True)]
    ppermute x0 -> x28, starting transfers between devices: none -> 60.8 us  [the longest x25 56.2 us: relay_send(): return lax.ppermute(value, 'tp', route)]
    all_gather x1, waiting for transfers between devices: 38.1 us -> 1.67 us  [per_device(): lax.all_gather(jnp.concatenate([query_proj, key_proj, value_proj, gate_pr...]
    pallas_call x1, Pallas kernels: 59.3 us -> 23.1 us  [delta_forward(): pl.pallas_call(functools.partial(forward_kernel, head_count, key_size, va...]
  transfers between devices with their start and end apart: 17 -> 41, of which waited for: 12 -> 25; matrix products, arithmetic and copies ran while one was open for 20% -> 32% of each run, Pallas kernels for 9% -> 8%
where the time goes in v2:
time: 799 us; the launch traced here: 789 us
  waiting for transfers between devices  311 us (39%)
  matrix products  166 us (21%)
  starting transfers between devices  84 us (11%)
  local copies, waits for them, and re-layouts  79 us (10%)
  other arithmetic  71.1 us (9%)
  Pallas kernels  61.5 us (8%)
  between operations  16 us (2%)
    ppermute x25, waiting for transfers between devices, relay_send(): return lax.ppermute(value, 'tp', route)  211 us
    all_to_all x4, waiting for transfers between devices, exchange(): return lax.all_to_all(sent, GROUP, split_axis=0, concat_axis=0, tiled=True)  58.8 us
    ppermute x25, starting transfers between devices, relay_send(): return lax.ppermute(value, 'tp', route)  56.2 us
    dot_general x4, matrix products, dot_nn(): lax.dot_general(left, right, (((1,), (0,)), ((), ())), preferred_element_...  48.5 us
    dot_general x4, matrix products, dot_nt(): lax.dot_general(left, right, (((1,), (1,)), ((), ())), preferred_element_...  45.1 us
    dot_general x4, matrix products, dot_tn(): lax.dot_general(left, right, (((0,), (0,)), ((), ())), preferred_element_...  40.6 us
    pallas_call x1, Pallas kernels, delta_backward(): pl.pallas_call(functools.partial(backward_kernel, head_count, key_size, v...  33.7 us
    unnamed x137, local copies, waits for them, and re-layouts  33.4 us
  transfers between devices with their start and end apart: 41, of which 25 were waited for; matrix products, arithmetic and copies ran while one was open for 32% of the time, Pallas kernels for 8%

profile of v2, /device:TPU:0, one launch (start us, length us, event | category | flops | bytes accessed | tf_op | source)
XLA Modules:
  0.0 789.2 jit_solution(7505016956262728957)
XLA Ops:
  40.7 38.2 %all-to-all-done = bf16[8,96,2048]{2,1,0:T(8,128)(2,1)} async-done(((bf16[8,96,2048]{2,1,0:T(8,128)(2,1)}), bf16[8,96,2048]{2,1,0:T(8,128)(2,1)}, u32[]{:S(2)}, u32[]{:S(2)}) %all-to-all-start) | async-done | bytes 3145760 | tf_op jit(solution)/shard_map/all_to_all | solution.py:755
  89.0 20.6 %all-to-all-done.1 = bf16[8,32,2048]{2,1,0:T(8,128)(2,1)} async-done(((bf16[8,32,2048]{2,1,0:T(8,128)(2,1)}), bf16[8,32,2048]{2,1,0:T(8,128)(2,1)}, u32[]{:S(2)}, u32[]{:S(2)}) %all-to-all-start.1) | async-done | bytes 1048608 | tf_op jit(solution)/shard_map/all_to_all | solution.py:755
  136.2 16.9 %fusion.23.proj.prior = f32[768,3200]{1,0:T(8,128)} fusion(bf16[2048,3200]{1,0:T(8,128)(2,1)} %all-gather.5.cloned.1.call-done, bf16[768,2048]{1,0:T(8,128)(2,1)S(1)} %get-tuple-element.303.x_ref, f32[2048]{0:T(1024)} %bitcast.124, f32[768]{0:T(1024)} %add_rsqrt_fusion), kind=kOutput, calls=%fused_computation.66 | convolution fusion | flops 10072621056 | bytes 26094592 | tf_op jit(solution)/shard_map/dot_general | solution.py:19
  153.1 23.1 %delta_forward.1 = (bf16[768,1024]{1,0:T(8,128)(2,1)S(1)}, f32[6,4,128,256]{3,2,1,0:T(8,128)S(1)}, bf16[6,4,128,128]{3,2,1,0:T(8,128)(2,1)S(1)}, f32[768,1024]{1,0:T(8,128)}, f32[768,1024]{1,0:T(8,128)}) custom-call(f32[768,3200]{1,0:T(8,128)} %fusion.23.proj.prior, f32[768,128]{1,0:T(8,128)S(1)} %pad.37.info_ref, f32[8,768]{1,0:T(8,128)S(1)} %broadcast_in_dim.149.segr, ...), custom_call_target="tpu_custom_call" | custom-call | tf_op jit(solution)/shard_map/delta_forward/pallas_call | solution.py:401
  212.2 15.3 %collective-permute-done.2 = bf16[192,2048]{1,0:T(8,128)(2,1)} collective-permute-done((bf16[192,2048]{1,0:T(8,128)(2,1)}, bf16[192,2048]{1,0:T(8,128)(2,1)}, u32[]{:S(2)}, u32[]{:S(2)}) %collective-permute-start.2) | collective-permute-done | bytes 786464 | tf_op jit(solution)/shard_map/ppermute | solution.py:608
  231.4 12.5 %collective-permute-start.7 = (bf16[192,2048]{1,0:T(8,128)(2,1)S(1)}, bf16[192,2048]{1,0:T(8,128)(2,1)S(1)}, u32[]{:S(2)}, u32[]{:S(2)}) collective-permute-start(bf16[192,2048]{1,0:T(8,128)(2,1)S(1)} %get-tuple-element.249), channel_id=1, source_target_pairs={{0,1},{1,2},{2,3},{4,5},{5,6},{6,7},{8,9},{9,10},{10,11},{12,13},{... | collective-permute-start | bytes 2359304 | tf_op jit(solution)/shard_map/ppermute | solution.py:608
  243.9 15.1 %collective-permute-done.6.after = bf16[192,2048]{1,0:T(8,128)(2,1)S(1)} collective-permute-done((bf16[192,2048]{1,0:T(8,128)(2,1)S(1)}, bf16[192,2048]{1,0:T(8,128)(2,1)S(1)}, u32[]{:S(2)}, u32[]{:S(2)}) %collective-permute-start.6) | collective-permute-done | bytes 786464 | tf_op jit(solution)/shard_map/ppermute | solution.py:608
  304.1 10.2 %collective-permute-done.10 = bf16[192,2048]{1,0:T(8,128)(2,1)} collective-permute-done((bf16[192,2048]{1,0:T(8,128)(2,1)}, bf16[192,2048]{1,0:T(8,128)(2,1)}, u32[]{:S(2)}, u32[]{:S(2)}) %collective-permute-start.10) | collective-permute-done | bytes 786464 | tf_op jit(solution)/shard_map/ppermute | solution.py:608
  314.4 13.1 %collective-permute-done.12 = bf16[192,2048]{1,0:T(8,128)(2,1)} collective-permute-done((bf16[192,2048]{1,0:T(8,128)(2,1)}, bf16[192,2048]{1,0:T(8,128)(2,1)}, u32[]{:S(2)}, u32[]{:S(2)}) %collective-permute-start.12) | collective-permute-done | bytes 786464 | tf_op jit(solution)/shard_map/ppermute | solution.py:608
  332.0 13.7 %fusion.83 = f32[768,2816]{1,0:T(8,128)S(1)} fusion(bf16[768,2048]{1,0:T(8,128)(2,1)} %pad_maximum_fusion.4, bf16[2048,2816]{1,0:T(8,128)(2,1)} %all-gather.11.cloned.1.call-done), kind=kOutput, calls=%fused_computation.246 | convolution fusion | flops 8858370048 | bytes 23330816 | tf_op jit(solution)/shard_map/dot_general | solution.py:19
  353.2 13.2 %convolution_convert_fusion.10 = bf16[768,2048]{1,0:T(8,128)(2,1)} fusion(bf16[2048,2816]{1,0:T(8,128)(2,1)} %all-gather.11.cloned.1.call-done, bf16[768,1408]{1,0:T(8,128)(2,1)S(1)} %get-tuple-element.247, bf16[768,1408]{1,0:T(8,128)(2,1)S(1)} %get-tuple-element.246), kind=kOutput, calls=%fused_computation.33 | convolution fusion | flops 8868593664 | bytes 19005440 | tf_op jit(solution)/shard_map/dot_general | solution.py:23
  382.9 12.2 %convolution_convert_fusion.1 = bf16[2048,2816]{1,0:T(8,128)(2,1)S(1)} fusion(bf16[768,2048]{1,0:T(8,128)(2,1)S(1)} %copy-done.34, bf16[768,2816]{1,0:T(8,128)(2,1)} %pad_maximum_fusion.2), kind=kOutput, calls=%fused_computation.3 | convolution fusion | flops 8864137216 | bytes 19005440 | tf_op jit(solution)/shard_map/dot_general | solution.py:27
  402.0 22.8 %reduce-scatter.5.cloned.1.call-done.moved = bf16[192,2048]{1,0:T(8,128)(2,1)} async-done(((bf16[768,2048]{1,0:T(8,128)(2,1)}), bf16[192,2048]{1,0:T(8,128)(2,1)}) %reduce-scatter.5.cloned.1.call-update) | async-done | bytes 786448 | tf_op jit(solution)/shard_map/reduce_scatter | solution.py:590
  433.8 15.5 %collective-permute-done.13 = bf16[192,2048]{1,0:T(8,128)(2,1)S(1)} collective-permute-done((bf16[192,2048]{1,0:T(8,128)(2,1)S(1)}, bf16[192,2048]{1,0:T(8,128)(2,1)S(1)}, u32[]{:S(2)}, u32[]{:S(2)}) %collective-permute-start.13) | collective-permute-done | bytes 786464 | tf_op jit(solution)/shard_map/ppermute | solution.py:608
  457.1 20.0 %collective-permute-done.15 = bf16[192,2048]{1,0:T(8,128)(2,1)S(1)} collective-permute-done((bf16[192,2048]{1,0:T(8,128)(2,1)S(1)}, bf16[192,2048]{1,0:T(8,128)(2,1)S(1)}, u32[]{:S(2)}, u32[]{:S(2)}) %collective-permute-start.15) | collective-permute-done | bytes 786464 | tf_op jit(solution)/shard_map/ppermute | solution.py:608
  477.1 14.7 %collective-permute-done.17 = bf16[192,2048]{1,0:T(8,128)(2,1)S(1)} collective-permute-done((bf16[192,2048]{1,0:T(8,128)(2,1)S(1)}, bf16[192,2048]{1,0:T(8,128)(2,1)S(1)}, u32[]{:S(2)}, u32[]{:S(2)}) %collective-permute-start.17) | collective-permute-done | bytes 786464 | tf_op jit(solution)/shard_map/ppermute | solution.py:608
  507.8 33.7 %delta_backward.1 = (bf16[768,3200]{1,0:T(8,128)(2,1)}, f32[32,2048]{1,0:T(8,128)S(1)}, f32[8,1024]{1,0:T(8,128)S(1)}, f32[16,128]{1,0:T(8,128)S(1)}) custom-call(f32[768,3200]{1,0:T(8,128)} %fusion.23.proj.prior, f32[768,3200]{1,0:T(8,128)} %fusion.23.proj.prior, f32[768,128]{1,0:T(8,128)S(1)} %pad.37.info_ref, f32[8,768]{1,0:T(8,128)S(1)} %copy-done.23, ...), custom_call_target="tpu_custom_call" | custom-call | tf_op jit(solution)/shard_map/delta_backward/pallas_call | solution.py:446
  543.3 16.5 %convolution_convert_fusion.8 = bf16[768,2048]{1,0:T(8,128)(2,1)} fusion(bf16[768,3200]{1,0:T(8,128)(2,1)} %get-tuple-element.117, bf16[2048,3200]{1,0:T(8,128)(2,1)} %all-gather.5.cloned.1.call-done), kind=kOutput, calls=%fused_computation.31 | convolution fusion | flops 10067902464 | bytes 21168128 | tf_op jit(solution)/shard_map/dot_general | solution.py:23
  559.9 10.2 %all-to-all-done.2 = bf16[4,192,2048]{2,1,0:T(8,128)(2,1)} async-done(((bf16[4,192,2048]{2,1,0:T(8,128)(2,1)}), bf16[4,192,2048]{2,1,0:T(8,128)(2,1)}, u32[]{:S(2)}, u32[]{:S(2)}) %all-to-all-start.2) | async-done | bytes 3145760 | tf_op jit(solution)/shard_map/all_to_all | solution.py:591
  581.0 16.3 %convolution_convert_fusion = bf16[2048,3200]{1,0:T(8,128)(2,1)} fusion(bf16[768,3200]{1,0:T(8,128)(2,1)} %get-tuple-element.117, bf16[768,2048]{1,0:T(8,128)(2,1)S(1)} %copy-done.4, f32[2048]{0:T(1024)S(1)} %bitcast.125, f32[768]{0:T(1024)S(1)} %copy-done.53), kind=kOutput, calls=%fused_computation.2 | convolution fusion | flops 10079174656 | bytes 21179392 | tf_op jit(solution)/shard_map/dot_general | solution.py:27
  608.3 14.0 %pad_maximum_fusion.1 = bf16[2048,4224]{1,0:T(8,128)(2,1)} fusion(bf16[2048,1024]{1,0:T(8,128)(2,1)} %convolution_convert_fusion.3, bf16[2048,3200]{1,0:T(8,128)(2,1)} %convolution_convert_fusion), kind=kLoop, calls=%fused_computation.1 | loop fusion | flops 34603008 | bytes 34603008 | tf_op jit(solution)/shard_map/concatenate | solution.py:911
  622.3 20.2 %collective-permute-done.18 = bf16[200,2048]{1,0:T(8,128)(2,1)} collective-permute-done((bf16[200,2048]{1,0:T(8,128)(2,1)}, bf16[200,2048]{1,0:T(8,128)(2,1)}, u32[]{:S(2)}, u32[]{:S(2)}) %collective-permute-start.18) | collective-permute-done | bytes 819232 | tf_op jit(solution)/shard_map/ppermute | solution.py:608
  679.3 15.8 %collective-permute-done.22 = bf16[200,2048]{1,0:T(8,128)(2,1)} collective-permute-done((bf16[200,2048]{1,0:T(8,128)(2,1)}, bf16[200,2048]{1,0:T(8,128)(2,1)}, u32[]{:S(2)}, u32[]{:S(2)}) %collective-permute-start.22) | collective-permute-done | bytes 819232 | tf_op jit(solution)/shard_map/ppermute | solution.py:608
  729.8 27.1 %collective-permute-done.26 = bf16[200,2048]{1,0:T(8,128)(2,1)} collective-permute-done((bf16[200,2048]{1,0:T(8,128)(2,1)S(1)}, bf16[200,2048]{1,0:T(8,128)(2,1)}, u32[]{:S(2)}, u32[]{:S(2)}) %collective-permute-start.26) | collective-permute-done | bytes 819232 | tf_op jit(solution)/shard_map/ppermute | solution.py:608
  (385 shorter events, 342.4 us)
Async XLA Ops:
  7.2 124.4 %all-gather.5.cloned.1.call-start = ((), (), s32[]{:S(2)}) async-start(), calls=%async_computation.9 | async-start | bytes 14745600 | tf_op jit(solution)/shard_map/all_gather | solution.py:780
  12.9 167.7 %all-gather.7.cloned.1.call-start = ((), (), s32[]{:S(2)}) async-start(), calls=%async_computation.10 | async-start | bytes 4718592 | tf_op jit(solution)/shard_map/all_gather | solution.py:799
  13.6 281.3 %all-gather.9.cloned.1.call-start = ((), (), s32[]{:S(2)}) async-start(), calls=%async_computation.11 | async-start | bytes 6488064 | tf_op jit(solution)/shard_map/all_gather | solution.py:800
  14.3 317.7 %all-gather.11.cloned.1.call-start = ((), (), s32[]{:S(2)}) async-start(), calls=%async_computation.12 | async-start | bytes 12976128 | tf_op jit(solution)/shard_map/all_gather | solution.py:835
  22.1 56.8 %all-to-all-start = ((bf16[8,96,2048]{2,1,0:T(8,128)(2,1)}), bf16[8,96,2048]{2,1,0:T(8,128)(2,1)}, u32[]{:S(2)}, u32[]{:S(2)}) async-start(bf16[8,96,2048]{2,1,0:T(8,128)(2,1)} %bitcast.100), calls=%async_computation | async-start | bytes 6291456 | tf_op jit(solution)/shard_map/all_to_all | solution.py:755
  78.9 30.7 %all-to-all-start.1 = ((bf16[8,32,2048]{2,1,0:T(8,128)(2,1)}), bf16[8,32,2048]{2,1,0:T(8,128)(2,1)}, u32[]{:S(2)}, u32[]{:S(2)}) async-start(bf16[8,32,2048]{2,1,0:T(8,128)(2,1)} %pad_maximum_fusion.7), calls=%async_computation.1 | async-start | bytes 2097152 | tf_op jit(solution)/shard_map/all_to_all | solution.py:755
  83.2 341.5 %reduce-scatter.5.cloned.1.call-start = ((), (), s32[]{:S(2)}) async-start(), calls=%async_computation.13 | async-start | bytes 3932160 | tf_op jit(solution)/shard_map/reduce_scatter | solution.py:590
  131.6 63.2 %collective-permute-start.5 = (bf16[192,2048]{1,0:T(8,128)(2,1)}, bf16[192,2048]{1,0:T(8,128)(2,1)}, u32[]{:S(2)}, u32[]{:S(2)}) collective-permute-start(bf16[192,2048]{1,0:T(8,128)(2,1)} %bitcast.103), channel_id=1, source_target_pairs={{0,3},{1,0},{2,1},{3,2},{4,7},{5,4},{6,5},{7,6},{8,11},{9,8},{10,9... | collective-permute-start | bytes 2359304 | tf_op jit(solution)/shard_map/ppermute | solution.py:680
  134.9 68.8 %collective-permute-start.4 = (bf16[192,2048]{1,0:T(8,128)(2,1)}, bf16[192,2048]{1,0:T(8,128)(2,1)}, u32[]{:S(2)}, u32[]{:S(2)}) collective-permute-start(bf16[192,2048]{1,0:T(8,128)(2,1)} %bitcast.104), channel_id=1, source_target_pairs={{0,2},{1,3},{2,0},{3,1},{4,6},{5,7},{6,4},{7,5},{8,10},{9,11},{10,... | collective-permute-start | bytes 2359304 | tf_op jit(solution)/shard_map/ppermute | solution.py:680
  134.9 68.8 %collective-permute-start.3 = (bf16[192,2048]{1,0:T(8,128)(2,1)}, bf16[192,2048]{1,0:T(8,128)(2,1)}, u32[]{:S(2)}, u32[]{:S(2)}) collective-permute-start(bf16[192,2048]{1,0:T(8,128)(2,1)} %bitcast.105), channel_id=1, source_target_pairs={{0,1},{1,2},{2,3},{3,0},{4,5},{5,6},{6,7},{7,4},{8,9},{9,10},{10,1... | collective-permute-start | bytes 2359304 | tf_op jit(solution)/shard_map/ppermute | solution.py:680
  194.8 32.7 %collective-permute-start.2 = (bf16[192,2048]{1,0:T(8,128)(2,1)}, bf16[192,2048]{1,0:T(8,128)(2,1)}, u32[]{:S(2)}, u32[]{:S(2)}) collective-permute-start(bf16[192,2048]{1,0:T(8,128)(2,1)} %get-tuple-element.257), channel_id=1, source_target_pairs={{3,1},{0,2},{7,5},{4,6},{11,9},{8,10},{15,13},{12,14},{19,17},{16,... | collective-permute-start | bytes 2359304 | tf_op jit(solution)/shard_map/ppermute | solution.py:608
  230.1 28.9 %collective-permute-start.6 = (bf16[192,2048]{1,0:T(8,128)(2,1)S(1)}, bf16[192,2048]{1,0:T(8,128)(2,1)S(1)}, u32[]{:S(2)}, u32[]{:S(2)}) collective-permute-start(bf16[192,2048]{1,0:T(8,128)(2,1)S(1)} %get-tuple-element.250), channel_id=1, source_target_pairs={{1,0},{2,1},{3,2},{5,4},{6,5},{7,6},{9,8},{10,9},{11,10},{13,12},{... | collective-permute-start | bytes 2359304 | tf_op jit(solution)/shard_map/ppermute | solution.py:608
  293.6 33.9 %collective-permute-start.12 = (bf16[192,2048]{1,0:T(8,128)(2,1)}, bf16[192,2048]{1,0:T(8,128)(2,1)}, u32[]{:S(2)}, u32[]{:S(2)}) collective-permute-start(bf16[192,2048]{1,0:T(8,128)(2,1)} %collective-permute-done.9), channel_id=1, source_target_pairs={{2,1},{1,0},{6,5},{5,4},{10,9},{9,8},{14,13},{13,12},{18,17},{17,1... | collective-permute-start | bytes 2359304 | tf_op jit(solution)/shard_map/ppermute | solution.py:608
  366.4 203.7 %reduce-scatter.7.cloned.1.call-start = ((), (), s32[]{:S(2)}) async-start(), calls=%async_computation.14 | async-start | bytes 19464192 | tf_op jit(solution)/shard_map/reduce_scatter | solution.py:888
  455.8 36.0 %collective-permute-start.17 = (bf16[192,2048]{1,0:T(8,128)(2,1)S(1)}, bf16[192,2048]{1,0:T(8,128)(2,1)S(1)}, u32[]{:S(2)}, u32[]{:S(2)}) collective-permute-start(bf16[192,2048]{1,0:T(8,128)(2,1)S(1)} %collective-permute-done.14), channel_id=1, source_target_pairs={{2,1},{1,0},{6,5},{5,4},{10,9},{9,8},{14,13},{13,12},{18,17},{17,1... | collective-permute-start | bytes 2359304 | tf_op jit(solution)/shard_map/ppermute | solution.py:608
  494.1 76.0 %all-to-all-start.2 = ((bf16[4,192,2048]{2,1,0:T(8,128)(2,1)}), bf16[4,192,2048]{2,1,0:T(8,128)(2,1)}, u32[]{:S(2)}, u32[]{:S(2)}) async-start(bf16[4,192,2048]{2,1,0:T(8,128)(2,1)} %bitcast.17), calls=%async_computation.4 | async-start | bytes 6291456 | tf_op jit(solution)/shard_map/all_to_all | solution.py:591
  498.7 146.8 %reduce-scatter.9.cloned.1.call-start = ((), (), s32[]{:S(2)}) async-start(), calls=%async_computation.15 | async-start | bytes 3932160 | tf_op jit(solution)/shard_map/reduce_scatter | solution.py:590
  580.9 190.5 %reduce-scatter.11.cloned.1.call-start = ((), (), s32[]{:S(2)}) async-start(), calls=%async_computation.16 | async-start | bytes 19464192 | tf_op jit(solution)/shard_map/reduce_scatter | solution.py:888
  604.8 37.7 %collective-permute-start.18 = (bf16[200,2048]{1,0:T(8,128)(2,1)}, bf16[200,2048]{1,0:T(8,128)(2,1)}, u32[]{:S(2)}, u32[]{:S(2)}) collective-permute-start(bf16[200,2048]{1,0:T(8,128)(2,1)} %get-tuple-element.274), channel_id=1, source_target_pairs={{0,1},{1,2},{2,3},{4,5},{5,6},{6,7},{8,9},{9,10},{10,11},{12,13},{... | collective-permute-start | bytes 2457608 | tf_op jit(solution)/shard_map/ppermute | solution.py:608
  607.0 38.5 %collective-permute-start.19 = (bf16[200,2048]{1,0:T(8,128)(2,1)}, bf16[200,2048]{1,0:T(8,128)(2,1)}, u32[]{:S(2)}, u32[]{:S(2)}) collective-permute-start(bf16[200,2048]{1,0:T(8,128)(2,1)} %get-tuple-element.274), channel_id=1, source_target_pairs={{1,0},{2,1},{3,2},{5,4},{6,5},{7,6},{9,8},{10,9},{11,10},{13,12},{... | collective-permute-start | bytes 2457608 | tf_op jit(solution)/shard_map/ppermute | solution.py:608
  657.7 37.5 %collective-permute-start.22 = (bf16[200,2048]{1,0:T(8,128)(2,1)}, bf16[200,2048]{1,0:T(8,128)(2,1)}, u32[]{:S(2)}, u32[]{:S(2)}) collective-permute-start(bf16[200,2048]{1,0:T(8,128)(2,1)} %get-tuple-element.272), channel_id=1, source_target_pairs={{1,3},{2,0},{5,7},{6,4},{9,11},{10,8},{13,15},{14,12},{17,19},{18,... | collective-permute-start | bytes 2457608 | tf_op jit(solution)/shard_map/ppermute | solution.py:608
  664.3 32.9 %all-to-all-start.4 = ((bf16[8,32,2048]{2,1,0:T(8,128)(2,1)}), bf16[8,32,2048]{2,1,0:T(8,128)(2,1)S(1)}, u32[]{:S(2)}, u32[]{:S(2)}) async-start(bf16[8,32,2048]{2,1,0:T(8,128)(2,1)} %fusion.21), calls=%async_computation.7 | async-start | bytes 2097152 | tf_op jit(solution)/shard_map/all_to_all | solution.py:755
  719.6 37.2 %collective-permute-start.26 = (bf16[200,2048]{1,0:T(8,128)(2,1)S(1)}, bf16[200,2048]{1,0:T(8,128)(2,1)}, u32[]{:S(2)}, u32[]{:S(2)}) collective-permute-start(bf16[200,2048]{1,0:T(8,128)(2,1)S(1)} %collective-permute-done.24), channel_id=1, source_target_pairs={{2,1},{1,0},{6,5},{5,4},{10,9},{9,8},{14,13},{13,12},{18,17},{17,1... | collective-permute-start | bytes 2457608 | tf_op jit(solution)/shard_map/ppermute | solution.py:608
  724.4 34.6 %collective-permute-start.27 = (bf16[200,2048]{1,0:T(8,128)(2,1)}, bf16[200,2048]{1,0:T(8,128)(2,1)}, u32[]{:S(2)}, u32[]{:S(2)}) collective-permute-start(bf16[200,2048]{1,0:T(8,128)(2,1)} %get-tuple-element.270), channel_id=1, source_target_pairs={{1,3},{2,0},{5,7},{6,4},{9,11},{10,8},{13,15},{14,12},{17,19},{18,... | collective-permute-start | bytes 2457608 | tf_op jit(solution)/shard_map/ppermute | solution.py:608
  (74 other events, 1270.7 us)
Sparse Core Ops, SparseCore 0:
  13.0 118.5 all-gather.4
  133.5 37.4 all-gather.6
  172.8 44.3 all-gather.8
  219.5 67.6 all-gather.10
  366.5 58.1 reduce-scatter.4
  428.2 118.6 reduce-scatter.6
  570.2 74.5 reduce-scatter.8
  649.0 120.5 reduce-scatter.10

commit v3 on v2

--- a/solution.py
+++ b/solution.py
@@ -513,13 +513,14 @@
     gain_out[...] += rows_summed(part)
 
 
-def first_back_kernel(place, moved, after, x_ref, gain, grad_out, gain_out):
+def first_back_kernel(place, own, after, before, late, x_ref, gain, grad_out, gain_out):
     @pl.when(pl.program_id(0) == 0)
     def start():
         gain_out[...] = jnp.zeros_like(gain_out)
 
-    back, part = norm_back(moved[...].astype(F32), x_ref[...].astype(F32), gain[0:1, :])
-    grad_out[...] = (after[...] + back).astype(BF16)
+    moved = own[...].astype(F32) + after[...].astype(F32) + before[...].astype(F32)
+    back, part = norm_back(moved, x_ref[...].astype(F32), gain[0:1, :])
+    grad_out[...] = (late[...] + back).astype(BF16)
     gain_out[...] += rows_summed(part)
 
 
@@ -546,6 +547,29 @@
         compiler_params=pltpu.CompilerParams(vmem_limit_bytes=40 * 1024 * 1024),
         name=kernel.__name__,
     )(place, *[value for kind, value in arrays])
+
+
+def widen_kernel(grads, *outs):
+    *direct, turned, out_turned = outs
+    start = 0
+    for out in direct:
+        stop = start + out.shape[1]
+        out[...] = grads[:, start:stop].astype(F32)
+        start = stop
+    turned[...] = jnp.transpose(grads[:, start : start + LANES].astype(F32))
+    out_turned[...] = jnp.transpose(grads[:, start + LANES :].astype(F32))
+
+
+def widened(grads, columns):
+    own, total = grads.shape
+    shapes = [(own, count) for count in columns]
+    shapes += [(LANES, own), (total - sum(columns) - LANES, own)]
+    return pl.pallas_call(
+        widen_kernel,
+        out_shape=[jax.ShapeDtypeStruct(shape, F32) for shape in shapes],
+        compiler_params=pltpu.CompilerParams(vmem_limit_bytes=40 * 1024 * 1024),
+        name="widen",
+    )(grads)
 
 
 def place_arrays(length_row, total):
@@ -581,7 +605,7 @@
     return jnp.stack([high, low], axis=-2)
 
 
-SC_SUM = "bn"
+SC_SUM = "by"
 SC_COPY = ""
 
 
@@ -625,27 +649,36 @@
     return (own, before, after, *relay_second(before, after))
 
 
-def sum_rows_relayed(part, rows, along):
+def sum_first(part, rows):
     place = lax.axis_index("tp")
-
+    block = rows_of(part, rows)
+    return (
+        relay_send(block(place - 2), [(2, 1), (3, 2)]),
+        relay_send(block(place + 2), [(1, 2), (0, 1)]),
+        relay_send(block(jnp.where(place == 3, 0, 3)), [(3, 1), (0, 2)]),
+    )
+
+
+def rows_of(part, rows):
     def block(index):
         return lax.dynamic_slice(part, (jnp.clip(index, 0, 3) * rows, 0), (rows, part.shape[1]))
 
-    from_after = relay_send(block(place - 2), [(2, 1), (3, 2)])
-    from_before = relay_send(block(place + 2), [(1, 2), (0, 1)])
-    far = relay_send(block(jnp.where(place == 3, 0, 3)), [(3, 1), (0, 2)])
-    from_after, from_before, far, along = together((from_after, from_before, far, along))
-    far = far.astype(F32)
-    to_before = (
-        block(place - 1).astype(F32) + from_after.astype(F32) + jnp.where(place == 1, far, 0.0)
-    )
-    to_after = (
-        block(place + 1).astype(F32) + from_before.astype(F32) + jnp.where(place == 2, far, 0.0)
-    )
+    return block
+
+
+def sum_middle(part, rows, came):
+    place = lax.axis_index("tp")
+    block = rows_of(part, rows)
+    from_after, from_before, far = (value.astype(F32) for value in came)
+    to_before = block(place - 1).astype(F32) + from_after + jnp.where(place == 1, far, 0.0)
+    to_after = block(place + 1).astype(F32) + from_before + jnp.where(place == 2, far, 0.0)
+    return to_before.astype(BF16), to_after.astype(BF16)
+
+
+def sum_second(to_before, to_after):
     return (
-        relay_send(to_before.astype(BF16), [(1, 0), (2, 1), (3, 2)]),
-        relay_send(to_after.astype(BF16), [(0, 1), (1, 2), (2, 3)]),
-        along,
+        relay_send(to_before, [(1, 0), (2, 1), (3, 2)]),
+        relay_send(to_after, [(0, 1), (1, 2), (2, 3)]),
     )
 
 
@@ -671,14 +704,6 @@
 
 
 RELAYED = 6
-
-
-def copy_rows_turned(own):
-    count = lax.axis_size("tp")
-    blocks = [own]
-    for turn in range(1, count):
-        blocks.append(lax.ppermute(own, "tp", [(i, (i + turn) % count) for i in range(count)]))
-    return jnp.concatenate(blocks, axis=0)
 
 
 together = lax.optimization_barrier
@@ -698,6 +723,7 @@
     all_rows = order.shape[1]
     pack_rows = all_rows // packs
     assert micros * packs == groups and pack_rows == tp_count * rows and tp_count == 4
+    assert rows // groups % 2 == 0
     share = rows // groups
     heads = decay_log.shape[0]
     spans = query_conv.shape[0]
@@ -725,28 +751,31 @@
     send_at = jnp.sum(jnp.where(hit, send_slot, 0), axis=2)
     back_at = jnp.sum(jnp.where(hit, back_slot, 0), axis=2).reshape(micros * rows)
     row_ids = jnp.arange(rows, dtype=jnp.int32)
-    send_row = send_at // (share * tp_count) * share + send_at % share
-    send_ids = jnp.arange(packs * share, dtype=jnp.int32)[None, :, None]
-    sent_here = send_at // share % tp_count == tp_place
-    part_pick = ((send_ids == send_row[:, None, :]) & sent_here[:, None, :]).astype(BF16)
-    send_pick = (row_ids[None, :, None] == send_at[:, None, :]).astype(BF16)
+    half = share // 2
+    near_ranges = tp_count // 2
+    near_rows = groups * near_ranges * share
+    far_rows = groups * half
+    send_rank = send_at % share
+    send_range = send_at // share % tp_count
+    send_pack = send_at // (share * tp_count)
+
+    def pick_rows(slot, wanted, count):
+        ids = jnp.arange(count, dtype=jnp.int32)[None, :, None]
+        return ((ids == slot[:, None, :]) & wanted[:, None, :]).astype(BF16)
+
+    send_pick = pick_rows(send_at, send_at >= 0, rows)
+    near_pick = pick_rows(
+        send_pack * (near_ranges * share) + send_range * share + send_rank,
+        send_range < near_ranges,
+        packs * near_ranges * share,
+    )
+    far_pick = pick_rows(
+        send_pack * half + send_rank % half,
+        (send_range == near_ranges + tp_place // 2) & (send_rank // half == tp_place % 2),
+        packs * half,
+    )
     back_ids = jnp.arange(RELAYED * held, dtype=jnp.int32)
     back_pick = (back_at[:, None] == back_ids[None, :]).astype(BF16)
-
-    pack_order = lax.dynamic_slice(order, (my_micro, my_pack * pack_rows), (1, pack_rows))
-    source = (pack_order // rows).reshape(tp_count, rows)
-    from_each = (source[:, :, None] == jnp.arange(groups, dtype=jnp.int32)).astype(BF16)
-    before = jnp.einsum(
-        "qp,tqg->tpg", strict_up, from_each, preferred_element_type=F32
-    )
-    source_rank = jnp.sum(before * from_each.astype(F32), axis=2).astype(jnp.int32)
-    arrive_at = source * (tp_count * share) + tp_id * share + source_rank
-    pack_ids = jnp.arange(pack_rows, dtype=jnp.int32)
-    arrive_pick = (arrive_at.reshape(pack_rows, 1) == pack_ids[None, :]).astype(BF16)
-    part_at = (tp_place - tp_id) % tp_count * rows + source * share + source_rank
-    place_pick = (part_at.reshape(pack_rows, 1) == pack_ids[None, :]).astype(BF16)
-    return_at = lax.dynamic_slice(source * share + source_rank, (tp_place, 0), (1, rows))
-    return_pick = (row_ids[:, None] == return_at).astype(BF16)
 
     def picked(pick, values):
         return jnp.einsum("msi,mid->msd", pick, values, preferred_element_type=F32).astype(BF16)
@@ -777,28 +806,68 @@
     small_size = small.shape[0]
     small = jnp.pad(small, (0, width - small_size))
     gates_pad = jnp.zeros((own, LANES - 2 * heads), BF16)
+    x_sent = picked(far_pick, tokens).reshape(far_rows, width)
+    query_proj, key_proj, value_proj, gate_proj = together(
+        (query_proj, key_proj, value_proj, gate_proj, x_sent)
+    )[:4]
     mixer_weight = lax.all_gather(
         jnp.concatenate(
             [query_proj, key_proj, value_proj, gate_proj, alpha_proj, beta_proj, gates_pad], axis=1
         ),
         GROUP, axis=0, tiled=True,
     )
-    dy_sent = jnp.concatenate(
-        [
-            picked(part_pick, cotangent).reshape(groups, share, width),
-            jnp.broadcast_to(small[None, None, :], (groups, PAD, width)),
-        ],
-        axis=1,
-    )
-    x_sent = picked(send_pick, tokens).reshape(pack_rows, width)
-    x_moved, dy_sent = together((exchange(x_sent), dy_sent))
-    x_low = jnp.dot(arrive_pick, x_moved, preferred_element_type=F32).astype(BF16)
-    dy_moved = exchange(dy_sent)
-    extras = dy_moved[:, share, :small_size].astype(F32)
-    dy_own = dy_moved[:, :share].reshape(rows, width)
+    small_count = PAD - half % PAD
+    x_moved, near_sent = together(
+        (
+            exchange(
+                jnp.concatenate(
+                    [
+                        x_sent.reshape(groups, half, width),
+                        jnp.broadcast_to(small[None, None, :], (groups, small_count, width)),
+                    ],
+                    axis=1,
+                )
+            ),
+            picked(near_pick, tokens).reshape(near_rows, width),
+        )
+    )
+    near_moved = exchange(near_sent)
+    far_own = x_moved[:, :half].reshape(far_rows, width)
+    x_near = relay_first(far_own)
+    x_moved, order, lengths = together((x_moved, order, lengths, *x_near))[:3]
+    extras = x_moved[:, half, :small_size].astype(F32)
+
+    pack_order = lax.dynamic_slice(order, (my_micro, my_pack * pack_rows), (1, pack_rows))
+    source = (pack_order // rows).reshape(tp_count, rows)
+    from_each = (source[:, :, None] == jnp.arange(groups, dtype=jnp.int32)).astype(BF16)
+    before = jnp.einsum(
+        "qp,tqg->tpg", strict_up, from_each, preferred_element_type=F32
+    )
+    source_rank = jnp.sum(before * from_each.astype(F32), axis=2).astype(jnp.int32)
+    relayer = 2 * (tp_id - near_ranges) + source_rank // half
+    arrive_at = jnp.where(
+        tp_id < near_ranges,
+        source * (near_ranges * share) + tp_id * share + source_rank,
+        near_rows
+        + relayed_block(tp_place, relayer) * far_rows
+        + source * half
+        + source_rank % half,
+    )
+    arrive_ids = jnp.arange(near_rows + RELAYED * far_rows, dtype=jnp.int32)
+    arrive_pick = (arrive_at.reshape(pack_rows, 1) == arrive_ids[None, :]).astype(BF16)
+    pack_ids = jnp.arange(pack_rows, dtype=jnp.int32)
+    full_at = source * (tp_count * share) + tp_id * share + source_rank
+    place_pick = (full_at.reshape(pack_rows, 1) == pack_ids[None, :]).astype(BF16)
+    return_at = lax.dynamic_slice(source * share + source_rank, (tp_place, 0), (1, rows))
+    return_pick = (row_ids[:, None] == return_at).astype(BF16)
+
+    x_all = jnp.concatenate((near_moved, far_own, *x_near, *relay_second(*x_near)), axis=0)
+    x_low = jnp.dot(arrive_pick, x_all, preferred_element_type=F32).astype(BF16)
+    dy_sent = picked(send_pick, cotangent).reshape(pack_rows, width)
+    out_proj, ffn_down = together((out_proj, ffn_down, x_low))[:2]
     out_weight = lax.all_gather(out_proj.T, GROUP, axis=0, tiled=True)
     down_weight = lax.all_gather(ffn_down.T, GROUP, axis=0, tiled=True)
-    pair_shard = jnp.concatenate([ffn_gate, ffn_up], axis=1)
+    pair_shard = jnp.concatenate(together((ffn_gate, ffn_up, x_moved))[:2], axis=1)
 
     tail_at = 2 * key_cols + 2 * value_cols
     gain_in_full = extras[:, :own].reshape(1, width)
@@ -827,11 +896,12 @@
     rate_in = lax.rsqrt(jnp.mean(x_float * x_float, axis=1, keepdims=True) + square_eps)
     normed_in = (x_float * rate_in * gain_in_full).astype(BF16)
     proj = dot_nn(normed_in, mixer_weight)
-    dy_all = copy_rows_turned(together((dy_own, mixer_weight))[0])
+    dy_all = exchange(together((dy_sent, proj))[0])
     normed_low, *saved = delta_forward(proj, info, seg_rows, par, taps, head_gain, sizes)
 
     mixed_part = dot_nt(normed_low, out_weight).astype(BF16)
-    from_after, from_before, dy_all = sum_rows_relayed(mixed_part, rows, dy_all)
+    *mixer_came, dy_all = together((*sum_first(mixed_part, rows), dy_all))
+    from_after, from_before = sum_second(*sum_middle(mixed_part, rows, mixer_came))
     pair_weight = lax.all_gather(pair_shard, GROUP, axis=0, tiled=True)
     dy_low = jnp.dot(place_pick, dy_all, preferred_element_type=F32).astype(BF16)
     own_f32 = jax.ShapeDtypeStruct((rows, width), F32)
@@ -875,14 +945,11 @@
     )
     back_moved = deal(back_part, "b")
     ffn_part = dot_nt(hidden_late, down_weight).astype(BF16)
-    grad_ffn_part = jnp.concatenate(
-        [
-            dot_tn(mid_late, pair_late).astype(BF16),
-            dot_tn(dy_low, hidden_late).astype(BF16),
-        ],
-        axis=1,
-    )
-    back_moved, ffn_part, grad_ffn_part = together((back_moved, ffn_part, grad_ffn_part))
+    grad_down_part = dot_tn(dy_low, hidden_late).astype(BF16)
+    grad_pair_part = dot_tn(mid_late, pair_late).astype(BF16)
+    back_moved, ffn_part, grad_down_part, grad_pair_part = together(
+        (back_moved, ffn_part, grad_down_part, grad_pair_part)
+    )
 
     def owners(value):
         return lax.psum_scatter(value, GROUP, scatter_dimension=0, tiled=True)
@@ -896,43 +963,40 @@
     )
     grad_mid_gain = jnp.sum(grad_mid_gain, axis=0)
     mix_low = copy_rows_ordered(mix_own)
-    mix_low, ffn_part = together((mix_low, ffn_part))
-    grad_ffn = owners(grad_ffn_part)
+    mix_low, ffn_part, grad_down = together((mix_low, ffn_part, owners(grad_down_part)))
     dnormed = dot_nn(mix_low, out_weight)
     grad_proj, conv_grad, head_gain_grad, decay_grads = delta_backward(
         proj, info, seg_rows, par, taps, head_gain, saved, dnormed, sizes
     )
     first_part = dot_nt(grad_proj, mixer_weight).astype(BF16)
     result_moved = deal(ffn_part, "y")
-    first_part, proj_late, mix_late, normed_late, grad_ffn, result_moved = together(
-        (first_part, grad_proj, mix_low, normed_low, grad_ffn, result_moved)
-    )
-    first_moved = deal(first_part, "n")
-    grad_mixer_part = jnp.concatenate(
-        [
-            dot_tn(normed_in, proj_late).astype(BF16),
-            dot_tn(mix_late, normed_late).astype(BF16),
-        ],
-        axis=1,
-    )
+    first_part, proj_late, mix_late, normed_late, result_moved, grad_pair_part = together(
+        (first_part, grad_proj, mix_low, normed_low, result_moved, grad_pair_part)
+    )
+    grad_pair = owners(grad_pair_part)
+    grad_out_part = dot_tn(mix_late, normed_late).astype(BF16)
+    grad_mixer_part = dot_tn(normed_in, proj_late).astype(BF16)
+    grad_mixer_part = jnp.concatenate([grad_mixer_part, grad_out_part], axis=1)
+    *first_came, grad_mixer_part = together((*sum_first(first_part, rows), grad_mixer_part))
+    first_middle = sum_middle(first_part, rows, first_came)
+    late_after, late_before = sum_second(*first_middle)
+    result_moved = together((result_moved, *first_middle))[0]
     result = (hidden_in + add_dealt(result_moved, "y")).astype(BF16)
     result_back = exchange(to_sources(result)).reshape(rows, width)
     result_back = jnp.pad(result_back, ((0, PAD), (0, 0)))
     result_near = relay_first(result_back)
-    first_moved, grad_mixer_part, *result_near = together(
-        (first_moved, grad_mixer_part, *result_near)
-    )
-
-    grad_mixer_all = owners(grad_mixer_part)
-    grad_mixer = grad_mixer_all[:, : mixer_weight.shape[1]].astype(F32)
-    grad_out = grad_mixer_all[:, mixer_weight.shape[1] :].astype(F32).T
-    grad_pair = grad_ffn[:, : 2 * units].astype(F32)
-    grad_down = grad_ffn[:, 2 * units :].astype(F32).T
 
     token_grad, grad_in_gain = row_parts(
         first_back_kernel,
         place,
-        [("own", first_moved), ("own", hidden_grad), ("all", x_low), ("one", gain_in_8)],
+        [
+            ("all", first_part),
+            ("own", late_after),
+            ("own", late_before),
+            ("own", hidden_grad),
+            ("all", x_low),
+            ("one", gain_in_8),
+        ],
         [("own", own_low), ("one", gain_part)],
         rows,
     )
@@ -961,9 +1025,8 @@
     extra = jnp.pad(pair_rows(packed), ((0, 0), (0, PAD - 2), (0, 0)))
     grad_sent = to_sources(token_grad)
     came = exchange(jnp.concatenate([grad_sent, extra], axis=1))
-    before, after = result_near
+    before, after, grad_down = together((*result_near, grad_down, grad_sent))[:3]
     result_far = relay_second(before, after)
-    mixed, unused = to_given((result_back, before, after, *result_far))
     summed = jnp.sum(came[:, share : share + 2].astype(F32), axis=(0, 1))
     block = jnp.concatenate(
         [
@@ -972,7 +1035,16 @@
         ],
         axis=0,
     )
+    result_far = together((*result_far, block))[:3]
+    mixed, unused = to_given((result_back, before, after, *result_far))
     grad_tokens, full = to_given(relayed_blocks(block))
+    *mixer_grads, gates_turned, grad_out = widened(
+        owners(grad_mixer_part), [key_cols, key_cols, value_cols, value_cols]
+    )
+    mixer_grads += [gates_turned[:heads].T, gates_turned[heads : 2 * heads].T]
+    grad_pair = grad_pair.astype(F32)
+    grad_down = grad_down.astype(F32).T
+
     tp_summed = jnp.sum(
         full.reshape(RELAYED, held, width)[:, rows : rows + 2].astype(F32), axis=(0, 1)
     )
@@ -983,17 +1055,11 @@
         pieces.append(origin[offset : offset + length])
         offset += length
     decay_pair = pieces[6].reshape(2, heads)
-    edges = [0, key_cols, 2 * key_cols, 2 * key_cols + value_cols, tail_at]
     return (
         mixed,
         grad_tokens,
         pieces[0],
-        grad_mixer[:, edges[0] : edges[1]],
-        grad_mixer[:, edges[1] : edges[2]],
-        grad_mixer[:, edges[2] : edges[3]],
-        grad_mixer[:, edges[3] : edges[4]],
-        grad_mixer[:, tail_at : tail_at + heads],
-        grad_mixer[:, tail_at + heads : tail_at + 2 * heads],
+        *mixer_grads,
         pieces[3].reshape(query_conv.shape),
         pieces[4].reshape(key_conv.shape),
         pieces[5].reshape(value_conv.shape),

time: 799 us -> 781 us (0.977)
  other arithmetic: 71.1 us -> 52 us
  starting transfers between devices: 84 us -> 103 us
  local copies, waits for them, and re-layouts: 79 us -> 64.2 us
  waiting for transfers between devices: 311 us -> 300 us
    all_to_all x4 -> x5, waiting for transfers between devices: 58.8 us -> 27 us  [exchange(): return lax.all_to_all(sent, GROUP, split_axis=0, concat_axis=0, tiled=True)]
    ppermute x25 -> x35, starting transfers between devices: 56.2 us -> 80.1 us  [relay_send(): return lax.ppermute(value, 'tp', route)]
    ppermute x25 -> x35, waiting for transfers between devices: 211 us -> 227 us  [relay_send(): return lax.ppermute(value, 'tp', route)]
    concatenate x5 -> x3, other arithmetic: 27.7 us -> 13.8 us  [the longest x1 9.34 us: per_device(): grad_mixer_part = jnp.concatenate([grad_mixer_part, grad_out_part], axis=1)]
    reduce_scatter x2 -> x3, waiting for transfers between devices: 0.01 us -> 13.1 us  [owners(): return lax.psum_scatter(value, GROUP, scatter_dimension=0, tiled=True)]
    all_to_all x1 -> x0, waiting for transfers between devices: 10.2 us -> none  [deal(): return lax.all_to_all(part, 'tp', split_axis=0, concat_axis=0, tiled=True)]
    reduce_scatter x2, waiting for transfers between devices: 22.8 us -> 31.8 us  [deal(): return lax.psum_scatter(part, 'tp', scatter_dimension=0, tiled=True)]
    all_to_all x4 -> x5, starting transfers between devices: 17.8 us -> 21.8 us  [exchange(): return lax.all_to_all(sent, GROUP, split_axis=0, concat_axis=0, tiled=True)]
  transfers between devices with their start and end apart: 41 -> 49, of which waited for: 25 -> 27; matrix products, arithmetic and copies ran while one was open for 32% -> 30% of each run, Pallas kernels for 8% -> 8%
where the time goes in v3:
time: 781 us; the launch traced here: 772 us
  waiting for transfers between devices  300 us (38%)
  matrix products  171 us (22%)
  starting transfers between devices  103 us (13%)
  Pallas kernels  65.6 us (8%)
  local copies, waits for them, and re-layouts  64.2 us (8%)
  other arithmetic  52 us (7%)
  between operations  15.8 us (2%)
    ppermute x35, waiting for transfers between devices, relay_send(): return lax.ppermute(value, 'tp', route)  227 us
    ppermute x35, starting transfers between devices, relay_send(): return lax.ppermute(value, 'tp', route)  80.1 us
    dot_general x4, matrix products, dot_nn(): lax.dot_general(left, right, (((1,), (0,)), ((), ())), preferred_element_...  49.4 us
    dot_general x4, matrix products, dot_nt(): lax.dot_general(left, right, (((1,), (1,)), ((), ())), preferred_element_...  44 us
    dot_general x4, matrix products, dot_tn(): lax.dot_general(left, right, (((0,), (0,)), ((), ())), preferred_element_...  43.7 us
    unnamed x137, local copies, waits for them, and re-layouts  34.8 us
    pallas_call x1, Pallas kernels, delta_backward(): pl.pallas_call(functools.partial(backward_kernel, head_count, key_size, v...  33.6 us
    reduce_scatter x2, waiting for transfers between devices, deal(): return lax.psum_scatter(part, 'tp', scatter_dimension=0, tiled=True)  31.8 us
  transfers between devices with their start and end apart: 49, of which 27 were waited for; matrix products, arithmetic and copies ran while one was open for 30% of the time, Pallas kernels for 8%

profile of v3, /device:TPU:0, one launch (start us, length us, event | category | flops | bytes accessed | tf_op | source)
XLA Modules:
  0.0 771.8 jit_solution(8937655946322767293)
XLA Ops:
  31.8 11.6 %all-to-all-done = bf16[8,16,2048]{2,1,0:T(8,128)(2,1)} async-done(((bf16[8,16,2048]{2,1,0:T(8,128)(2,1)}), bf16[8,16,2048]{2,1,0:T(8,128)(2,1)}, u32[]{:S(2)}, u32[]{:S(2)}) %all-to-all-start) | async-done | bytes 524320 | tf_op jit(solution)/shard_map/all_to_all | solution.py:784
  110.8 17.9 %fusion.27.proj.prior = f32[768,3200]{1,0:T(8,128)} fusion(bf16[2048,3200]{1,0:T(8,128)(2,1)} %all-gather.5.cloned.1.call-done, bf16[768,2048]{1,0:T(8,128)(2,1)} %get-tuple-element.365.x_ref, f32[2048]{0:T(1024)S(1)} %bitcast.121, f32[768]{0:T(1024)S(1)} %add_rsqrt_fusion), kind=kOutput, calls=%fused_computation.66 | convolution fusion | flops 10072621056 | bytes 26094592 | tf_op jit(solution)/shard_map/dot_general | solution.py:19
  135.7 23.1 %delta_forward.1 = (bf16[768,1024]{1,0:T(8,128)(2,1)S(1)}, f32[6,4,128,256]{3,2,1,0:T(8,128)S(1)}, bf16[6,4,128,128]{3,2,1,0:T(8,128)(2,1)S(1)}, f32[768,1024]{1,0:T(8,128)}, f32[768,1024]{1,0:T(8,128)}) custom-call(f32[768,3200]{1,0:T(8,128)} %fusion.27.proj.prior, f32[768,128]{1,0:T(8,128)S(1)} %pad.37.info_ref, f32[8,768]{1,0:T(8,128)S(1)} %broadcast_in_dim.182.segr, ...), custom_call_target="tpu_custom_call" | custom-call | tf_op jit(solution)/shard_map/delta_forward/pallas_call | solution.py:401
  180.0 13.7 %collective-permute-done.6 = bf16[192,2048]{1,0:T(8,128)(2,1)} collective-permute-done((bf16[192,2048]{1,0:T(8,128)(2,1)}, bf16[192,2048]{1,0:T(8,128)(2,1)}, u32[]{:S(2)}, u32[]{:S(2)}) %collective-permute-start.6) | collective-permute-done | bytes 786464 | tf_op jit(solution)/shard_map/ppermute | solution.py:632
  193.7 16.3 %collective-permute-done.7 = bf16[192,2048]{1,0:T(8,128)(2,1)} collective-permute-done((bf16[192,2048]{1,0:T(8,128)(2,1)}, bf16[192,2048]{1,0:T(8,128)(2,1)}, u32[]{:S(2)}, u32[]{:S(2)}) %collective-permute-start.7) | collective-permute-done | bytes 786464 | tf_op jit(solution)/shard_map/ppermute | solution.py:632
  218.9 15.5 %collective-permute-done.8.after = bf16[192,2048]{1,0:T(8,128)(2,1)S(1)} collective-permute-done((bf16[192,2048]{1,0:T(8,128)(2,1)S(1)}, bf16[192,2048]{1,0:T(8,128)(2,1)S(1)}, u32[]{:S(2)}, u32[]{:S(2)}) %collective-permute-start.8) | collective-permute-done | bytes 786464 | tf_op jit(solution)/shard_map/ppermute | solution.py:632
  280.0 10.2 %collective-permute-done.12 = bf16[192,2048]{1,0:T(8,128)(2,1)} collective-permute-done((bf16[192,2048]{1,0:T(8,128)(2,1)}, bf16[192,2048]{1,0:T(8,128)(2,1)}, u32[]{:S(2)}, u32[]{:S(2)}) %collective-permute-start.12) | collective-permute-done | bytes 786464 | tf_op jit(solution)/shard_map/ppermute | solution.py:632
  290.2 13.6 %collective-permute-done.14 = bf16[192,2048]{1,0:T(8,128)(2,1)} collective-permute-done((bf16[192,2048]{1,0:T(8,128)(2,1)}, bf16[192,2048]{1,0:T(8,128)(2,1)}, u32[]{:S(2)}, u32[]{:S(2)}) %collective-permute-start.14) | collective-permute-done | bytes 786464 | tf_op jit(solution)/shard_map/ppermute | solution.py:632
  308.4 13.7 %fusion.95 = f32[768,2816]{1,0:T(8,128)S(1)} fusion(bf16[768,2048]{1,0:T(8,128)(2,1)} %pad_maximum_fusion.2, bf16[2048,2816]{1,0:T(8,128)(2,1)} %all-gather.11.cloned.1.call-done), kind=kOutput, calls=%fused_computation.279 | convolution fusion | flops 8858370048 | bytes 23330816 | tf_op jit(solution)/shard_map/dot_general | solution.py:19
  329.6 13.1 %convolution_convert_fusion.10 = bf16[768,2048]{1,0:T(8,128)(2,1)} fusion(bf16[2048,2816]{1,0:T(8,128)(2,1)} %all-gather.11.cloned.1.call-done, bf16[768,1408]{1,0:T(8,128)(2,1)S(1)} %get-tuple-element.302, bf16[768,1408]{1,0:T(8,128)(2,1)S(1)} %get-tuple-element.301), kind=kOutput, calls=%fused_computation.31 | convolution fusion | flops 8868593664 | bytes 19005440 | tf_op jit(solution)/shard_map/dot_general | solution.py:23
  351.8 9.5 %convolution_convert_fusion.9 = bf16[768,2048]{1,0:T(8,128)(2,1)} fusion(bf16[768,1408]{1,0:T(8,128)(2,1)} %get-tuple-element.142, bf16[2048,1408]{0,1:T(8,128)(2,1)} %all-gather.9.cloned.1.call-done), kind=kOutput, calls=%fused_computation.30 | convolution fusion | flops 4430757888 | bytes 11075584 | tf_op jit(solution)/shard_map/dot_general | solution.py:23
  361.2 14.7 %convolution_convert_fusion.1 = bf16[2048,2816]{1,0:T(8,128)(2,1)} fusion(bf16[768,2048]{1,0:T(8,128)(2,1)} %pad_maximum_fusion.2, bf16[768,2816]{1,0:T(8,128)(2,1)} %pad_maximum_fusion.1), kind=kOutput, calls=%fused_computation.2 | convolution fusion | flops 8864137216 | bytes 19005440 | tf_op jit(solution)/shard_map/dot_general | solution.py:27
  375.9 31.8 %reduce-scatter.6.cloned.1.call-done.moved = bf16[192,2048]{1,0:T(8,128)(2,1)} async-done(((bf16[768,2048]{1,0:T(8,128)(2,1)}), bf16[192,2048]{1,0:T(8,128)(2,1)}) %reduce-scatter.6.cloned.1.call-update) | async-done | bytes 786448 | tf_op jit(solution)/shard_map/reduce_scatter | solution.py:614
  416.8 15.5 %collective-permute-done.15 = bf16[192,2048]{1,0:T(8,128)(2,1)S(1)} collective-permute-done((bf16[192,2048]{1,0:T(8,128)(2,1)S(1)}, bf16[192,2048]{1,0:T(8,128)(2,1)S(1)}, u32[]{:S(2)}, u32[]{:S(2)}) %collective-permute-start.15) | collective-permute-done | bytes 786464 | tf_op jit(solution)/shard_map/ppermute | solution.py:632
  440.1 20.0 %collective-permute-done.17 = bf16[192,2048]{1,0:T(8,128)(2,1)S(1)} collective-permute-done((bf16[192,2048]{1,0:T(8,128)(2,1)S(1)}, bf16[192,2048]{1,0:T(8,128)(2,1)S(1)}, u32[]{:S(2)}, u32[]{:S(2)}) %collective-permute-start.17) | collective-permute-done | bytes 786464 | tf_op jit(solution)/shard_map/ppermute | solution.py:632
  460.1 14.8 %collective-permute-done.19 = bf16[192,2048]{1,0:T(8,128)(2,1)S(1)} collective-permute-done((bf16[192,2048]{1,0:T(8,128)(2,1)S(1)}, bf16[192,2048]{1,0:T(8,128)(2,1)S(1)}, u32[]{:S(2)}, u32[]{:S(2)}) %collective-permute-start.19) | collective-permute-done | bytes 786464 | tf_op jit(solution)/shard_map/ppermute | solution.py:632
  486.0 33.6 %delta_backward.1 = (bf16[768,3200]{1,0:T(8,128)(2,1)}, f32[32,2048]{1,0:T(8,128)S(1)}, f32[8,1024]{1,0:T(8,128)S(1)}, f32[16,128]{1,0:T(8,128)S(1)}) custom-call(f32[768,3200]{1,0:T(8,128)} %fusion.27.proj.prior, f32[768,3200]{1,0:T(8,128)} %fusion.27.proj.prior, f32[768,128]{1,0:T(8,128)S(1)} %pad.37.info_ref, f32[8,768]{1,0:T(8,128)S(1)} %copy-done.24, ...), custom_call_target="tpu_custom_call" | custom-call | tf_op jit(solution)/shard_map/delta_backward/pallas_call | solution.py:446
  521.5 15.3 %convolution_convert_fusion.8.own = bf16[768,2048]{1,0:T(8,128)(2,1)S(1)} fusion(bf16[768,3200]{1,0:T(8,128)(2,1)} %get-tuple-element.155, bf16[2048,3200]{1,0:T(8,128)(2,1)} %all-gather.5.cloned.1.call-done), kind=kOutput, calls=%fused_computation.29 | convolution fusion | flops 10067902464 | bytes 21168128 | tf_op jit(solution)/shard_map/dot_general | solution.py:23
  552.2 15.5 %convolution_convert_fusion = bf16[2048,3200]{1,0:T(8,128)(2,1)S(1)} fusion(bf16[768,3200]{1,0:T(8,128)(2,1)} %get-tuple-element.155, bf16[768,2048]{1,0:T(8,128)(2,1)S(1)} %copy-done.3, f32[2048]{0:T(1024)S(1)} %bitcast.122, f32[768]{0:T(1024)S(1)} %copy-done.50), kind=kOutput, calls=%fused_computation.1 | convolution fusion | flops 10079174656 | bytes 21179392 | tf_op jit(solution)/shard_map/dot_general | solution.py:27
  567.7 9.3 %pad_maximum_fusion = bf16[2048,4224]{1,0:T(8,128)(2,1)} fusion(bf16[2048,1024]{1,0:T(8,128)(2,1)} %convolution_convert_fusion.3, bf16[2048,3200]{1,0:T(8,128)(2,1)S(1)} %convolution_convert_fusion), kind=kLoop, calls=%fused_computation | loop fusion | flops 34603008 | bytes 34603008 | tf_op jit(solution)/shard_map/concatenate | solution.py:979
  595.4 12.9 %all-to-all-done.3 = bf16[8,24,2048]{2,1,0:T(8,128)(2,1)} async-done(((bf16[8,24,2048]{2,1,0:T(8,128)(2,1)}), bf16[8,24,2048]{2,1,0:T(8,128)(2,1)}, u32[]{:S(2)}, u32[]{:S(2)}) %all-to-all-start.3) | async-done | bytes 786464 | tf_op jit(solution)/shard_map/all_to_all | solution.py:784
  665.0 17.9 %collective-permute-done.29 = bf16[200,2048]{1,0:T(8,128)(2,1)} collective-permute-done((bf16[200,2048]{1,0:T(8,128)(2,1)}, bf16[200,2048]{1,0:T(8,128)(2,1)}, u32[]{:S(2)}, u32[]{:S(2)}) %collective-permute-start.29) | collective-permute-done | bytes 819232 | tf_op jit(solution)/shard_map/ppermute | solution.py:632
  706.9 30.2 %collective-permute-done.33 = bf16[200,2048]{1,0:T(8,128)(2,1)S(1)} collective-permute-done((bf16[200,2048]{1,0:T(8,128)(2,1)S(1)}, bf16[200,2048]{1,0:T(8,128)(2,1)S(1)}, u32[]{:S(2)}, u32[]{:S(2)}) %collective-permute-start.33) | collective-permute-done | bytes 819232 | tf_op jit(solution)/shard_map/ppermute | solution.py:632
  747.3 13.1 %reduce-scatter.12.cloned.1.call-done.grads = bf16[256,4224]{1,0:T(8,128)(2,1)} async-done(((bf16[2048,4224]{1,0:T(8,128)(2,1)}), bf16[256,4224]{1,0:T(8,128)(2,1)}) %reduce-scatter.12.cloned.1.call-update) | async-done | bytes 2162704 | tf_op jit(solution)/shard_map/reduce_scatter | solution.py:955
  (406 shorter events, 353.1 us)
Async XLA Ops:
  7.3 103.5 %all-gather.5.cloned.1.call-start = ((), (), s32[]{:S(2)}) async-start(), calls=%async_computation.10 | async-start | bytes 14745600 | tf_op jit(solution)/shard_map/all_gather | solution.py:813
  43.4 33.5 %all-to-all-start.1 = ((bf16[8,48,2048]{2,1,0:T(8,128)(2,1)}), bf16[8,48,2048]{2,1,0:T(8,128)(2,1)}, u32[]{:S(2)}, u32[]{:S(2)}) async-start(bf16[8,48,2048]{2,1,0:T(8,128)(2,1)} %bitcast.104), calls=%async_computation.1 | async-start | bytes 3145728 | tf_op jit(solution)/shard_map/all_to_all | solution.py:784
  47.7 116.1 %all-gather.7.cloned.1.call-start = ((), (), s32[]{:S(2)}) async-start(), calls=%async_computation.11 | async-start | bytes 4718592 | tf_op jit(solution)/shard_map/all_gather | solution.py:868
  101.0 169.8 %all-gather.9.cloned.1.call-start = ((), (), s32[]{:S(2)}) async-start(), calls=%async_computation.12 | async-start | bytes 6488064 | tf_op jit(solution)/shard_map/all_gather | solution.py:869
  101.7 206.6 %all-gather.11.cloned.1.call-start = ((), (), s32[]{:S(2)}) async-start(), calls=%async_computation.13 | async-start | bytes 12976128 | tf_op jit(solution)/shard_map/all_gather | solution.py:905
  128.7 81.3 %all-to-all-start.2 = ((bf16[8,96,2048]{2,1,0:T(8,128)(2,1)}), bf16[8,96,2048]{2,1,0:T(8,128)(2,1)}, u32[]{:S(2)}, u32[]{:S(2)}) async-start(bf16[8,96,2048]{2,1,0:T(8,128)(2,1)} %bitcast.16), calls=%async_computation.2 | async-start | bytes 6291456 | tf_op jit(solution)/shard_map/all_to_all | solution.py:784
  133.2 274.5 %reduce-scatter.6.cloned.1.call-start = ((), (), s32[]{:S(2)}) async-start(), calls=%async_computation.14 | async-start | bytes 3932160 | tf_op jit(solution)/shard_map/reduce_scatter | solution.py:614
  176.4 33.6 %collective-permute-start.7 = (bf16[192,2048]{1,0:T(8,128)(2,1)}, bf16[192,2048]{1,0:T(8,128)(2,1)}, u32[]{:S(2)}, u32[]{:S(2)}) collective-permute-start(bf16[192,2048]{1,0:T(8,128)(2,1)} %get-tuple-element.311), channel_id=1, source_target_pairs={{3,1},{0,2},{7,5},{4,6},{11,9},{8,10},{15,13},{12,14},{19,17},{16,... | collective-permute-start | bytes 2359304 | tf_op jit(solution)/shard_map/ppermute | solution.py:632
  269.4 34.4 %collective-permute-start.14 = (bf16[192,2048]{1,0:T(8,128)(2,1)}, bf16[192,2048]{1,0:T(8,128)(2,1)}, u32[]{:S(2)}, u32[]{:S(2)}) collective-permute-start(bf16[192,2048]{1,0:T(8,128)(2,1)} %collective-permute-done.11), channel_id=1, source_target_pairs={{2,1},{1,0},{6,5},{5,4},{10,9},{9,8},{14,13},{13,12},{18,17},{17,1... | collective-permute-start | bytes 2359304 | tf_op jit(solution)/shard_map/ppermute | solution.py:632
  342.8 134.3 %reduce-scatter.8.cloned.1.call-start = ((), (), s32[]{:S(2)}) async-start(), calls=%async_computation.15 | async-start | bytes 6488064 | tf_op jit(solution)/shard_map/reduce_scatter | solution.py:955
  407.7 129.1 %reduce-scatter.10.cloned.1.call-start = ((), (), s32[]{:S(2)}) async-start(), calls=%async_computation.16 | async-start | bytes 3932160 | tf_op jit(solution)/shard_map/reduce_scatter | solution.py:614
  438.8 36.1 %collective-permute-start.19 = (bf16[192,2048]{1,0:T(8,128)(2,1)S(1)}, bf16[192,2048]{1,0:T(8,128)(2,1)S(1)}, u32[]{:S(2)}, u32[]{:S(2)}) collective-permute-start(bf16[192,2048]{1,0:T(8,128)(2,1)S(1)} %collective-permute-done.16), channel_id=1, source_target_pairs={{2,1},{1,0},{6,5},{5,4},{10,9},{9,8},{14,13},{13,12},{18,17},{17,1... | collective-permute-start | bytes 2359304 | tf_op jit(solution)/shard_map/ppermute | solution.py:632
  477.2 267.0 %reduce-scatter.14.cloned.1.call-start = ((), (), s32[]{:S(2)}) async-start(), calls=%async_computation.18 | async-start | bytes 12976128 | tf_op jit(solution)/shard_map/reduce_scatter | solution.py:955
  536.8 223.5 %reduce-scatter.12.cloned.1.call-start = ((), (), s32[]{:S(2)}) async-start(), calls=%async_computation.17 | async-start | bytes 19464192 | tf_op jit(solution)/shard_map/reduce_scatter | solution.py:955
  538.4 38.6 %collective-permute-start.20 = (bf16[192,2048]{1,0:T(8,128)(2,1)}, bf16[192,2048]{1,0:T(8,128)(2,1)}, u32[]{:S(2)}, u32[]{:S(2)}) collective-permute-start(bf16[192,2048]{1,0:T(8,128)(2,1)} %get-tuple-element.310), channel_id=1, source_target_pairs={{2,1},{3,2},{6,5},{7,6},{10,9},{11,10},{14,13},{15,14},{18,17},{19... | collective-permute-start | bytes 2359304 | tf_op jit(solution)/shard_map/ppermute | solution.py:632
  540.1 36.9 %collective-permute-start.21 = (bf16[192,2048]{1,0:T(8,128)(2,1)}, bf16[192,2048]{1,0:T(8,128)(2,1)}, u32[]{:S(2)}, u32[]{:S(2)}) collective-permute-start(bf16[192,2048]{1,0:T(8,128)(2,1)} %get-tuple-element.309), channel_id=1, source_target_pairs={{1,2},{0,1},{5,6},{4,5},{9,10},{8,9},{13,14},{12,13},{17,18},{16,1... | collective-permute-start | bytes 2359304 | tf_op jit(solution)/shard_map/ppermute | solution.py:632
  543.2 33.8 %collective-permute-start.22 = (bf16[192,2048]{1,0:T(8,128)(2,1)}, bf16[192,2048]{1,0:T(8,128)(2,1)}, u32[]{:S(2)}, u32[]{:S(2)}) collective-permute-start(bf16[192,2048]{1,0:T(8,128)(2,1)} %get-tuple-element.308), channel_id=1, source_target_pairs={{3,1},{0,2},{7,5},{4,6},{11,9},{8,10},{15,13},{12,14},{19,17},{16,... | collective-permute-start | bytes 2359304 | tf_op jit(solution)/shard_map/ppermute | solution.py:632
  587.5 28.5 %collective-permute-start.25 = (bf16[192,2048]{1,0:T(8,128)(2,1)}, bf16[192,2048]{1,0:T(8,128)(2,1)}, u32[]{:S(2)}, u32[]{:S(2)}) collective-permute-start(bf16[192,2048]{1,0:T(8,128)(2,1)} %get-tuple-element.305), channel_id=1, source_target_pairs={{1,0},{2,1},{3,2},{5,4},{6,5},{7,6},{9,8},{10,9},{11,10},{13,12},{... | collective-permute-start | bytes 2359304 | tf_op jit(solution)/shard_map/ppermute | solution.py:632
  588.8 27.3 %collective-permute-start.26 = (bf16[192,2048]{1,0:T(8,128)(2,1)}, bf16[192,2048]{1,0:T(8,128)(2,1)}, u32[]{:S(2)}, u32[]{:S(2)}) collective-permute-start(bf16[192,2048]{1,0:T(8,128)(2,1)} %get-tuple-element.304), channel_id=1, source_target_pairs={{0,1},{1,2},{2,3},{4,5},{5,6},{6,7},{8,9},{9,10},{10,11},{12,13},{... | collective-permute-start | bytes 2359304 | tf_op jit(solution)/shard_map/ppermute | solution.py:632
  644.7 38.2 %collective-permute-start.29 = (bf16[200,2048]{1,0:T(8,128)(2,1)}, bf16[200,2048]{1,0:T(8,128)(2,1)}, u32[]{:S(2)}, u32[]{:S(2)}) collective-permute-start(bf16[200,2048]{1,0:T(8,128)(2,1)} %get-tuple-element.326), channel_id=1, source_target_pairs={{1,3},{2,0},{5,7},{6,4},{9,11},{10,8},{13,15},{14,12},{17,19},{18,... | collective-permute-start | bytes 2457608 | tf_op jit(solution)/shard_map/ppermute | solution.py:632
  649.6 39.9 %collective-permute-start.30 = (bf16[200,2048]{1,0:T(8,128)(2,1)S(1)}, bf16[200,2048]{1,0:T(8,128)(2,1)S(1)}, u32[]{:S(2)}, u32[]{:S(2)}) collective-permute-start(bf16[200,2048]{1,0:T(8,128)(2,1)S(1)} %pad_maximum_fusion.5), channel_id=1, source_target_pairs={{0,1},{1,2},{2,3},{4,5},{5,6},{6,7},{8,9},{9,10},{10,11},{12,13},{... | collective-permute-start | bytes 2457608 | tf_op jit(solution)/shard_map/ppermute | solution.py:632
  657.1 39.9 %collective-permute-start.31 = (bf16[200,2048]{1,0:T(8,128)(2,1)S(1)}, bf16[200,2048]{1,0:T(8,128)(2,1)S(1)}, u32[]{:S(2)}, u32[]{:S(2)}) collective-permute-start(bf16[200,2048]{1,0:T(8,128)(2,1)S(1)} %pad_maximum_fusion.5), channel_id=1, source_target_pairs={{1,0},{2,1},{3,2},{5,4},{6,5},{7,6},{9,8},{10,9},{11,10},{13,12},{... | collective-permute-start | bytes 2457608 | tf_op jit(solution)/shard_map/ppermute | solution.py:632
  697.3 39.8 %collective-permute-start.34 = (bf16[200,2048]{1,0:T(8,128)(2,1)S(1)}, bf16[200,2048]{1,0:T(8,128)(2,1)S(1)}, u32[]{:S(2)}, u32[]{:S(2)}) collective-permute-start(bf16[200,2048]{1,0:T(8,128)(2,1)S(1)} %get-tuple-element.324), channel_id=1, source_target_pairs={{1,3},{2,0},{5,7},{6,4},{9,11},{10,8},{13,15},{14,12},{17,19},{18,... | collective-permute-start | bytes 2457608 | tf_op jit(solution)/shard_map/ppermute | solution.py:632
  699.3 37.7 %collective-permute-start.33 = (bf16[200,2048]{1,0:T(8,128)(2,1)S(1)}, bf16[200,2048]{1,0:T(8,128)(2,1)S(1)}, u32[]{:S(2)}, u32[]{:S(2)}) collective-permute-start(bf16[200,2048]{1,0:T(8,128)(2,1)S(1)} %collective-permute-done.31), channel_id=1, source_target_pairs={{2,1},{1,0},{6,5},{5,4},{10,9},{9,8},{14,13},{13,12},{18,17},{17,1... | collective-permute-start | bytes 2457608 | tf_op jit(solution)/shard_map/ppermute | solution.py:632
  (81 other events, 1145.8 us)
Sparse Core Ops, SparseCore 0:
  13.1 91.9 all-gather.4
  107.0 44.3 all-gather.6
  153.2 63.3 all-gather.8
  219.0 67.6 all-gather.10
  342.9 64.7 reduce-scatter.5
  411.0 59.0 reduce-scatter.7
  477.3 58.3 reduce-scatter.9
  539.6 95.2 reduce-scatter.13
  639.0 121.3 reduce-scatter.11

commit v4 on v3

--- a/solution.py
+++ b/solution.py
@@ -173,8 +173,8 @@
         tail = jnp.exp(last - cum) * tail_mask
         keep = carried[rows - 1 : rows, :]
         before = state[head]
-        state_out[0, head] = before
         sb = before.astype(BF16)
+        state_out[0, head] = sb
         target = values - carried * dot_nn(kb, sb)
         ib = inverse.astype(BF16)
         pseudo = dot_nn(ib, target.astype(BF16))
@@ -279,8 +279,8 @@
         tail = jnp.exp(cum[rows - 1 : rows, :] - cum) * tail_mask
         keep = carried[rows - 1 : rows, :]
         yield
-        before = state_in[0, head]
-        sb = before.astype(BF16)
+        sb = state_in[0, head]
+        before = sb.astype(F32)
         ib = inverse_in[0, head]
         pseudo = pseudo_in[:, head * vs : (head + 1) * vs]
         output = output_in[:, head * vs : (head + 1) * vs]
@@ -418,7 +418,7 @@
         ],
         out_shape=[
             jax.ShapeDtypeStruct((total, span), BF16),
-            jax.ShapeDtypeStruct((steps, head_count, key_size, value_size), F32),
+            jax.ShapeDtypeStruct((steps, head_count, key_size, value_size), BF16),
             jax.ShapeDtypeStruct((steps, head_count, CHUNK, CHUNK), BF16),
             jax.ShapeDtypeStruct((total, span), F32),
             jax.ShapeDtypeStruct((total, span), F32),
@@ -550,26 +550,42 @@
 
 
 def widen_kernel(grads, *outs):
-    *direct, turned, out_turned = outs
+    *direct, turned = outs
     start = 0
     for out in direct:
         stop = start + out.shape[1]
         out[...] = grads[:, start:stop].astype(F32)
         start = stop
     turned[...] = jnp.transpose(grads[:, start : start + LANES].astype(F32))
-    out_turned[...] = jnp.transpose(grads[:, start + LANES :].astype(F32))
 
 
 def widened(grads, columns):
     own, total = grads.shape
-    shapes = [(own, count) for count in columns]
-    shapes += [(LANES, own), (total - sum(columns) - LANES, own)]
+    shapes = [(own, count) for count in columns] + [(LANES, own)]
     return pl.pallas_call(
         widen_kernel,
         out_shape=[jax.ShapeDtypeStruct(shape, F32) for shape in shapes],
         compiler_params=pltpu.CompilerParams(vmem_limit_bytes=40 * 1024 * 1024),
         name="widen",
     )(grads)
+
+
+def sum_turn_kernel(parts, out):
+    out[...] = jnp.transpose(jnp.sum(parts[...].astype(F32), axis=0))
+
+
+def summed_turned(parts):
+    count, own, columns = parts.shape
+    tile = 2 * LANES
+    return pl.pallas_call(
+        sum_turn_kernel,
+        grid=(columns // tile,),
+        in_specs=[pl.BlockSpec((count, own, tile), lambda i: (0, 0, i))],
+        out_specs=pl.BlockSpec((tile, own), lambda i: (i, 0)),
+        out_shape=jax.ShapeDtypeStruct((columns, own), F32),
+        compiler_params=pltpu.CompilerParams(vmem_limit_bytes=40 * 1024 * 1024),
+        name="sum_turn",
+    )(parts)
 
 
 def place_arrays(length_row, total):
@@ -970,19 +986,20 @@
     )
     first_part = dot_nt(grad_proj, mixer_weight).astype(BF16)
     result_moved = deal(ffn_part, "y")
-    first_part, proj_late, mix_late, normed_late, result_moved, grad_pair_part = together(
-        (first_part, grad_proj, mix_low, normed_low, result_moved, grad_pair_part)
+    grad_out_moved = exchange(dot_tn(mix_low, normed_low).astype(BF16))
+    first_part, proj_late, result_moved, grad_pair_part, grad_out_moved = together(
+        (first_part, grad_proj, result_moved, grad_pair_part, grad_out_moved)
     )
     grad_pair = owners(grad_pair_part)
-    grad_out_part = dot_tn(mix_late, normed_late).astype(BF16)
     grad_mixer_part = dot_tn(normed_in, proj_late).astype(BF16)
-    grad_mixer_part = jnp.concatenate([grad_mixer_part, grad_out_part], axis=1)
-    *first_came, grad_mixer_part = together((*sum_first(first_part, rows), grad_mixer_part))
+    result = (hidden_in + add_dealt(result_moved, "y")).astype(BF16)
+    result_back = exchange(to_sources(result)).reshape(rows, width)
+    *first_came, grad_mixer_part, result_back = together(
+        (*sum_first(first_part, rows), grad_mixer_part, result_back)
+    )
     first_middle = sum_middle(first_part, rows, first_came)
     late_after, late_before = sum_second(*first_middle)
-    result_moved = together((result_moved, *first_middle))[0]
-    result = (hidden_in + add_dealt(result_moved, "y")).astype(BF16)
-    result_back = exchange(to_sources(result)).reshape(rows, width)
+    result_back = together((result_back, *first_middle))[0]
     result_back = jnp.pad(result_back, ((0, PAD), (0, 0)))
     result_near = relay_first(result_back)
 
@@ -1025,7 +1042,10 @@
     extra = jnp.pad(pair_rows(packed), ((0, 0), (0, PAD - 2), (0, 0)))
     grad_sent = to_sources(token_grad)
     came = exchange(jnp.concatenate([grad_sent, extra], axis=1))
-    before, after, grad_down = together((*result_near, grad_down, grad_sent))[:3]
+    before, after, grad_down, grad_out_moved = together(
+        (*result_near, grad_down, grad_out_moved, grad_sent)
+    )[:4]
+    grad_out = summed_turned(grad_out_moved.reshape(groups, own, -1))
     result_far = relay_second(before, after)
     summed = jnp.sum(came[:, share : share + 2].astype(F32), axis=(0, 1))
     block = jnp.concatenate(
@@ -1035,14 +1055,19 @@
         ],
         axis=0,
     )
-    result_far = together((*result_far, block))[:3]
+    token_near = relay_first(block)
+    result_far = together((*result_far, *token_near))[:3]
     mixed, unused = to_given((result_back, before, after, *result_far))
-    grad_tokens, full = to_given(relayed_blocks(block))
-    *mixer_grads, gates_turned, grad_out = widened(
+    grad_gate = grad_pair[:, :units].astype(F32)
+    grad_up = grad_pair[:, units:].astype(F32)
+    *token_blocks, grad_gate, grad_up = together(
+        (block, *token_near, *relay_second(*token_near), grad_gate, grad_up)
+    )
+    grad_tokens, full = to_given(token_blocks)
+    *mixer_grads, gates_turned = widened(
         owners(grad_mixer_part), [key_cols, key_cols, value_cols, value_cols]
     )
     mixer_grads += [gates_turned[:heads].T, gates_turned[heads : 2 * heads].T]
-    grad_pair = grad_pair.astype(F32)
     grad_down = grad_down.astype(F32).T
 
     tp_summed = jnp.sum(
@@ -1068,8 +1093,8 @@
         pieces[2],
         grad_out,
         pieces[1],
-        grad_pair[:, :units],
-        grad_pair[:, units:],
+        grad_gate,
+        grad_up,
         grad_down,
     )
 

time: 781 us -> 767 us (0.982)
  waiting for transfers between devices: 300 us -> 275 us
  starting transfers between devices: 103 us -> 113 us
    reduce_scatter x3, waiting for transfers between devices: 13.1 us -> 0.01 us  [owners(): return lax.psum_scatter(value, GROUP, scatter_dimension=0, tiled=True)]
    all_to_all x5 -> x6, waiting for transfers between devices: 27 us -> 14.5 us  [exchange(): return lax.all_to_all(sent, GROUP, split_axis=0, concat_axis=0, tiled=True)]
    concatenate x1 -> x0, other arithmetic: 9.34 us -> none  [per_device(): grad_mixer_part = jnp.concatenate([grad_mixer_part, grad_out_part], axis=1)]
    all_to_all x5 -> x6, starting transfers between devices: 21.8 us -> 26.6 us  [exchange(): return lax.all_to_all(sent, GROUP, split_axis=0, concat_axis=0, tiled=True)]
    unnamed x137 -> x136, local copies, waits for them, and re-layouts: 34.8 us -> 36.8 us
  transfers between devices with their start and end apart: 49 -> 50, of which waited for: 27 -> 27; matrix products, arithmetic and copies ran while one was open for 30% -> 30% of each run, Pallas kernels for 8% -> 9%
where the time goes in v4:
time: 767 us; the launch traced here: 758 us
  waiting for transfers between devices  275 us (36%)
  matrix products  174 us (23%)
  starting transfers between devices  113 us (15%)
  Pallas kernels  69.6 us (9%)
  local copies, waits for them, and re-layouts  63 us (8%)
  other arithmetic  48 us (6%)
  between operations  15.6 us (2%)
    ppermute x35, waiting for transfers between devices, relay_send(): return lax.ppermute(value, 'tp', route)  226 us
    ppermute x35, starting transfers between devices, relay_send(): return lax.ppermute(value, 'tp', route)  85 us
    dot_general x4, matrix products, dot_nn(): lax.dot_general(left, right, (((1,), (0,)), ((), ())), preferred_element_...  49.3 us
    dot_general x4, matrix products, dot_tn(): lax.dot_general(left, right, (((0,), (0,)), ((), ())), preferred_element_...  47.6 us
    dot_general x4, matrix products, dot_nt(): lax.dot_general(left, right, (((1,), (1,)), ((), ())), preferred_element_...  40.9 us
    unnamed x136, local copies, waits for them, and re-layouts  36.8 us
    pallas_call x1, Pallas kernels, delta_backward(): pl.pallas_call(functools.partial(backward_kernel, head_count, key_size, v...  33.8 us
    reduce_scatter x2, waiting for transfers between devices, deal(): return lax.psum_scatter(part, 'tp', scatter_dimension=0, tiled=True)  32.9 us
  transfers between devices with their start and end apart: 50, of which 27 were waited for; matrix products, arithmetic and copies ran while one was open for 30% of the time, Pallas kernels for 9%

profile of v4, /device:TPU:0, one launch (start us, length us, event | category | flops | bytes accessed | tf_op | source)
XLA Modules:
  0.0 757.5 jit_solution(13118867276386602548)
XLA Ops:
  31.8 11.6 %all-to-all-done = bf16[8,16,2048]{2,1,0:T(8,128)(2,1)} async-done(((bf16[8,16,2048]{2,1,0:T(8,128)(2,1)}), bf16[8,16,2048]{2,1,0:T(8,128)(2,1)}, u32[]{:S(2)}, u32[]{:S(2)}) %all-to-all-start) | async-done | bytes 524320 | tf_op jit(solution)/shard_map/all_to_all | solution.py:800
  110.7 17.9 %fusion.27.proj.prior = f32[768,3200]{1,0:T(8,128)} fusion(bf16[2048,3200]{1,0:T(8,128)(2,1)} %all-gather.5.cloned.1.call-done, bf16[768,2048]{1,0:T(8,128)(2,1)} %get-tuple-element.377.x_ref, f32[2048]{0:T(1024)S(1)} %bitcast.124, f32[768]{0:T(1024)S(1)} %add_rsqrt_fusion), kind=kOutput, calls=%fused_computation.65 | convolution fusion | flops 10072621056 | bytes 26094592 | tf_op jit(solution)/shard_map/dot_general | solution.py:19
  135.6 23.0 %delta_forward.1 = (bf16[768,1024]{1,0:T(8,128)(2,1)S(1)}, bf16[6,4,128,256]{3,2,1,0:T(8,128)(2,1)S(1)}, bf16[6,4,128,128]{3,2,1,0:T(8,128)(2,1)S(1)}, f32[768,1024]{1,0:T(8,128)}, f32[768,1024]{1,0:T(8,128)}) custom-call(f32[768,3200]{1,0:T(8,128)} %fusion.27.proj.prior, f32[768,128]{1,0:T(8,128)S(1)} %pad.37.info_ref, ...), custom_call_target="tpu_custom_call" | custom-call | tf_op jit(solution)/shard_map/delta_forward/pallas_call | solution.py:401
  179.8 13.4 %collective-permute-done.6 = bf16[192,2048]{1,0:T(8,128)(2,1)} collective-permute-done((bf16[192,2048]{1,0:T(8,128)(2,1)}, bf16[192,2048]{1,0:T(8,128)(2,1)}, u32[]{:S(2)}, u32[]{:S(2)}) %collective-permute-start.6) | collective-permute-done | bytes 786464 | tf_op jit(solution)/shard_map/ppermute | solution.py:648
  193.2 16.3 %collective-permute-done.7 = bf16[192,2048]{1,0:T(8,128)(2,1)} collective-permute-done((bf16[192,2048]{1,0:T(8,128)(2,1)}, bf16[192,2048]{1,0:T(8,128)(2,1)}, u32[]{:S(2)}, u32[]{:S(2)}) %collective-permute-start.7) | collective-permute-done | bytes 786464 | tf_op jit(solution)/shard_map/ppermute | solution.py:648
  218.4 15.5 %collective-permute-done.8.after = bf16[192,2048]{1,0:T(8,128)(2,1)S(1)} collective-permute-done((bf16[192,2048]{1,0:T(8,128)(2,1)S(1)}, bf16[192,2048]{1,0:T(8,128)(2,1)S(1)}, u32[]{:S(2)}, u32[]{:S(2)}) %collective-permute-start.8) | collective-permute-done | bytes 786464 | tf_op jit(solution)/shard_map/ppermute | solution.py:648
  249.9 9.2 %collective-permute-done.10 = bf16[192,2048]{1,0:T(8,128)(2,1)} collective-permute-done((bf16[192,2048]{1,0:T(8,128)(2,1)}, bf16[192,2048]{1,0:T(8,128)(2,1)}, u32[]{:S(2)}, u32[]{:S(2)}) %collective-permute-start.10) | collective-permute-done | bytes 786464 | tf_op jit(solution)/shard_map/ppermute | solution.py:648
  270.4 9.3 %fusion.93 = f32[768,1408]{1,0:T(8,128)} fusion(bf16[768,2048]{1,0:T(8,128)(2,1)S(1)} %convolution_convert_fusion.5.dy_ref, bf16[2048,1408]{0,1:T(8,128)(2,1)} %all-gather.9.cloned.1.call-done), kind=kOutput, calls=%fused_computation.277 | convolution fusion | flops 4429185024 | bytes 13238272 | tf_op jit(solution)/shard_map/dot_general | solution.py:19
  279.6 10.2 %collective-permute-done.12 = bf16[192,2048]{1,0:T(8,128)(2,1)} collective-permute-done((bf16[192,2048]{1,0:T(8,128)(2,1)}, bf16[192,2048]{1,0:T(8,128)(2,1)}, u32[]{:S(2)}, u32[]{:S(2)}) %collective-permute-start.12) | collective-permute-done | bytes 786464 | tf_op jit(solution)/shard_map/ppermute | solution.py:648
  289.8 13.6 %collective-permute-done.14 = bf16[192,2048]{1,0:T(8,128)(2,1)} collective-permute-done((bf16[192,2048]{1,0:T(8,128)(2,1)}, bf16[192,2048]{1,0:T(8,128)(2,1)}, u32[]{:S(2)}, u32[]{:S(2)}) %collective-permute-start.14) | collective-permute-done | bytes 786464 | tf_op jit(solution)/shard_map/ppermute | solution.py:648
  308.1 13.7 %fusion.94 = f32[768,2816]{1,0:T(8,128)S(1)} fusion(bf16[768,2048]{1,0:T(8,128)(2,1)} %pad_maximum_fusion.1, bf16[2048,2816]{1,0:T(8,128)(2,1)} %all-gather.11.cloned.1.call-done), kind=kOutput, calls=%fused_computation.278 | convolution fusion | flops 8858370048 | bytes 23330816 | tf_op jit(solution)/shard_map/dot_general | solution.py:19
  329.3 13.2 %convolution_convert_fusion.10 = bf16[768,2048]{1,0:T(8,128)(2,1)} fusion(bf16[2048,2816]{1,0:T(8,128)(2,1)} %all-gather.11.cloned.1.call-done, bf16[768,1408]{1,0:T(8,128)(2,1)S(1)} %get-tuple-element.318, bf16[768,1408]{1,0:T(8,128)(2,1)S(1)} %get-tuple-element.317), kind=kOutput, calls=%fused_computation.30 | convolution fusion | flops 8868593664 | bytes 19005440 | tf_op jit(solution)/shard_map/dot_general | solution.py:23
  360.3 14.7 %convolution_convert_fusion.1 = bf16[2048,2816]{1,0:T(8,128)(2,1)} fusion(bf16[768,2048]{1,0:T(8,128)(2,1)} %pad_maximum_fusion.1, bf16[768,2816]{1,0:T(8,128)(2,1)} %pad_maximum_fusion), kind=kOutput, calls=%fused_computation.1 | convolution fusion | flops 8864137216 | bytes 19005440 | tf_op jit(solution)/shard_map/dot_general | solution.py:27
  375.0 32.9 %reduce-scatter.6.cloned.1.call-done.moved = bf16[192,2048]{1,0:T(8,128)(2,1)} async-done(((bf16[768,2048]{1,0:T(8,128)(2,1)}), bf16[192,2048]{1,0:T(8,128)(2,1)}) %reduce-scatter.6.cloned.1.call-update) | async-done | bytes 786448 | tf_op jit(solution)/shard_map/reduce_scatter | solution.py:630
  417.0 15.5 %collective-permute-done.15 = bf16[192,2048]{1,0:T(8,128)(2,1)S(1)} collective-permute-done((bf16[192,2048]{1,0:T(8,128)(2,1)S(1)}, bf16[192,2048]{1,0:T(8,128)(2,1)S(1)}, u32[]{:S(2)}, u32[]{:S(2)}) %collective-permute-start.15) | collective-permute-done | bytes 786464 | tf_op jit(solution)/shard_map/ppermute | solution.py:648
  440.3 20.0 %collective-permute-done.17 = bf16[192,2048]{1,0:T(8,128)(2,1)S(1)} collective-permute-done((bf16[192,2048]{1,0:T(8,128)(2,1)S(1)}, bf16[192,2048]{1,0:T(8,128)(2,1)S(1)}, u32[]{:S(2)}, u32[]{:S(2)}) %collective-permute-start.17) | collective-permute-done | bytes 786464 | tf_op jit(solution)/shard_map/ppermute | solution.py:648
  460.3 14.7 %collective-permute-done.19 = bf16[192,2048]{1,0:T(8,128)(2,1)S(1)} collective-permute-done((bf16[192,2048]{1,0:T(8,128)(2,1)S(1)}, bf16[192,2048]{1,0:T(8,128)(2,1)S(1)}, u32[]{:S(2)}, u32[]{:S(2)}) %collective-permute-start.19) | collective-permute-done | bytes 786464 | tf_op jit(solution)/shard_map/ppermute | solution.py:648
  497.8 33.8 %delta_backward.1 = (bf16[768,3200]{1,0:T(8,128)(2,1)}, f32[32,2048]{1,0:T(8,128)S(1)}, f32[8,1024]{1,0:T(8,128)S(1)}, f32[16,128]{1,0:T(8,128)S(1)}) custom-call(f32[768,3200]{1,0:T(8,128)} %fusion.27.proj.prior, f32[768,3200]{1,0:T(8,128)} %fusion.27.proj.prior, f32[768,128]{1,0:T(8,128)S(1)} %pad.37.info_ref, f32[8,768]{1,0:T(8,128)S(1)} %copy-done.23, ...), custom_call_target="tpu_custom_call" | custom-call | tf_op jit(solution)/shard_map/delta_backward/pallas_call | solution.py:446
  533.5 12.6 %convolution_convert_fusion.8.own = bf16[768,2048]{1,0:T(8,128)(2,1)S(1)} fusion(bf16[768,3200]{1,0:T(8,128)(2,1)} %get-tuple-element.162, bf16[2048,3200]{1,0:T(8,128)(2,1)S(1)} %bitcast.133), kind=kOutput, calls=%fused_computation.28 | convolution fusion | flops 10067902464 | bytes 21168128 | tf_op jit(solution)/shard_map/dot_general | solution.py:23
  562.8 17.3 %convolution_convert_fusion = bf16[2048,3200]{1,0:T(8,128)(2,1)} fusion(bf16[768,3200]{1,0:T(8,128)(2,1)} %get-tuple-element.162, bf16[768,2048]{1,0:T(8,128)(2,1)} %get-tuple-element.377.x_ref, f32[2048]{0:T(1024)S(1)} %bitcast.125, f32[768]{0:T(1024)S(1)} %copy-done.45), kind=kOutput, calls=%fused_computation | convolution fusion | flops 10079174656 | bytes 21179392 | tf_op jit(solution)/shard_map/dot_general | solution.py:27
  644.5 10.7 %collective-permute-start.30 = (bf16[200,2048]{1,0:T(8,128)(2,1)S(1)}, bf16[200,2048]{1,0:T(8,128)(2,1)S(1)}, u32[]{:S(2)}, u32[]{:S(2)}) collective-permute-start(bf16[200,2048]{1,0:T(8,128)(2,1)S(1)} %pad_maximum_fusion.4), channel_id=1, source_target_pairs={{0,1},{1,2},{2,3},{4,5},{5,6},{6,7},{8,9},{9,10},{10,11},{12,13},{... | collective-permute-start | bytes 2457608 | tf_op jit(solution)/shard_map/ppermute | solution.py:648
  662.1 16.6 %collective-permute-done.29 = bf16[200,2048]{1,0:T(8,128)(2,1)} collective-permute-done((bf16[200,2048]{1,0:T(8,128)(2,1)}, bf16[200,2048]{1,0:T(8,128)(2,1)}, u32[]{:S(2)}, u32[]{:S(2)}) %collective-permute-start.29) | collective-permute-done | bytes 819232 | tf_op jit(solution)/shard_map/ppermute | solution.py:648
  678.7 15.3 %collective-permute-done.31 = bf16[200,2048]{1,0:T(8,128)(2,1)} collective-permute-done((bf16[200,2048]{1,0:T(8,128)(2,1)S(1)}, bf16[200,2048]{1,0:T(8,128)(2,1)}, u32[]{:S(2)}, u32[]{:S(2)}) %collective-permute-start.31) | collective-permute-done | bytes 819232 | tf_op jit(solution)/shard_map/ppermute | solution.py:648
  717.9 18.2 %collective-permute-done.33 = bf16[200,2048]{1,0:T(8,128)(2,1)} collective-permute-done((bf16[200,2048]{1,0:T(8,128)(2,1)}, bf16[200,2048]{1,0:T(8,128)(2,1)}, u32[]{:S(2)}, u32[]{:S(2)}) %collective-permute-start.33) | collective-permute-done | bytes 819232 | tf_op jit(solution)/shard_map/ppermute | solution.py:648
  (408 shorter events, 352.6 us)
Async XLA Ops:
  7.3 103.4 %all-gather.5.cloned.1.call-start = ((), (), s32[]{:S(2)}) async-start(), calls=%async_computation.11 | async-start | bytes 14745600 | tf_op jit(solution)/shard_map/all_gather | solution.py:829
  43.4 33.5 %all-to-all-start.1 = ((bf16[8,48,2048]{2,1,0:T(8,128)(2,1)}), bf16[8,48,2048]{2,1,0:T(8,128)(2,1)}, u32[]{:S(2)}, u32[]{:S(2)}) async-start(bf16[8,48,2048]{2,1,0:T(8,128)(2,1)} %bitcast.105), calls=%async_computation.1 | async-start | bytes 3145728 | tf_op jit(solution)/shard_map/all_to_all | solution.py:800
  47.7 114.3 %all-gather.7.cloned.1.call-start = ((), (), s32[]{:S(2)}) async-start(), calls=%async_computation.12 | async-start | bytes 4718592 | tf_op jit(solution)/shard_map/all_gather | solution.py:884
  100.9 169.5 %all-gather.9.cloned.1.call-start = ((), (), s32[]{:S(2)}) async-start(), calls=%async_computation.13 | async-start | bytes 6488064 | tf_op jit(solution)/shard_map/all_gather | solution.py:885
  101.6 206.5 %all-gather.11.cloned.1.call-start = ((), (), s32[]{:S(2)}) async-start(), calls=%async_computation.14 | async-start | bytes 12976128 | tf_op jit(solution)/shard_map/all_gather | solution.py:921
  128.6 80.9 %all-to-all-start.2 = ((bf16[8,96,2048]{2,1,0:T(8,128)(2,1)}), bf16[8,96,2048]{2,1,0:T(8,128)(2,1)}, u32[]{:S(2)}, u32[]{:S(2)}) async-start(bf16[8,96,2048]{2,1,0:T(8,128)(2,1)} %bitcast.15), calls=%async_computation.2 | async-start | bytes 6291456 | tf_op jit(solution)/shard_map/all_to_all | solution.py:800
  133.1 274.8 %reduce-scatter.6.cloned.1.call-start = ((), (), s32[]{:S(2)}) async-start(), calls=%async_computation.15 | async-start | bytes 3932160 | tf_op jit(solution)/shard_map/reduce_scatter | solution.py:630
  175.9 33.6 %collective-permute-start.7 = (bf16[192,2048]{1,0:T(8,128)(2,1)}, bf16[192,2048]{1,0:T(8,128)(2,1)}, u32[]{:S(2)}, u32[]{:S(2)}) collective-permute-start(bf16[192,2048]{1,0:T(8,128)(2,1)} %get-tuple-element.327), channel_id=1, source_target_pairs={{3,1},{0,2},{7,5},{4,6},{11,9},{8,10},{15,13},{12,14},{19,17},{16,... | collective-permute-start | bytes 2359304 | tf_op jit(solution)/shard_map/ppermute | solution.py:648
  269.1 34.4 %collective-permute-start.14 = (bf16[192,2048]{1,0:T(8,128)(2,1)}, bf16[192,2048]{1,0:T(8,128)(2,1)}, u32[]{:S(2)}, u32[]{:S(2)}) collective-permute-start(bf16[192,2048]{1,0:T(8,128)(2,1)} %collective-permute-done.11), channel_id=1, source_target_pairs={{2,1},{1,0},{6,5},{5,4},{10,9},{9,8},{14,13},{13,12},{18,17},{17,1... | collective-permute-start | bytes 2359304 | tf_op jit(solution)/shard_map/ppermute | solution.py:648
  342.5 134.7 %reduce-scatter.8.cloned.1.call-start = ((), (), s32[]{:S(2)}) async-start(), calls=%async_computation.16 | async-start | bytes 6488064 | tf_op jit(solution)/shard_map/reduce_scatter | solution.py:971
  407.9 138.3 %reduce-scatter.10.cloned.1.call-start = ((), (), s32[]{:S(2)}) async-start(), calls=%async_computation.17 | async-start | bytes 3932160 | tf_op jit(solution)/shard_map/reduce_scatter | solution.py:630
  439.0 36.0 %collective-permute-start.19 = (bf16[192,2048]{1,0:T(8,128)(2,1)S(1)}, bf16[192,2048]{1,0:T(8,128)(2,1)S(1)}, u32[]{:S(2)}, u32[]{:S(2)}) collective-permute-start(bf16[192,2048]{1,0:T(8,128)(2,1)S(1)} %collective-permute-done.16), channel_id=1, source_target_pairs={{2,1},{1,0},{6,5},{5,4},{10,9},{9,8},{14,13},{13,12},{18,17},{17,1... | collective-permute-start | bytes 2359304 | tf_op jit(solution)/shard_map/ppermute | solution.py:648
  484.4 61.8 %all-to-all-start.3 = ((bf16[8,256,1024]{2,1,0:T(8,128)(2,1)}), bf16[8,256,1024]{2,1,0:T(8,128)(2,1)}, u32[]{:S(2)}, u32[]{:S(2)}) async-start(bf16[8,256,1024]{2,1,0:T(8,128)(2,1)} %bitcast.106), calls=%async_computation.6 | async-start | bytes 8388608 | tf_op jit(solution)/shard_map/all_to_all | solution.py:800
  489.0 225.8 %reduce-scatter.12.cloned.1.call-start = ((), (), s32[]{:S(2)}) async-start(), calls=%async_computation.18 | async-start | bytes 12976128 | tf_op jit(solution)/shard_map/reduce_scatter | solution.py:971
  548.6 31.5 %collective-permute-start.20 = (bf16[192,2048]{1,0:T(8,128)(2,1)}, bf16[192,2048]{1,0:T(8,128)(2,1)}, u32[]{:S(2)}, u32[]{:S(2)}) collective-permute-start(bf16[192,2048]{1,0:T(8,128)(2,1)} %get-tuple-element.326), channel_id=1, source_target_pairs={{2,1},{3,2},{6,5},{7,6},{10,9},{11,10},{14,13},{15,14},{18,17},{19... | collective-permute-start | bytes 2359304 | tf_op jit(solution)/shard_map/ppermute | solution.py:648
  553.4 33.6 %collective-permute-start.22 = (bf16[192,2048]{1,0:T(8,128)(2,1)}, bf16[192,2048]{1,0:T(8,128)(2,1)}, u32[]{:S(2)}, u32[]{:S(2)}) collective-permute-start(bf16[192,2048]{1,0:T(8,128)(2,1)} %get-tuple-element.324), channel_id=1, source_target_pairs={{3,1},{0,2},{7,5},{4,6},{11,9},{8,10},{15,13},{12,14},{19,17},{16,... | collective-permute-start | bytes 2359304 | tf_op jit(solution)/shard_map/ppermute | solution.py:648
  562.7 184.4 %reduce-scatter.14.cloned.1.call-start = ((), (), s32[]{:S(2)}) async-start(), calls=%async_computation.19 | async-start | bytes 14745600 | tf_op jit(solution)/shard_map/reduce_scatter | solution.py:971
  630.5 31.6 %collective-permute-start.27 = (bf16[200,2048]{1,0:T(8,128)(2,1)}, bf16[200,2048]{1,0:T(8,128)(2,1)}, u32[]{:S(2)}, u32[]{:S(2)}) collective-permute-start(bf16[200,2048]{1,0:T(8,128)(2,1)} %collective-permute-done.23), channel_id=1, source_target_pairs={{1,2},{2,3},{5,6},{6,7},{9,10},{10,11},{13,14},{14,15},{17,18},{18... | collective-permute-start | bytes 2457608 | tf_op jit(solution)/shard_map/ppermute | solution.py:648
  632.1 30.0 %collective-permute-start.28 = (bf16[200,2048]{1,0:T(8,128)(2,1)}, bf16[200,2048]{1,0:T(8,128)(2,1)}, u32[]{:S(2)}, u32[]{:S(2)}) collective-permute-start(bf16[200,2048]{1,0:T(8,128)(2,1)} %collective-permute-done.24), channel_id=1, source_target_pairs={{2,1},{1,0},{6,5},{5,4},{10,9},{9,8},{14,13},{13,12},{18,17},{17,1... | collective-permute-start | bytes 2457608 | tf_op jit(solution)/shard_map/ppermute | solution.py:648
  638.2 40.5 %collective-permute-start.29 = (bf16[200,2048]{1,0:T(8,128)(2,1)}, bf16[200,2048]{1,0:T(8,128)(2,1)}, u32[]{:S(2)}, u32[]{:S(2)}) collective-permute-start(bf16[200,2048]{1,0:T(8,128)(2,1)} %get-tuple-element.340), channel_id=1, source_target_pairs={{1,3},{2,0},{5,7},{6,4},{9,11},{10,8},{13,15},{14,12},{17,19},{18,... | collective-permute-start | bytes 2457608 | tf_op jit(solution)/shard_map/ppermute | solution.py:648
  644.5 34.2 %collective-permute-start.30 = (bf16[200,2048]{1,0:T(8,128)(2,1)S(1)}, bf16[200,2048]{1,0:T(8,128)(2,1)S(1)}, u32[]{:S(2)}, u32[]{:S(2)}) collective-permute-start(bf16[200,2048]{1,0:T(8,128)(2,1)S(1)} %pad_maximum_fusion.4), channel_id=1, source_target_pairs={{0,1},{1,2},{2,3},{4,5},{5,6},{6,7},{8,9},{9,10},{10,11},{12,13},{... | collective-permute-start | bytes 2457608 | tf_op jit(solution)/shard_map/ppermute | solution.py:648
  655.2 38.7 %collective-permute-start.31 = (bf16[200,2048]{1,0:T(8,128)(2,1)S(1)}, bf16[200,2048]{1,0:T(8,128)(2,1)}, u32[]{:S(2)}, u32[]{:S(2)}) collective-permute-start(bf16[200,2048]{1,0:T(8,128)(2,1)S(1)} %pad_maximum_fusion.4), channel_id=1, source_target_pairs={{1,0},{2,1},{3,2},{5,4},{6,5},{7,6},{9,8},{10,9},{11,10},{13,12},{... | collective-permute-start | bytes 2457608 | tf_op jit(solution)/shard_map/ppermute | solution.py:648
  696.0 40.1 %collective-permute-start.34 = (bf16[200,2048]{1,0:T(8,128)(2,1)}, bf16[200,2048]{1,0:T(8,128)(2,1)S(1)}, u32[]{:S(2)}, u32[]{:S(2)}) collective-permute-start(bf16[200,2048]{1,0:T(8,128)(2,1)} %broadcast_select_fusion), channel_id=1, source_target_pairs={{1,3},{2,0},{5,7},{6,4},{9,11},{10,8},{13,15},{14,12},{17,19},{18,... | collective-permute-start | bytes 2457608 | tf_op jit(solution)/shard_map/ppermute | solution.py:648
  698.9 37.3 %collective-permute-start.33 = (bf16[200,2048]{1,0:T(8,128)(2,1)}, bf16[200,2048]{1,0:T(8,128)(2,1)}, u32[]{:S(2)}, u32[]{:S(2)}) collective-permute-start(bf16[200,2048]{1,0:T(8,128)(2,1)} %collective-permute-done.31), channel_id=1, source_target_pairs={{2,1},{1,0},{6,5},{5,4},{10,9},{9,8},{14,13},{13,12},{18,17},{17,1... | collective-permute-start | bytes 2457608 | tf_op jit(solution)/shard_map/ppermute | solution.py:648
  (81 other events, 1245.9 us)
Sparse Core Ops, SparseCore 0:
  13.1 92.0 all-gather.4
  107.0 44.4 all-gather.6
  153.3 63.3 all-gather.8
  219.1 67.6 all-gather.10
  342.6 65.2 reduce-scatter.5
  411.2 59.0 reduce-scatter.7
  477.4 58.4 reduce-scatter.9
  546.3 85.4 reduce-scatter.11
  635.8 95.1 reduce-scatter.13

commit v5 on v4

--- a/solution.py
+++ b/solution.py
@@ -179,7 +179,7 @@
         ib = inverse.astype(BF16)
         pseudo = dot_nn(ib, target.astype(BF16))
         inverse_out[0, head] = ib
-        pseudo_out[:, head * vs : (head + 1) * vs] = pseudo
+        pseudo_out[:, head * vs : (head + 1) * vs] = pseudo.astype(BF16)
         yield
         weighted = beta * pseudo
         mix = decays * dot_nt(qb, kb)
@@ -282,7 +282,8 @@
         sb = state_in[0, head]
         before = sb.astype(F32)
         ib = inverse_in[0, head]
-        pseudo = pseudo_in[:, head * vs : (head + 1) * vs]
+        pb = pseudo_in[:, head * vs : (head + 1) * vs]
+        pseudo = pb.astype(F32)
         output = output_in[:, head * vs : (head + 1) * vs]
         gate = proj[:, gate_at + head * vs : gate_at + (head + 1) * vs]
         given = dnormed[:, head * vs : (head + 1) * vs] * valid
@@ -325,7 +326,7 @@
         yield
         dmix = dot_nt(dob, wb)
         dcross = (dmix * decays).astype(BF16)
-        dlower = jnp.where(strict, -dot_nt(dtb, pseudo.astype(BF16)), 0.0) * decays
+        dlower = jnp.where(strict, -dot_nt(dtb, pb), 0.0) * decays
         dgram = (dlower * beta_row).astype(BF16)
         plain = dlower * gram
         inner_grad = dmix * mix + plain * beta_row
@@ -420,7 +421,7 @@
             jax.ShapeDtypeStruct((total, span), BF16),
             jax.ShapeDtypeStruct((steps, head_count, key_size, value_size), BF16),
             jax.ShapeDtypeStruct((steps, head_count, CHUNK, CHUNK), BF16),
-            jax.ShapeDtypeStruct((total, span), F32),
+            jax.ShapeDtypeStruct((total, span), BF16),
             jax.ShapeDtypeStruct((total, span), F32),
         ],
         scratch_shapes=[

time: 767 us -> 769 us (level)
    unnamed x136 -> x132, local copies, waits for them, and re-layouts: 36.8 us -> 37.8 us
where the time goes in v5:
time: 769 us; the launch traced here: 759 us
  waiting for transfers between devices  273 us (36%)
  matrix products  177 us (23%)
  starting transfers between devices  112 us (15%)
  Pallas kernels  69.3 us (9%)
  local copies, waits for them, and re-layouts  64 us (8%)
  other arithmetic  48 us (6%)
  between operations  15.5 us (2%)
    ppermute x35, waiting for transfers between devices, relay_send(): return lax.ppermute(value, 'tp', route)  227 us
    ppermute x35, starting transfers between devices, relay_send(): return lax.ppermute(value, 'tp', route)  84.2 us
    dot_general x4, matrix products, dot_nn(): lax.dot_general(left, right, (((1,), (0,)), ((), ())), preferred_element_...  49.3 us
    dot_general x4, matrix products, dot_tn(): lax.dot_general(left, right, (((0,), (0,)), ((), ())), preferred_element_...  47.4 us
    dot_general x4, matrix products, dot_nt(): lax.dot_general(left, right, (((1,), (1,)), ((), ())), preferred_element_...  44 us
    unnamed x132, local copies, waits for them, and re-layouts  37.8 us
    pallas_call x1, Pallas kernels, delta_backward(): pl.pallas_call(functools.partial(backward_kernel, head_count, key_size, v...  33.5 us
    reduce_scatter x2, waiting for transfers between devices, deal(): return lax.psum_scatter(part, 'tp', scatter_dimension=0, tiled=True)  31.3 us
  transfers between devices with their start and end apart: 50, of which 27 were waited for; matrix products, arithmetic and copies ran while one was open for 30% of the time, Pallas kernels for 9%

profile of v5, /device:TPU:0, one launch (start us, length us, event | category | flops | bytes accessed | tf_op | source)
XLA Modules:
  0.0 759.4 jit_solution(10603424623302103862)
XLA Ops:
  31.8 11.6 %all-to-all-done = bf16[8,16,2048]{2,1,0:T(8,128)(2,1)} async-done(((bf16[8,16,2048]{2,1,0:T(8,128)(2,1)}), bf16[8,16,2048]{2,1,0:T(8,128)(2,1)}, u32[]{:S(2)}, u32[]{:S(2)}) %all-to-all-start) | async-done | bytes 524320 | tf_op jit(solution)/shard_map/all_to_all | solution.py:801
  110.8 17.9 %fusion.27.proj.prior = f32[768,3200]{1,0:T(8,128)} fusion(bf16[2048,3200]{1,0:T(8,128)(2,1)} %all-gather.5.cloned.1.call-done, bf16[768,2048]{1,0:T(8,128)(2,1)} %get-tuple-element.377.x_ref, f32[2048]{0:T(1024)S(1)} %bitcast.124, f32[768]{0:T(1024)S(1)} %add_rsqrt_fusion), kind=kOutput, calls=%fused_computation.65 | convolution fusion | flops 10072621056 | bytes 26094592 | tf_op jit(solution)/shard_map/dot_general | solution.py:19
  135.8 23.0 %delta_forward.1 = (bf16[768,1024]{1,0:T(8,128)(2,1)S(1)}, bf16[6,4,128,256]{3,2,1,0:T(8,128)(2,1)S(1)}, bf16[6,4,128,128]{3,2,1,0:T(8,128)(2,1)S(1)}, bf16[768,1024]{1,0:T(8,128)(2,1)S(1)}, f32[768,1024]{1,0:T(8,128)}) custom-call(f32[768,3200]{1,0:T(8,128)} %fusion.27.proj.prior, f32[768,128]{1,0:T(8,128)S(1)} %pad.37.info_ref, ...), custom_call_target="tpu_custom_call" | custom-call | tf_op jit(solution)/shard_map/delta_forward/pallas_call | solution.py:402
  180.9 13.4 %collective-permute-done.6 = bf16[192,2048]{1,0:T(8,128)(2,1)} collective-permute-done((bf16[192,2048]{1,0:T(8,128)(2,1)}, bf16[192,2048]{1,0:T(8,128)(2,1)}, u32[]{:S(2)}, u32[]{:S(2)}) %collective-permute-start.6) | collective-permute-done | bytes 786464 | tf_op jit(solution)/shard_map/ppermute | solution.py:649
  194.3 16.3 %collective-permute-done.7 = bf16[192,2048]{1,0:T(8,128)(2,1)} collective-permute-done((bf16[192,2048]{1,0:T(8,128)(2,1)}, bf16[192,2048]{1,0:T(8,128)(2,1)}, u32[]{:S(2)}, u32[]{:S(2)}) %collective-permute-start.7) | collective-permute-done | bytes 786464 | tf_op jit(solution)/shard_map/ppermute | solution.py:649
  219.5 15.5 %collective-permute-done.8.after = bf16[192,2048]{1,0:T(8,128)(2,1)S(1)} collective-permute-done((bf16[192,2048]{1,0:T(8,128)(2,1)S(1)}, bf16[192,2048]{1,0:T(8,128)(2,1)S(1)}, u32[]{:S(2)}, u32[]{:S(2)}) %collective-permute-start.8) | collective-permute-done | bytes 786464 | tf_op jit(solution)/shard_map/ppermute | solution.py:649
  271.3 9.2 %fusion.93 = f32[768,1408]{1,0:T(8,128)} fusion(bf16[768,2048]{1,0:T(8,128)(2,1)S(1)} %convolution_convert_fusion.5.dy_ref, bf16[2048,1408]{0,1:T(8,128)(2,1)} %all-gather.9.cloned.1.call-done), kind=kOutput, calls=%fused_computation.277 | convolution fusion | flops 4429185024 | bytes 13238272 | tf_op jit(solution)/shard_map/dot_general | solution.py:19
  280.6 10.2 %collective-permute-done.12 = bf16[192,2048]{1,0:T(8,128)(2,1)} collective-permute-done((bf16[192,2048]{1,0:T(8,128)(2,1)}, bf16[192,2048]{1,0:T(8,128)(2,1)}, u32[]{:S(2)}, u32[]{:S(2)}) %collective-permute-start.12) | collective-permute-done | bytes 786464 | tf_op jit(solution)/shard_map/ppermute | solution.py:649
  290.8 13.6 %collective-permute-done.14 = bf16[192,2048]{1,0:T(8,128)(2,1)} collective-permute-done((bf16[192,2048]{1,0:T(8,128)(2,1)}, bf16[192,2048]{1,0:T(8,128)(2,1)}, u32[]{:S(2)}, u32[]{:S(2)}) %collective-permute-start.14) | collective-permute-done | bytes 786464 | tf_op jit(solution)/shard_map/ppermute | solution.py:649
  308.9 13.7 %fusion.94 = f32[768,2816]{1,0:T(8,128)S(1)} fusion(bf16[768,2048]{1,0:T(8,128)(2,1)} %pad_maximum_fusion.1, bf16[2048,2816]{1,0:T(8,128)(2,1)} %all-gather.11.cloned.1.call-done), kind=kOutput, calls=%fused_computation.278 | convolution fusion | flops 8858370048 | bytes 23330816 | tf_op jit(solution)/shard_map/dot_general | solution.py:19
  330.1 13.2 %convolution_convert_fusion.10 = bf16[768,2048]{1,0:T(8,128)(2,1)} fusion(bf16[2048,2816]{1,0:T(8,128)(2,1)} %all-gather.11.cloned.1.call-done, bf16[768,1408]{1,0:T(8,128)(2,1)S(1)} %get-tuple-element.318, bf16[768,1408]{1,0:T(8,128)(2,1)S(1)} %get-tuple-element.317), kind=kOutput, calls=%fused_computation.30 | convolution fusion | flops 8868593664 | bytes 19005440 | tf_op jit(solution)/shard_map/dot_general | solution.py:23
  352.1 9.5 %convolution_convert_fusion.9 = bf16[768,2048]{1,0:T(8,128)(2,1)} fusion(bf16[768,1408]{1,0:T(8,128)(2,1)} %get-tuple-element.149, bf16[2048,1408]{0,1:T(8,128)(2,1)} %all-gather.9.cloned.1.call-done), kind=kOutput, calls=%fused_computation.29 | convolution fusion | flops 4430757888 | bytes 11075584 | tf_op jit(solution)/shard_map/dot_general | solution.py:23
  361.6 14.7 %convolution_convert_fusion.1 = bf16[2048,2816]{1,0:T(8,128)(2,1)} fusion(bf16[768,2048]{1,0:T(8,128)(2,1)} %pad_maximum_fusion.1, bf16[768,2816]{1,0:T(8,128)(2,1)} %pad_maximum_fusion), kind=kOutput, calls=%fused_computation.1 | convolution fusion | flops 8864137216 | bytes 19005440 | tf_op jit(solution)/shard_map/dot_general | solution.py:27
  376.2 31.3 %reduce-scatter.6.cloned.1.call-done.moved = bf16[192,2048]{1,0:T(8,128)(2,1)} async-done(((bf16[768,2048]{1,0:T(8,128)(2,1)}), bf16[192,2048]{1,0:T(8,128)(2,1)}) %reduce-scatter.6.cloned.1.call-update) | async-done | bytes 786448 | tf_op jit(solution)/shard_map/reduce_scatter | solution.py:631
  416.6 15.5 %collective-permute-done.15 = bf16[192,2048]{1,0:T(8,128)(2,1)S(1)} collective-permute-done((bf16[192,2048]{1,0:T(8,128)(2,1)S(1)}, bf16[192,2048]{1,0:T(8,128)(2,1)S(1)}, u32[]{:S(2)}, u32[]{:S(2)}) %collective-permute-start.15) | collective-permute-done | bytes 786464 | tf_op jit(solution)/shard_map/ppermute | solution.py:649
  439.9 20.0 %collective-permute-done.17 = bf16[192,2048]{1,0:T(8,128)(2,1)S(1)} collective-permute-done((bf16[192,2048]{1,0:T(8,128)(2,1)S(1)}, bf16[192,2048]{1,0:T(8,128)(2,1)S(1)}, u32[]{:S(2)}, u32[]{:S(2)}) %collective-permute-start.17) | collective-permute-done | bytes 786464 | tf_op jit(solution)/shard_map/ppermute | solution.py:649
  459.9 14.7 %collective-permute-done.19 = bf16[192,2048]{1,0:T(8,128)(2,1)S(1)} collective-permute-done((bf16[192,2048]{1,0:T(8,128)(2,1)S(1)}, bf16[192,2048]{1,0:T(8,128)(2,1)S(1)}, u32[]{:S(2)}, u32[]{:S(2)}) %collective-permute-start.19) | collective-permute-done | bytes 786464 | tf_op jit(solution)/shard_map/ppermute | solution.py:649
  497.3 33.5 %delta_backward.1 = (bf16[768,3200]{1,0:T(8,128)(2,1)}, f32[32,2048]{1,0:T(8,128)S(1)}, f32[8,1024]{1,0:T(8,128)S(1)}, f32[16,128]{1,0:T(8,128)S(1)}) custom-call(f32[768,3200]{1,0:T(8,128)} %fusion.27.proj.prior, f32[768,3200]{1,0:T(8,128)} %fusion.27.proj.prior, f32[768,128]{1,0:T(8,128)S(1)} %pad.37.info_ref, f32[8,768]{1,0:T(8,128)S(1)} %copy-done.25, ...), custom_call_target="tpu_custom_call" | custom-call | tf_op jit(solution)/shard_map/delta_backward/pallas_call | solution.py:447
  532.8 15.3 %convolution_convert_fusion.8.own = bf16[768,2048]{1,0:T(8,128)(2,1)S(1)} fusion(bf16[768,3200]{1,0:T(8,128)(2,1)} %get-tuple-element.162, bf16[2048,3200]{1,0:T(8,128)(2,1)} %all-gather.5.cloned.1.call-done), kind=kOutput, calls=%fused_computation.28 | convolution fusion | flops 10067902464 | bytes 21168128 | tf_op jit(solution)/shard_map/dot_general | solution.py:23
  564.7 17.3 %convolution_convert_fusion = bf16[2048,3200]{1,0:T(8,128)(2,1)} fusion(bf16[768,3200]{1,0:T(8,128)(2,1)} %get-tuple-element.162, bf16[768,2048]{1,0:T(8,128)(2,1)} %get-tuple-element.377.x_ref, f32[2048]{0:T(1024)S(1)} %bitcast.125, f32[768]{0:T(1024)S(1)} %copy-done.47), kind=kOutput, calls=%fused_computation | convolution fusion | flops 10079174656 | bytes 21179392 | tf_op jit(solution)/shard_map/dot_general | solution.py:27
  646.4 10.7 %collective-permute-start.30 = (bf16[200,2048]{1,0:T(8,128)(2,1)S(1)}, bf16[200,2048]{1,0:T(8,128)(2,1)S(1)}, u32[]{:S(2)}, u32[]{:S(2)}) collective-permute-start(bf16[200,2048]{1,0:T(8,128)(2,1)S(1)} %pad_maximum_fusion.4), channel_id=1, source_target_pairs={{0,1},{1,2},{2,3},{4,5},{5,6},{6,7},{8,9},{9,10},{10,11},{12,13},{... | collective-permute-start | bytes 2457608 | tf_op jit(solution)/shard_map/ppermute | solution.py:649
  664.0 16.6 %collective-permute-done.29 = bf16[200,2048]{1,0:T(8,128)(2,1)} collective-permute-done((bf16[200,2048]{1,0:T(8,128)(2,1)}, bf16[200,2048]{1,0:T(8,128)(2,1)}, u32[]{:S(2)}, u32[]{:S(2)}) %collective-permute-start.29) | collective-permute-done | bytes 819232 | tf_op jit(solution)/shard_map/ppermute | solution.py:649
  680.6 15.2 %collective-permute-done.31 = bf16[200,2048]{1,0:T(8,128)(2,1)} collective-permute-done((bf16[200,2048]{1,0:T(8,128)(2,1)S(1)}, bf16[200,2048]{1,0:T(8,128)(2,1)}, u32[]{:S(2)}, u32[]{:S(2)}) %collective-permute-start.31) | collective-permute-done | bytes 819232 | tf_op jit(solution)/shard_map/ppermute | solution.py:649
  719.9 18.2 %collective-permute-done.33 = bf16[200,2048]{1,0:T(8,128)(2,1)} collective-permute-done((bf16[200,2048]{1,0:T(8,128)(2,1)}, bf16[200,2048]{1,0:T(8,128)(2,1)}, u32[]{:S(2)}, u32[]{:S(2)}) %collective-permute-start.33) | collective-permute-done | bytes 819232 | tf_op jit(solution)/shard_map/ppermute | solution.py:649
  (403 shorter events, 353.7 us)
Async XLA Ops:
  7.3 103.5 %all-gather.5.cloned.1.call-start = ((), (), s32[]{:S(2)}) async-start(), calls=%async_computation.11 | async-start | bytes 14745600 | tf_op jit(solution)/shard_map/all_gather | solution.py:830
  43.4 33.5 %all-to-all-start.1 = ((bf16[8,48,2048]{2,1,0:T(8,128)(2,1)}), bf16[8,48,2048]{2,1,0:T(8,128)(2,1)}, u32[]{:S(2)}, u32[]{:S(2)}) async-start(bf16[8,48,2048]{2,1,0:T(8,128)(2,1)} %bitcast.105), calls=%async_computation.1 | async-start | bytes 3145728 | tf_op jit(solution)/shard_map/all_to_all | solution.py:801
  47.7 115.5 %all-gather.7.cloned.1.call-start = ((), (), s32[]{:S(2)}) async-start(), calls=%async_computation.12 | async-start | bytes 4718592 | tf_op jit(solution)/shard_map/all_gather | solution.py:885
  101.0 170.4 %all-gather.9.cloned.1.call-start = ((), (), s32[]{:S(2)}) async-start(), calls=%async_computation.13 | async-start | bytes 6488064 | tf_op jit(solution)/shard_map/all_gather | solution.py:886
  101.7 207.3 %all-gather.11.cloned.1.call-start = ((), (), s32[]{:S(2)}) async-start(), calls=%async_computation.14 | async-start | bytes 12976128 | tf_op jit(solution)/shard_map/all_gather | solution.py:922
  128.7 81.9 %all-to-all-start.2 = ((bf16[8,96,2048]{2,1,0:T(8,128)(2,1)}), bf16[8,96,2048]{2,1,0:T(8,128)(2,1)}, u32[]{:S(2)}, u32[]{:S(2)}) async-start(bf16[8,96,2048]{2,1,0:T(8,128)(2,1)} %bitcast.15), calls=%async_computation.2 | async-start | bytes 6291456 | tf_op jit(solution)/shard_map/all_to_all | solution.py:801
  133.2 274.3 %reduce-scatter.6.cloned.1.call-start = ((), (), s32[]{:S(2)}) async-start(), calls=%async_computation.15 | async-start | bytes 3932160 | tf_op jit(solution)/shard_map/reduce_scatter | solution.py:631
  177.0 33.6 %collective-permute-start.7 = (bf16[192,2048]{1,0:T(8,128)(2,1)}, bf16[192,2048]{1,0:T(8,128)(2,1)}, u32[]{:S(2)}, u32[]{:S(2)}) collective-permute-start(bf16[192,2048]{1,0:T(8,128)(2,1)} %get-tuple-element.327), channel_id=1, source_target_pairs={{3,1},{0,2},{7,5},{4,6},{11,9},{8,10},{15,13},{12,14},{19,17},{16,... | collective-permute-start | bytes 2359304 | tf_op jit(solution)/shard_map/ppermute | solution.py:649
  270.0 34.4 %collective-permute-start.14 = (bf16[192,2048]{1,0:T(8,128)(2,1)}, bf16[192,2048]{1,0:T(8,128)(2,1)}, u32[]{:S(2)}, u32[]{:S(2)}) collective-permute-start(bf16[192,2048]{1,0:T(8,128)(2,1)} %collective-permute-done.11), channel_id=1, source_target_pairs={{2,1},{1,0},{6,5},{5,4},{10,9},{9,8},{14,13},{13,12},{18,17},{17,1... | collective-permute-start | bytes 2359304 | tf_op jit(solution)/shard_map/ppermute | solution.py:649
  343.3 133.6 %reduce-scatter.8.cloned.1.call-start = ((), (), s32[]{:S(2)}) async-start(), calls=%async_computation.16 | async-start | bytes 6488064 | tf_op jit(solution)/shard_map/reduce_scatter | solution.py:972
  407.5 140.6 %reduce-scatter.10.cloned.1.call-start = ((), (), s32[]{:S(2)}) async-start(), calls=%async_computation.17 | async-start | bytes 3932160 | tf_op jit(solution)/shard_map/reduce_scatter | solution.py:631
  438.6 36.0 %collective-permute-start.19 = (bf16[192,2048]{1,0:T(8,128)(2,1)S(1)}, bf16[192,2048]{1,0:T(8,128)(2,1)S(1)}, u32[]{:S(2)}, u32[]{:S(2)}) collective-permute-start(bf16[192,2048]{1,0:T(8,128)(2,1)S(1)} %collective-permute-done.16), channel_id=1, source_target_pairs={{2,1},{1,0},{6,5},{5,4},{10,9},{9,8},{14,13},{13,12},{18,17},{17,1... | collective-permute-start | bytes 2359304 | tf_op jit(solution)/shard_map/ppermute | solution.py:649
  484.0 64.1 %all-to-all-start.3 = ((bf16[8,256,1024]{2,1,0:T(8,128)(2,1)}), bf16[8,256,1024]{2,1,0:T(8,128)(2,1)}, u32[]{:S(2)}, u32[]{:S(2)}) async-start(bf16[8,256,1024]{2,1,0:T(8,128)(2,1)} %bitcast.106), calls=%async_computation.6 | async-start | bytes 8388608 | tf_op jit(solution)/shard_map/all_to_all | solution.py:801
  488.6 228.2 %reduce-scatter.12.cloned.1.call-start = ((), (), s32[]{:S(2)}) async-start(), calls=%async_computation.18 | async-start | bytes 12976128 | tf_op jit(solution)/shard_map/reduce_scatter | solution.py:972
  550.5 31.4 %collective-permute-start.20 = (bf16[192,2048]{1,0:T(8,128)(2,1)}, bf16[192,2048]{1,0:T(8,128)(2,1)}, u32[]{:S(2)}, u32[]{:S(2)}) collective-permute-start(bf16[192,2048]{1,0:T(8,128)(2,1)} %get-tuple-element.326), channel_id=1, source_target_pairs={{2,1},{3,2},{6,5},{7,6},{10,9},{11,10},{14,13},{15,14},{18,17},{19... | collective-permute-start | bytes 2359304 | tf_op jit(solution)/shard_map/ppermute | solution.py:649
  552.1 29.9 %collective-permute-start.21 = (bf16[192,2048]{1,0:T(8,128)(2,1)}, bf16[192,2048]{1,0:T(8,128)(2,1)}, u32[]{:S(2)}, u32[]{:S(2)}) collective-permute-start(bf16[192,2048]{1,0:T(8,128)(2,1)} %get-tuple-element.325), channel_id=1, source_target_pairs={{1,2},{0,1},{5,6},{4,5},{9,10},{8,9},{13,14},{12,13},{17,18},{16,1... | collective-permute-start | bytes 2359304 | tf_op jit(solution)/shard_map/ppermute | solution.py:649
  555.3 33.5 %collective-permute-start.22 = (bf16[192,2048]{1,0:T(8,128)(2,1)}, bf16[192,2048]{1,0:T(8,128)(2,1)}, u32[]{:S(2)}, u32[]{:S(2)}) collective-permute-start(bf16[192,2048]{1,0:T(8,128)(2,1)} %get-tuple-element.324), channel_id=1, source_target_pairs={{3,1},{0,2},{7,5},{4,6},{11,9},{8,10},{15,13},{12,14},{19,17},{16,... | collective-permute-start | bytes 2359304 | tf_op jit(solution)/shard_map/ppermute | solution.py:649
  564.2 184.8 %reduce-scatter.14.cloned.1.call-start = ((), (), s32[]{:S(2)}) async-start(), calls=%async_computation.19 | async-start | bytes 14745600 | tf_op jit(solution)/shard_map/reduce_scatter | solution.py:972
  632.7 31.3 %collective-permute-start.27 = (bf16[200,2048]{1,0:T(8,128)(2,1)}, bf16[200,2048]{1,0:T(8,128)(2,1)}, u32[]{:S(2)}, u32[]{:S(2)}) collective-permute-start(bf16[200,2048]{1,0:T(8,128)(2,1)} %collective-permute-done.23), channel_id=1, source_target_pairs={{1,2},{2,3},{5,6},{6,7},{9,10},{10,11},{13,14},{14,15},{17,18},{18... | collective-permute-start | bytes 2457608 | tf_op jit(solution)/shard_map/ppermute | solution.py:649
  640.3 40.3 %collective-permute-start.29 = (bf16[200,2048]{1,0:T(8,128)(2,1)}, bf16[200,2048]{1,0:T(8,128)(2,1)}, u32[]{:S(2)}, u32[]{:S(2)}) collective-permute-start(bf16[200,2048]{1,0:T(8,128)(2,1)} %get-tuple-element.340), channel_id=1, source_target_pairs={{1,3},{2,0},{5,7},{6,4},{9,11},{10,8},{13,15},{14,12},{17,19},{18,... | collective-permute-start | bytes 2457608 | tf_op jit(solution)/shard_map/ppermute | solution.py:649
  646.4 34.2 %collective-permute-start.30 = (bf16[200,2048]{1,0:T(8,128)(2,1)S(1)}, bf16[200,2048]{1,0:T(8,128)(2,1)S(1)}, u32[]{:S(2)}, u32[]{:S(2)}) collective-permute-start(bf16[200,2048]{1,0:T(8,128)(2,1)S(1)} %pad_maximum_fusion.4), channel_id=1, source_target_pairs={{0,1},{1,2},{2,3},{4,5},{5,6},{6,7},{8,9},{9,10},{10,11},{12,13},{... | collective-permute-start | bytes 2457608 | tf_op jit(solution)/shard_map/ppermute | solution.py:649
  657.1 38.7 %collective-permute-start.31 = (bf16[200,2048]{1,0:T(8,128)(2,1)S(1)}, bf16[200,2048]{1,0:T(8,128)(2,1)}, u32[]{:S(2)}, u32[]{:S(2)}) collective-permute-start(bf16[200,2048]{1,0:T(8,128)(2,1)S(1)} %pad_maximum_fusion.4), channel_id=1, source_target_pairs={{1,0},{2,1},{3,2},{5,4},{6,5},{7,6},{9,8},{10,9},{11,10},{13,12},{... | collective-permute-start | bytes 2457608 | tf_op jit(solution)/shard_map/ppermute | solution.py:649
  697.9 40.1 %collective-permute-start.34 = (bf16[200,2048]{1,0:T(8,128)(2,1)}, bf16[200,2048]{1,0:T(8,128)(2,1)S(1)}, u32[]{:S(2)}, u32[]{:S(2)}) collective-permute-start(bf16[200,2048]{1,0:T(8,128)(2,1)} %broadcast_select_fusion), channel_id=1, source_target_pairs={{1,3},{2,0},{5,7},{6,4},{9,11},{10,8},{13,15},{14,12},{17,19},{18,... | collective-permute-start | bytes 2457608 | tf_op jit(solution)/shard_map/ppermute | solution.py:649
  700.8 37.2 %collective-permute-start.33 = (bf16[200,2048]{1,0:T(8,128)(2,1)}, bf16[200,2048]{1,0:T(8,128)(2,1)}, u32[]{:S(2)}, u32[]{:S(2)}) collective-permute-start(bf16[200,2048]{1,0:T(8,128)(2,1)} %collective-permute-done.31), channel_id=1, source_target_pairs={{2,1},{1,0},{6,5},{5,4},{10,9},{9,8},{14,13},{13,12},{18,17},{17,1... | collective-permute-start | bytes 2457608 | tf_op jit(solution)/shard_map/ppermute | solution.py:649
  (79 other events, 1094.5 us)
Sparse Core Ops, SparseCore 0:
  13.1 92.0 all-gather.4
  107.0 44.2 all-gather.6
  153.2 63.3 all-gather.8
  218.9 67.6 all-gather.10
  343.4 64.0 reduce-scatter.5
  410.8 59.0 reduce-scatter.7
  477.1 58.4 reduce-scatter.9
  548.3 85.3 reduce-scatter.11
  637.7 95.1 reduce-scatter.13
